TPU v7x, 32 devices: a whole 2x2x4 slice. The times are simulated.
32 devices in a mesh: row: 4 (over x, core), col: 8 (over z, y).
Axes of the slice: x: 2, y: 2, z: 4, core: 2. Of those that a mesh axis runs over, the one named last changes fastest.
Arguments:
- density_tiles: float32 [3, 1024, 4096], P(None, ('row', 'col')), may hold values from -0.012 to 0.012
- tile_ids: int32 [1024], P(('row', 'col')), may hold values from 0 to 16383, as said below
- batch_blocks: int32 [32, 8], replicated, may hold values from 0 to 127, as said below
- basis_values: float32 [32, 512, 1024], P(('row', 'col')), may hold values from -6 to 6
- grid_weight: float32 [32, 1024], P(('row', 'col')), may hold values from 0.0002 to 0.002
- xc_kernel: float32 [32, 1024], P(('row', 'col')), may hold values from -2 to -0.5
- grid_coord: float32 [3, 32, 1024], P(None, ('row', 'col')), may hold values from -1 to 1
- orbitals: float32 [8192, 512], P('row'), may hold values from -1.5 to 1.5
- precond_diag: float32 [8192], P('row'), may hold values from 1 to 4
- orbital_energy: float32 [512], replicated, may hold values from -3 to -0.5
Outputs:
- new_density: float32 [3, 1024, 4096], P(None, ('row', 'col'))
Inputs may be any that keep to these rules, and one draw needn't show every extreme that they name: `tile_ids`: the 32 slots of device (r, c), counted in row+col order, list distinct tiles I * 128 + J with I in the r-th range of 32 blocks and J in the c-th range of 16 blocks. `batch_blocks`: each row holds 8 ascending blocks, no two in the same range of 16 blocks, and exactly 2 of them in each range of 32 blocks.
All inputs are finite; a program needn't handle non-finite values.
Results may differ from a plain program's by a relative error of at most 0.0003.
Values sent between devices are 32-bit elements; how exact they have to be, the bound alone decides.
No kernel may reach another device: no remote copies, remote signals or barrier semaphores. Data moves between devices by JAX's collectives and lax.ppermute only.
A program may use at most 192 MiB of HBM per device.

v0:
```python
import jax
import jax.numpy as jnp
from jax import lax
from jax.sharding import PartitionSpec as P

NB = 8192
TILE = 64
FB = 8


PRECISE = lax.Precision.HIGHEST


def from_root(value, axis, source):
    kept = jnp.where(lax.axis_index(axis) == source, value, 0).astype(value.dtype)
    return lax.psum(kept, axis)


def slot_plan(blocks, owner_row, owner_col, col_blocks, per_range):
    matched = blocks // col_blocks == owner_col[..., None]
    active = jnp.any(matched, axis=-1)
    positions = jnp.arange(blocks.shape[-1], dtype=jnp.int32)
    column_place = jnp.sum(jnp.where(matched, positions, 0), axis=-1)
    row_place = owner_row[..., None] * per_range + jnp.arange(per_range, dtype=jnp.int32)
    return (active, row_place, column_place)


def local(
    density_tiles,
    tile_ids,
    batch_blocks,
    basis_values,
    grid_weight,
    xc_kernel,
    grid_coord,
    orbitals,
    precond_diag,
    orbital_energy,
):
    row_count = lax.axis_size("row")
    col_count = lax.axis_size("col")
    device_count = row_count * col_count
    own_row = lax.axis_index("row")
    own_col = lax.axis_index("col")
    own_index = own_row * col_count + own_col
    block_count = NB // TILE
    row_blocks = block_count // row_count
    col_blocks = block_count // col_count
    per_range = FB // row_count
    batch_count = basis_values.shape[0]
    slot_count = batch_count * per_range
    tile_area = TILE * TILE
    tile_local = tile_ids.shape[0]
    orbital_count = orbitals.shape[1]
    col_ratio = col_count // row_count
    col_width = col_blocks * TILE
    batch_width = FB * TILE
    orbital_piece = lax.dynamic_slice_in_dim(
        orbitals, own_col % col_ratio * col_width, col_width, 0
    )
    orbital_cols = from_root(orbital_piece, "row", own_col // col_ratio)
    requests = batch_blocks.reshape(device_count, batch_count, FB)
    owner_rows = jnp.full((device_count, batch_count), own_row, dtype=jnp.int32)
    owner_cols = jnp.full((device_count, batch_count), own_col, dtype=jnp.int32)
    active, row_place, column_place = slot_plan(
        requests, owner_rows, owner_cols, col_blocks, per_range
    )
    want_rows = jnp.take_along_axis(requests, row_place, axis=2)
    want_col = jnp.take_along_axis(requests, column_place[..., None], axis=2)
    wanted = jnp.where(active[..., None], want_rows * block_count + want_col, -1).reshape(-1)
    selector = (wanted[:, None] == tile_ids[None, :]).astype(jnp.float32)
    outgoing = jnp.einsum("ns,dsx->dnx", selector, density_tiles, precision=PRECISE)
    arrived = lax.all_to_all(outgoing, ("row", "col"), split_axis=1, concat_axis=1, tiled=True)
    own_blocks = lax.dynamic_slice_in_dim(requests, own_index, 1, 0)[0]
    block_pos = jnp.arange(FB, dtype=jnp.int32)
    batch_pos = jnp.arange(batch_count, dtype=jnp.int32)
    source = (block_pos // per_range)[None, :, None] * col_count + (own_blocks // col_blocks)[
        :, None, :
    ]
    lookup = (
        source * slot_count
        + batch_pos[:, None, None] * per_range
        + (block_pos % per_range)[None, :, None]
    )
    density = jnp.take(arrived, lookup.reshape(-1), axis=1).reshape(
        3, batch_count, FB, FB, TILE, TILE
    )
    density = density.transpose(0, 1, 2, 4, 3, 5).reshape(3, batch_count, batch_width, batch_width)
    projected = jnp.einsum("dkmn,knp->dkmp", density, basis_values, precision=PRECISE)
    response = jnp.sum(basis_values[None] * projected, axis=2)
    potential = xc_kernel[None] * response + grid_coord
    weighted = basis_values[None] * (grid_weight[None] * potential)[:, :, None, :]
    hamiltonian = jnp.einsum("dkmp,knp->dkmn", weighted, basis_values, precision=PRECISE)
    ham_tiles = (
        hamiltonian.reshape(3, batch_count, FB, TILE, FB, TILE)
        .transpose(0, 1, 2, 4, 3, 5)
        .reshape(3, batch_count * FB * FB, tile_area)
    )
    owners = jnp.arange(device_count, dtype=jnp.int32)
    target_rows = (owners // col_count)[:, None]
    target_cols = (owners % col_count)[:, None]
    mine_all = jnp.broadcast_to(own_blocks[None], (device_count, batch_count, FB))
    back_active, back_rows, back_col = slot_plan(
        mine_all, target_rows, target_cols, col_blocks, per_range
    )
    pick_index = (batch_pos[None, :, None] * FB + back_rows) * FB + back_col[..., None]
    keep_mask = jnp.broadcast_to(back_active[..., None], pick_index.shape).reshape(-1)
    returning = jnp.where(
        keep_mask[None, :, None], jnp.take(ham_tiles, pick_index.reshape(-1), axis=1), 0.0
    )
    returned = lax.all_to_all(returning, ("row", "col"), split_axis=1, concat_axis=1, tiled=True)
    ham_listed = jnp.einsum("ns,dnx->dsx", selector, returned, precision=PRECISE)
    local_rows = tile_ids // block_count - own_row * row_blocks
    local_cols = tile_ids % block_count - own_col * col_blocks
    row_hot = (local_rows[None, :] == jnp.arange(row_blocks, dtype=jnp.int32)[:, None]).astype(
        jnp.float32
    )
    col_hot = (local_cols[None, :] == jnp.arange(col_blocks, dtype=jnp.int32)[:, None]).astype(
        jnp.float32
    )
    block_matrix = jnp.einsum(
        "rs,cs,dsab->dracb",
        row_hot,
        col_hot,
        ham_listed.reshape(3, tile_local, TILE, TILE),
        precision=PRECISE,
    )
    block_matrix = block_matrix.reshape(3, row_blocks * TILE, col_width)
    partial_rows = jnp.einsum("drc,co->dro", block_matrix, orbital_cols, precision=PRECISE)
    orbital_share = orbital_count // col_count
    summed_share = lax.psum_scatter(partial_rows, "col", scatter_dimension=2, tiled=True)
    energy_share = lax.dynamic_slice_in_dim(
        orbital_energy, own_col * orbital_share, orbital_share, 0
    )
    response_share = -summed_share / (precond_diag[:, None] - energy_share[None, :])
    response_orbs = lax.all_gather(response_share, "col", axis=2, tiled=True)
    response_piece = lax.dynamic_slice_in_dim(
        response_orbs, own_col % col_ratio * col_width, col_width, 1
    )
    response_cols = from_root(response_piece, "row", own_col // col_ratio)
    x_rows = jnp.take(response_orbs.reshape(3, row_blocks, TILE, orbital_count), local_rows, axis=1)
    c_rows = jnp.take(orbitals.reshape(row_blocks, TILE, orbital_count), local_rows, axis=0)
    x_cols = jnp.take(response_cols.reshape(3, col_blocks, TILE, orbital_count), local_cols, axis=1)
    c_cols = jnp.take(orbital_cols.reshape(col_blocks, TILE, orbital_count), local_cols, axis=0)
    renewed = jnp.einsum("dsao,sbo->dsab", x_rows, c_cols, precision=PRECISE)
    renewed = renewed + jnp.einsum("sao,dsbo->dsab", c_rows, x_cols, precision=PRECISE)
    return renewed.reshape(3, tile_local, tile_area)


def solution(mesh):
    placed = (
        P(None, ("row", "col"), None),
        P(("row", "col")),
        P(),
        P(("row", "col"), None, None),
        P(("row", "col"), None),
        P(("row", "col"), None),
        P(None, ("row", "col"), None),
        P("row", None),
        P("row"),
        P(),
    )
    return jax.shard_map(
        local, mesh=mesh, in_specs=placed, out_specs=P(None, ("row", "col"), None), check_vma=False
    )
```

profile of v0, /device:TPU:0, one launch (start us, length us, event | category | flops | bytes accessed | tf_op | source)
XLA Modules:
  0.0 1075.1 jit_solution(7821054473080784483)
XLA Ops:
  16.5 7.4 all-to-all-start
  24.7 95.2 %all-to-all-done = f32[3,64,4096]{2,0,1:T(4,128)} async-done(((f32[3,64,4096]{2,0,1:T(4,128)}), f32[3,64,4096]{2,0,1:T(4,128)}, u32[]{:S(2)}, u32[]{:S(2)}) %all-to-all-start) | async-done | bytes 3145760 | tf_op jit(solution)/shard_map/all_to_all | solution.py:73
  119.9 6.9 gather_fusion.6
  139.9 10.9 %copy.68 = f32[3,1,8,64,8,64]{5,4,3,2,0,1:T(8,128)} copy(f32[3,1,8,64,8,64]{5,3,4,2,0,1:T(8,128)} %bitcast.142) | data formatting | bytes 6291456 | tf_op jit(solution)/shard_map/transpose | solution.py:88
  157.1 13.7 %fusion.6 = f32[3,1024]{1,0:T(4,128)S(1)} fusion(f32[512,1024]{1,0:T(8,128)} %bitcast.149, f32[3,512,512]{2,1,0:T(8,128)} %reshape.671, f32[1,512,1024]{2,1,0:T(8,128)} %param.15), kind=kOutput, calls=%fused_computation.16 | convolution fusion | flops 9666819072 | bytes 7352320 | tf_op jit(solution)/shard_map/dkmn,knp->dkmp/dot_general | solution.py:89
  170.9 11.9 %fusion.30 = f32[3,1,512,512]{3,2,0,1:T(8,128)} fusion(f32[1,512,1024]{2,1,0:T(8,128)S(1)} %copy-done.10, f32[3,1024]{1,0:T(4,128)S(1)} %bitcast.146, f32[512,1024]{1,0:T(8,128)S(1)} %bitcast.150), kind=kOutput, calls=%fused_computation.47 | convolution fusion | flops 9665249280 | bytes 7352320 | tf_op jit(solution)/shard_map/dkmp,knp->dkmn/dot_general | solution.py:93
  188.8 6.6 copy.90
  207.3 6.9 gather_fusion.7
  214.2 6.5 bitcast_select_fusion
  233.7 86.7 %all-to-all-done.1 = f32[3,64,4096]{2,0,1:T(4,128)} async-done(((f32[3,64,4096]{2,0,1:T(4,128)}), f32[3,64,4096]{2,0,1:T(4,128)}, u32[]{:S(2)}, u32[]{:S(2)}) %all-to-all-start.1) | async-done | bytes 3145760 | tf_op jit(solution)/shard_map/all_to_all | solution.py:111
  328.0 44.7 %convolution_bitcast_fusion = f32[3,32,64,16,64]{4,1,2,0,3:T(8,128)} fusion(f32[3,32,64,64]{3,2,1,0:T(8,128)} %reshape.674, f32[32,32]{0,1:T(8,128)S(1)} %convert_bitcast_fusion, f32[32,16]{0,1:T(8,128)S(1)} %convert_bitcast_fusion.1), kind=kOutput, calls=%fused_computation.8 | convolution fusion | flops 2415935488 | bytes 26744832 | tf_op jit(solution)/shard_map/rs,cs,dsab->dracb/dot_general | solution.py:121
  372.7 46.1 %copy.73 = f32[3,32,64,16,64]{4,3,2,1,0:T(8,128)} copy(f32[3,32,64,16,64]{4,1,2,0,3:T(8,128)} %convolution_bitcast_fusion) | data formatting | bytes 50331648 | tf_op jit(solution)/shard_map/rs,cs,dsab->dracb/transpose | solution.py:121
  418.8 42.1 %reshape.675 = f32[3,2048,1024]{2,1,0:T(8,128)} reshape(f32[3,32,64,16,64]{4,3,2,1,0:T(8,128)} %copy.73) | data formatting | bytes 50331648 | tf_op jit(solution)/shard_map/reshape | solution.py:128
  460.9 45.9 %fusion.22 = f32[3,2048,512]{1,2,0:T(8,128)} fusion(f32[3,2048,1024]{2,1,0:T(8,128)} %reshape.675, f32[1024,512]{0,1:T(8,128)} %all-reduce.3.cloned.1.call-done), kind=kOutput, calls=%fused_computation.39 | convolution fusion | flops 38654705664 | bytes 39845888 | tf_op jit(solution)/shard_map/drc,co->dro/dot_general | solution.py:129
  507.8 204.2 %reduce-scatter.2.cloned.1.call-done = f32[3,2048,64]{1,2,0:T(8,128)} async-done(((f32[3,2048,512]{1,2,0:T(8,128)}), f32[3,2048,64]{1,2,0:T(8,128)}) %reduce-scatter.2.cloned.1.call-update) | async-done | bytes 1572880 | tf_op jit(solution)/shard_map/reduce_scatter | solution.py:131
  714.8 175.6 %all-gather.2.cloned.1.call-done = f32[3,2048,512]{1,2,0:T(8,128)} async-done(((f32[3,2048,64]{1,2,0:T(8,128)}), f32[3,2048,512]{1,2,0:T(8,128)}) %all-gather.2.cloned.1.call-update) | async-done | bytes 12582928 | tf_op jit(solution)/shard_map/all_gather | solution.py:136
  890.5 6.7 dynamic-slice_select_fusion
  897.2 7.1 copy.75
  916.9 12.6 %copy.74 = f32[3,2048,512]{2,1,0:T(8,128)} copy(f32[3,2048,512]{1,2,0:T(8,128)} %all-gather.2.cloned.1.call-done) | data formatting | bytes 25165824 | tf_op jit(solution)/shard_map/all_gather | solution.py:136
  929.5 10.5 gather_fusion.1
  940.0 82.2 %all-reduce.5.cloned.1.call-done = f32[3,16,64,512]{3,2,1,0:T(8,128)} async-done(((f32[3,16,64,512]{3,2,1,0:T(8,128)}), f32[3,16,64,512]{3,2,1,0:T(8,128)}) %all-reduce.5.cloned.1.call-update) | async-done | bytes 6291472 | tf_op jit(solution)/shard_map/psum | solution.py:16
  1022.2 8.6 gather_fusion.2
  1030.8 15.3 %fusion = f32[32,3,64,64]{3,2,1,0:T(8,128)S(1)} fusion(f32[32,3,64,512]{3,2,1,0:T(8,128)} %gather_fusion.2, pred[32]{0:T(512)(128)(4,1)S(1)} %get-tuple-element.10, f32[32,64,512]{2,1,0:T(8,128)} %gather_fusion.3, pred[32]{0:T(512)(128)(4,1)S(1)} %get-tuple-element.18), kind=kOutput, calls=%fused_computation.9 | convolution fusion | flops 2420113408 | bytes 18350144 | tf_op jit(solution)/shard_map/sao,dsbo->dsab/dot_general | solution.py:146
  1046.2 15.4 %bitcast_add_fusion = f32[3,32,64,64]{2,3,0,1:T(8,128)} fusion(f32[32,3,64,64]{3,2,1,0:T(8,128)S(1)} %fusion, f32[32,3,64,512]{3,2,1,0:T(8,128)S(1)} %copy-done.3, pred[32]{0:T(512)(128)(4,1)S(1)} %get-tuple-element.18, f32[32,64,512]{2,1,0:T(8,128)S(1)} %copy-done.4, pred[32]{0:T(512)(128)(4,1)S(1)} %get-tuple-element.10), kind=kOutput, calls=%fused_computation.33 | convolution fusion | flops 2420506624 | bytes 19923008 | tf_op jit(solution)/shard_map/dsao,sbo->dsab/dot_general | solution.py:145
  (106 shorter events, 91.5 us)
Async XLA Ops:
  6.5 4.3 copy-start
  6.5 2.3 copy-start.2
  8.8 2.0 copy-start.7
  16.5 103.4 %all-to-all-start = ((f32[3,64,4096]{2,0,1:T(4,128)}), f32[3,64,4096]{2,0,1:T(4,128)}, u32[]{:S(2)}, u32[]{:S(2)}) async-start(f32[3,64,4096]{2,0,1:T(4,128)} %copy.66), calls=%async_computation | async-start | bytes 8388608 | tf_op jit(solution)/shard_map/all_to_all | solution.py:73
  157.1 13.8 %copy-start.5 = (f32[3,1,1024]{2,1,0:T(1,128)S(1)}, f32[3,1,1024]{2,1,0:T(1,128)}, u32[]{:S(2)}) copy-start(f32[3,1,1024]{2,1,0:T(1,128)} %param.18) | copy-start | bytes 36868
  157.1 13.8 %copy-start.8 = (f32[1,1024]{1,0:T(1,128)S(1)}, f32[1,1024]{1,0:T(1,128)}, u32[]{:S(2)}) copy-start(f32[1,1024]{1,0:T(1,128)} %param.17) | copy-start | bytes 12292
  157.1 13.8 %copy-start.9 = (f32[1,1024]{1,0:T(1,128)S(1)}, f32[1,1024]{1,0:T(1,128)}, u32[]{:S(2)}) copy-start(f32[1,1024]{1,0:T(1,128)} %param.16) | copy-start | bytes 12292
  157.1 13.8 %copy-start.10 = (f32[1,512,1024]{2,1,0:T(8,128)S(1)}, f32[1,512,1024]{2,1,0:T(8,128)}, u32[]{:S(2)}) copy-start(f32[1,512,1024]{2,1,0:T(8,128)} %param.15) | copy-start | bytes 6291460
  220.7 99.6 %all-to-all-start.1 = ((f32[3,64,4096]{2,0,1:T(4,128)}), f32[3,64,4096]{2,0,1:T(4,128)}, u32[]{:S(2)}, u32[]{:S(2)}) async-start(f32[3,64,4096]{2,0,1:T(4,128)} %bitcast_select_fusion), calls=%async_computation.1 | async-start | bytes 8388608 | tf_op jit(solution)/shard_map/all_to_all | solution.py:111
  224.3 236.6 %all-reduce.3.cloned.1.call-start = ((), (), s32[]{:S(2)}) async-start(), calls=%async_computation.3 | async-start | bytes 4194304 | tf_op jit(solution)/shard_map/psum | solution.py:16
  233.6 478.4 %reduce-scatter.2.cloned.1.call-start = ((), (), s32[]{:S(2)}) async-start(), calls=%async_computation.4 | async-start | bytes 14155776 | tf_op jit(solution)/shard_map/reduce_scatter | solution.py:131
  506.8 0.8 copy-start.6
  506.8 383.6 %all-gather.2.cloned.1.call-start = ((), (), s32[]{:S(2)}) async-start(), calls=%async_computation.5 | async-start | bytes 14155776 | tf_op jit(solution)/shard_map/all_gather | solution.py:136
  714.8 307.5 %all-reduce.5.cloned.1.call-start = ((), (), s32[]{:S(2)}) async-start(), calls=%async_computation.6 | async-start | bytes 12582912 | tf_op jit(solution)/shard_map/psum | solution.py:16
  1030.8 15.3 %copy-start.3 = (f32[32,3,64,512]{3,2,1,0:T(8,128)S(1)}, f32[32,3,64,512]{3,2,1,0:T(8,128)}, u32[]{:S(2)}) copy-start(f32[32,3,64,512]{3,2,1,0:T(8,128)} %gather_fusion.1) | copy-start | bytes 37748740
  1030.8 15.3 %copy-start.4 = (f32[32,64,512]{2,1,0:T(8,128)S(1)}, f32[32,64,512]{2,1,0:T(8,128)}, u32[]{:S(2)}) copy-start(f32[32,64,512]{2,1,0:T(8,128)} %gather_fusion) | copy-start | bytes 12582916
  1046.1 22.2 %copy-start.1 = (f32[3,32,4096]{2,1,0:T(8,128)S(1)}, f32[3,32,4096]{2,1,0:T(8,128)}, u32[]{:S(2)}) copy-start(f32[3,32,4096]{2,1,0:T(8,128)} %param.12) | copy-start | bytes 4718596
Sparse Core Ops, SparseCore 0:
  233.7 80.4 all-reduce.2
  507.0 204.9 reduce-scatter.1
  714.9 175.5 all-gather.1
  904.4 117.7 all-reduce.4
where the time goes:
time: 1090 us; the launch traced here: 1080 us
  waiting for transfers between devices  644 us (59%)
  local copies, waits for them, and re-layouts  228 us (21%)
  matrix products  153 us (14%)
  other arithmetic  24.8 us (2%)
  between operations  13.7 us (1%)
  starting transfers between devices  11.2 us (1%)
    reduce_scatter x1, waiting for transfers between devices, local(): lax.psum_scatter(partial_rows, 'col', scatter_dimension=2, tiled=True)  204 us
    all_gather x1, waiting for transfers between devices, local(): response_orbs = lax.all_gather(response_share, 'col', axis=2, tiled=True)  176 us
    all_to_all x1, waiting for transfers between devices, local(): lax.all_to_all(outgoing, ('row', 'col'), split_axis=1, concat_axis=1, til...  95.2 us
    all_to_all x1, waiting for transfers between devices, local(): lax.all_to_all(returning, ('row', 'col'), split_axis=1, concat_axis=1, ti...  86.7 us
    psum x2, waiting for transfers between devices, from_root(): return lax.psum(kept, axis)  82.2 us
    transpose x1, local copies, waits for them, and re-layouts, local(): jnp.einsum('rs,cs,dsab->dracb', row_hot, col_hot, ham_listed.reshape(3, t...  46.1 us
    dot_general x1, matrix products, local(): jnp.einsum('drc,co->dro', block_matrix, orbital_cols, precision=PRECISE)  45.9 us
    dot_general x1, matrix products, local(): jnp.einsum('rs,cs,dsab->dracb', row_hot, col_hot, ham_listed.reshape(3, t...  44.7 us
  transfers between devices with their start and end apart: 6, of which 5 were waited for; matrix products, arithmetic and copies ran while one was open for 17% of the time, Pallas kernels for 0%

commit v1 on v0

v1 whole, which is shorter than its diff:
```python
import functools

import jax
import jax.numpy as jnp
from jax import lax
from jax.experimental import pallas as pl
from jax.experimental.pallas import tpu as pltpu
from jax.sharding import PartitionSpec as P

NB = 8192
TILE = 64
FB = 8
LANES = 2 * TILE
ROWS = TILE * TILE // LANES
F32 = jnp.float32
BF16 = jnp.bfloat16
NT = (((1,), (1,)), ((), ()))


def split(value):
    high = value.astype(BF16)
    return high, (value - high.astype(F32)).astype(BF16)


def dot(a, b):
    return jnp.dot(a, b, preferred_element_type=F32)


def dot_nt(a, b):
    return lax.dot_general(a, b, NT, preferred_element_type=F32)


def low_lanes(shape):
    return lax.broadcasted_iota(jnp.int32, shape, len(shape) - 1) < TILE


def params(mib):
    return pltpu.CompilerParams(vmem_limit_bytes=mib * 2**20)


VMEM = pl.BlockSpec(memory_space=pltpu.VMEM)
SMEM = pl.BlockSpec(memory_space=pltpu.SMEM)


def pick_kernel(slot_ref, tiles_ref, out_ref):
    count = out_ref.shape[0]

    def step(n, carry):
        slot = slot_ref[n]
        data = tiles_ref[:, jnp.maximum(slot, 0)]
        out_ref[n] = jnp.where(slot >= 0, data, 0.0)
        return carry

    lax.fori_loop(0, count, step, 0)


def pick_tiles(slots, tiles):
    nd = tiles.shape[0]
    return pl.pallas_call(
        pick_kernel,
        out_shape=jax.ShapeDtypeStruct((slots.shape[0], nd, ROWS, LANES), F32),
        in_specs=[SMEM, VMEM],
        out_specs=VMEM,
        compiler_params=params(32),
        name="pick_tiles",
    )(slots, tiles)


def batch_kernel(
    per_range, col_count, col_ref, tiles_ref, basis_ref, weight_ref, xc_ref, coord_ref, out_ref,
    bh, bl, wh, wl, square,
):
    nd = tiles_ref.shape[1]
    width, pts = basis_ref.shape
    low = low_lanes((ROWS, LANES))
    if col_count > FB:
        out_ref[...] = jnp.zeros(out_ref.shape, F32)

    def place(i, j):
        owner = (i // per_range) * col_count + col_ref[j]
        return owner * per_range + i % per_range

    high, rest = split(basis_ref[...])
    bh[...] = high
    bl[...] = rest

    def direction(d, carry):
        for i in range(FB):
            for jj in range(FB // 2):
                first = tiles_ref[place(i, 2 * jj), d]
                second = tiles_ref[place(i, 2 * jj + 1), d]
                square[jj, pl.ds(i * TILE, ROWS, stride=2), :] = jnp.where(
                    low, first, pltpu.roll(second, TILE, 1)
                )
                square[jj, pl.ds(i * TILE + 1, ROWS, stride=2), :] = jnp.where(
                    low, pltpu.roll(first, TILE, 1), second
                )
        eh, el = split(jnp.concatenate([square[jj] for jj in range(FB // 2)], axis=1))
        piece = 256
        for start in range(0, pts, piece):
            cols = slice(start, start + piece)
            projected = dot(eh, bh[:, cols]) + dot(eh, bl[:, cols]) + dot(el, bh[:, cols])
            values = basis_ref[:, cols]
            response = jnp.sum(values * projected, axis=0, keepdims=True)
            potential = xc_ref[:, cols] * response + coord_ref[d, :, cols]
            weighted = values * (weight_ref[:, cols] * potential)
            high, rest = split(weighted)
            wh[:, cols] = high
            wl[:, cols] = rest
        for start in range(0, width, piece):
            rows = slice(start, start + piece)
            value = (
                dot_nt(wh[...], bh[rows]) + dot_nt(wh[...], bl[rows]) + dot_nt(wl[...], bh[rows])
            )
            for lane in range(0, piece, LANES):
                square[(start + lane) // LANES] = value[:, lane : lane + LANES]
        for i in range(FB):
            for jj in range(FB // 2):
                even = square[jj, pl.ds(i * TILE, ROWS, stride=2), :]
                odd = square[jj, pl.ds(i * TILE + 1, ROWS, stride=2), :]
                out_ref[place(i, 2 * jj), d] = jnp.where(low, even, pltpu.roll(odd, TILE, 1))
                out_ref[place(i, 2 * jj + 1), d] = jnp.where(low, pltpu.roll(even, TILE, 1), odd)
        return carry

    lax.fori_loop(0, nd, direction, 0)


def batch_tiles(per_range, col_count, cols, tiles, basis, weight, xc, coord):
    width, pts = basis.shape
    return pl.pallas_call(
        functools.partial(batch_kernel, per_range, col_count),
        out_shape=jax.ShapeDtypeStruct(tiles.shape, F32),
        in_specs=[SMEM] + [VMEM] * 5,
        out_specs=VMEM,
        scratch_shapes=[
            pltpu.VMEM((width, pts), BF16),
            pltpu.VMEM((width, pts), BF16),
            pltpu.VMEM((width, pts), BF16),
            pltpu.VMEM((width, pts), BF16),
            pltpu.VMEM((width // LANES, width, LANES), F32),
        ],
        compiler_params=params(48),
        name="batch_tiles",
    )(cols, tiles, basis, weight, xc, coord)


def add_kernel(slot_ref, tiles_ref, out_ref):
    count = tiles_ref.shape[0]
    out_ref[...] = jnp.zeros(out_ref.shape, F32)

    def step(n, carry):
        slot = slot_ref[n]

        @pl.when(slot >= 0)
        def _():
            out_ref[slot] += tiles_ref[n]

        return carry

    lax.fori_loop(0, count, step, 0)


def add_tiles(slots, tiles, slot_count):
    return pl.pallas_call(
        add_kernel,
        out_shape=jax.ShapeDtypeStruct((slot_count,) + tiles.shape[1:], F32),
        in_specs=[SMEM, VMEM],
        out_specs=VMEM,
        compiler_params=params(32),
        name="add_tiles",
    )(slots, tiles)


def rows_kernel(chunk_count, fresh, *refs):
    refs = list(refs)
    col_ref, row_id, col_id = refs[:3]
    chunks = refs[3 : 3 + chunk_count]
    orbs = refs[3 + chunk_count : 3 + 2 * chunk_count]
    rest = refs[3 + 2 * chunk_count :]
    if fresh:
        out_ref, stacked = rest
        out_ref[...] = jnp.zeros(out_ref.shape, F32)
    else:
        in_ref, out_ref, stacked = rest
        out_ref[...] = in_ref[...]
    accumulate(chunks, orbs, row_id, col_id, out_ref, stacked)


def accumulate(chunks, orbs, row_id, col_id, out_ref, stacked):
    low = low_lanes((ROWS, LANES))
    offset = 0
    for chunk, orb in zip(chunks, orbs):
        count, nd = chunk.shape[:2]

        def stack(b, carry, orb=orb):
            high, rest = split(orb[pl.ds(pl.multiple_of(b * TILE, TILE), TILE), :])
            stacked[b, 0 * TILE : 1 * TILE] = high
            stacked[b, 1 * TILE : 2 * TILE] = rest
            stacked[b, 2 * TILE : 3 * TILE] = high
            stacked[b, 3 * TILE : 4 * TILE] = rest
            return carry

        lax.fori_loop(0, orb.shape[0] // TILE, stack, 0)

        def step(s, carry, chunk=chunk, offset=offset, nd=nd):
            parts = []
            for d in range(nd):
                tile = chunk[s, d]
                turned = pltpu.roll(tile, TILE, 1)
                for value in (jnp.where(low, tile, turned), jnp.where(low, turned, tile)):
                    parts.append(jnp.concatenate(split(value), axis=1))
            left = jnp.concatenate(parts, axis=0)
            product = dot(left, stacked[col_id[offset + s]])
            out_ref[row_id[offset + s]] += product
            return carry

        lax.fori_loop(0, count, step, 0)
        offset += count


def add_rows(total, chunks, places, row_ids, col_ids, orbitals, row_blocks, col_width):
    nd = chunks[0].shape[1]
    count = len(chunks)
    nocc = orbitals.shape[1]
    shape = jax.ShapeDtypeStruct((row_blocks, nd * TILE, nocc), F32)
    whole = lambda a: pl.BlockSpec(a.shape, lambda g, *_, n=len(a.shape): (0,) * n)
    in_specs = [whole(c) for c in chunks]
    for k in range(count):
        in_specs.append(pl.BlockSpec((col_width, nocc), lambda g, p, r, c, k=k: (p[k], 0)))
    args = list(chunks) + [orbitals] * count
    aliases = {}
    if total is not None:
        in_specs.append(whole(shape))
        args.append(total)
        aliases = {3 + len(args) - 1: 0}
    return pl.pallas_call(
        functools.partial(rows_kernel, count, total is None),
        out_shape=shape,
        grid_spec=pltpu.PrefetchScalarGridSpec(
            num_scalar_prefetch=3,
            grid=(1,),
            in_specs=in_specs,
            out_specs=whole(shape),
            scratch_shapes=[pltpu.VMEM((col_width // TILE, 4 * TILE, nocc), BF16)],
        ),
        input_output_aliases=aliases,
        compiler_params=params(60),
        name="add_rows",
    )(places, row_ids, col_ids, *args)


def response_kernel(
    nd, piece_blocks, part_ref, total_ref, diag_ref, energy_ref, out_ref, piece_ref, square
):
    blocks = total_ref.shape[0]
    first = part_ref[0] * piece_blocks

    def step(b, carry):
        inverse = -1.0 / (diag_ref[b] - energy_ref[...])
        inside = jnp.logical_and(b >= first, b < first + piece_blocks)
        for d in range(nd):
            rows = slice(d * TILE, (d + 1) * TILE)
            out_ref[b, rows] = total_ref[b, rows] * inverse

        @pl.when(inside)
        def _():
            for d in range(nd):
                for k in range(square.shape[0]):
                    lanes = slice(k * LANES, (k + 1) * LANES)
                    for parity in range(2):
                        start = d * TILE + parity * ROWS
                        square[k, pl.ds(parity, ROWS, stride=2), :] = out_ref[
                            b, start : start + ROWS, lanes
                        ]
                    piece_ref[d, b - first, :, lanes] = square[k]

        return carry

    lax.fori_loop(0, blocks, step, 0)


def response(total, diag, energy, part, piece_blocks):
    blocks, rows, nocc = total.shape
    nd = rows // TILE
    return pl.pallas_call(
        functools.partial(response_kernel, nd, piece_blocks),
        out_shape=(
            jax.ShapeDtypeStruct(total.shape, F32),
            jax.ShapeDtypeStruct((nd, piece_blocks, TILE, nocc), F32),
        ),
        in_specs=[SMEM] + [VMEM] * 3,
        out_specs=(VMEM, VMEM),
        scratch_shapes=[pltpu.VMEM((nocc // LANES, TILE, LANES), F32)],
        compiler_params=params(60),
        name="response_orbitals",
    )(part, total, diag, energy)


def first_kernel(nd, row_id, col_id, x_ref, orb_ref, out_ref, both):
    low = low_lanes((ROWS, LANES))

    def stack(b, carry):
        high, rest = split(orb_ref[pl.ds(pl.multiple_of(b * TILE, TILE), TILE), :])
        both[b, 0:TILE] = high
        both[b, TILE : 2 * TILE] = rest
        return carry

    lax.fori_loop(0, both.shape[0], stack, 0)

    def step(s, carry):
        high, rest = split(x_ref[row_id[s]])
        pair = both[col_id[s]]
        value = dot_nt(high, pair) + dot_nt(rest, pair)
        value = value + pltpu.roll(value, TILE, 1)
        for d in range(nd):
            start = d * TILE
            even = value[start : start + ROWS]
            odd = value[start + ROWS : start + TILE]
            out_ref[d, s] = jnp.where(low, even, odd)
        return carry

    lax.fori_loop(0, out_ref.shape[1], step, 0)


def first_term(row_ids, col_ids, x, orb_cols):
    slots = row_ids.shape[0]
    nd = x.shape[1] // TILE
    nocc = x.shape[2]
    return pl.pallas_call(
        functools.partial(first_kernel, nd),
        out_shape=jax.ShapeDtypeStruct((nd, slots, ROWS, LANES), F32),
        in_specs=[SMEM, SMEM, VMEM, VMEM],
        out_specs=VMEM,
        scratch_shapes=[
            pltpu.VMEM((orb_cols.shape[0] // TILE, 2 * TILE, nocc), BF16),
        ],
        compiler_params=params(60),
        name="first_term",
    )(row_ids, col_ids, x, orb_cols)


def second_kernel(nd, row_id, col_id, x_ref, orb_ref, first_ref, out_ref, square):
    low = low_lanes((ROWS, LANES))

    def step(s, carry):
        block = pl.ds(pl.multiple_of(row_id[s] * TILE, TILE), TILE)
        high, rest = split(orb_ref[block, :])
        left = jnp.concatenate([high, rest], axis=0)
        for d in range(nd):
            x_high, x_rest = split(x_ref[d, col_id[s]])
            pair = jnp.concatenate([x_high, x_rest], axis=0)
            value = dot_nt(left, pair)
            value = value[:TILE] + value[TILE:]
            square[...] = value + pltpu.roll(value, TILE, 1)
            even = square[pl.ds(0, ROWS, stride=2), :]
            odd = square[pl.ds(1, ROWS, stride=2), :]
            out_ref[d, s] = first_ref[d, s] + jnp.where(low, even, odd)
        return carry

    lax.fori_loop(0, out_ref.shape[1], step, 0)


def second_term(row_ids, col_ids, x_cols, orbitals, first):
    nd = x_cols.shape[0]
    return pl.pallas_call(
        functools.partial(second_kernel, nd),
        out_shape=jax.ShapeDtypeStruct(first.shape, F32),
        in_specs=[SMEM, SMEM, VMEM, VMEM, VMEM],
        out_specs=VMEM,
        scratch_shapes=[pltpu.VMEM((TILE, LANES), F32)],
        compiler_params=params(60),
        name="second_term",
    )(row_ids, col_ids, x_cols, orbitals, first)


def ring_order(count):
    return list(range(0, count, 2)) + list(range(count - 1, 0, -2))


def row_broadcast(value, row_count, col_count, ratio, own_row, own_col):
    away = own_row ^ (own_col // ratio)
    bit = row_count // 2
    passed = 0
    while bit:
        pairs = []
        for c in range(col_count):
            for r in range(row_count):
                if (r ^ (c // ratio)) & ~passed == 0:
                    pairs.append((r * col_count + c, (r ^ bit) * col_count + c))
        got = lax.ppermute(value, ("row", "col"), pairs)
        passed |= bit
        taken = jnp.logical_and((away & bit) != 0, (away & ~passed) == 0)
        value = jnp.where(taken, got, value)
        bit //= 2
    return value


def local(
    density_tiles,
    tile_ids,
    batch_blocks,
    basis_values,
    grid_weight,
    xc_kernel,
    grid_coord,
    orbitals,
    precond_diag,
    orbital_energy,
):
    row_count = lax.axis_size("row")
    col_count = lax.axis_size("col")
    device_count = row_count * col_count
    own_row = lax.axis_index("row")
    own_col = lax.axis_index("col")
    own_index = own_row * col_count + own_col
    block_count = NB // TILE
    row_blocks = block_count // row_count
    col_blocks = block_count // col_count
    per_range = FB // row_count
    slot_count = tile_ids.shape[0]
    ratio = col_count // row_count
    col_width = col_blocks * TILE
    nd = density_tiles.shape[0]
    nocc = orbitals.shape[1]

    ask = batch_blocks
    match = ask // col_blocks == own_col
    ask_col = jnp.sum(jnp.where(match, ask, 0), axis=1)
    ask_row = lax.dynamic_slice_in_dim(ask, own_row * per_range, per_range, 1)
    wanted = jnp.where(jnp.any(match, axis=1)[:, None], ask_row * block_count + ask_col[:, None], -1)
    hit = wanted.reshape(-1)[:, None] == tile_ids[None, :]
    slots = jnp.max(jnp.where(hit, jnp.arange(slot_count, dtype=jnp.int32)[None, :], -1), axis=1)
    own_cols = lax.dynamic_slice_in_dim(ask, own_index, 1, 0)[0] // col_blocks

    listed = lax.all_gather(tile_ids, "col", axis=0, tiled=False)
    listed_rows = listed // block_count - own_row * row_blocks
    listed_cols = listed % col_blocks
    local_rows = tile_ids // block_count - own_row * row_blocks
    local_cols = tile_ids % col_blocks
    all_orbitals = lax.all_gather(orbitals, "row", axis=0, tiled=True)

    tiles = density_tiles.reshape(nd, slot_count, ROWS, LANES)
    picked = pick_tiles(slots, tiles)
    exchange = lambda a: lax.all_to_all(
        a.reshape(device_count, -1, LANES), ("row", "col"), split_axis=0, concat_axis=0, tiled=True
    ).reshape(a.shape)
    arrived = exchange(picked)
    built = batch_tiles(
        per_range, col_count, own_cols, arrived, basis_values[0], grid_weight, xc_kernel, grid_coord
    )
    returned = exchange(built)
    ham = add_tiles(slots, returned, slot_count)

    order = ring_order(col_count)
    place = [order.index(c) for c in range(col_count)]
    forward = [(order[i], order[(i + 1) % col_count]) for i in range(col_count)]
    backward = [(b, a) for a, b in forward]
    ring = jnp.asarray(order, jnp.int32)
    at = jnp.asarray(place, jnp.int32)[own_col]

    def rows(total, chunks, offsets, starts):
        cols = [ring[(at + o) % col_count] for o in offsets]
        take = lambda table: jnp.concatenate(
            [table[c, s : s + k.shape[0]] for c, s, k in zip(cols, starts, chunks)]
        )
        return add_rows(
            total, chunks, jnp.stack(cols), take(listed_rows), take(listed_cols), all_orbitals,
            row_blocks, col_width,
        )

    up = down = ham
    half = slot_count // 2
    total = None
    held = [(ham,)]
    offsets = [(0,)]
    for step in range(1, col_count // 2):
        up = lax.ppermute(up, "col", forward)
        down = lax.ppermute(down, "col", backward)
        held.append((up, down))
        offsets.append((-step, step))
    up = lax.ppermute(up[:half], "col", forward)
    down = lax.ppermute(down[half:], "col", backward)
    held.append((up, down))
    offsets.append((col_count // 2, col_count // 2))
    for chunks, offs in zip(held, offsets):
        starts = [0, half] if chunks[0].shape[0] == half else [0] * len(chunks)
        total = rows(total, chunks, offs, starts)

    diag = precond_diag.reshape(row_blocks, ROWS, 2).swapaxes(1, 2).reshape(row_blocks, TILE, 1)
    part = (own_col % ratio).reshape(1)
    x, piece = response(total, diag, orbital_energy[None], part, col_blocks)
    x_cols = row_broadcast(piece, row_count, col_count, ratio, own_row, own_col)
    orb_cols = lax.dynamic_slice_in_dim(all_orbitals, own_col * col_width, col_width, 0)
    first = first_term(local_rows, local_cols, x, orb_cols)
    renewed = second_term(local_rows, local_cols, x_cols, orbitals, first)
    return renewed.reshape(nd, slot_count, TILE * TILE)


def solution(mesh):
    placed = (
        P(None, ("row", "col"), None),
        P(("row", "col")),
        P(),
        P(("row", "col"), None, None),
        P(("row", "col"), None),
        P(("row", "col"), None),
        P(None, ("row", "col"), None),
        P("row", None),
        P("row"),
        P(),
    )
    return jax.shard_map(
        local, mesh=mesh, in_specs=placed, out_specs=P(None, ("row", "col"), None), check_vma=False
    )
```

time: 1090 us -> 603 us (0.55); the launches traced: 1080 us -> 602 us
  waiting for transfers between devices: 644 us -> 207 us
  local copies, waits for them, and re-layouts: 228 us -> 18 us
  Pallas kernels: 0 us -> 196 us
  matrix products: 153 us -> 0 us
  blocking collectives: 0 us -> 93.8 us
  between operations: 13.7 us -> 35.8 us
  starting transfers between devices: 11.2 us -> 26.1 us
    reduce_scatter x1 -> x0, waiting for transfers between devices: 204 us -> none  [local(): lax.psum_scatter(partial_rows, 'col', scatter_dimension=2, tiled=True)]
    pallas_call x0 -> x11, Pallas kernels: none -> 196 us  [the longest x5 127 us: add_rows(): pl.pallas_call(functools.partial(rows_kernel, count, total is None), out_...]
    all_gather x1, waiting for transfers between devices: 176 us -> 0.01 us  [local(): all_orbitals = lax.all_gather(orbitals, 'row', axis=0, tiled=True)]
    dot_general x8 -> x0, matrix products: 153 us -> none  [the longest x1 45.9 us: local(): jnp.einsum('drc,co->dro', block_matrix, orbital_cols, precision=PRECISE)]
    ppermute x0 -> x10, waiting for transfers between devices: none -> 133 us  [the longest x3 67.1 us: local(): up = lax.ppermute(up, 'col', forward)]
    all_to_all x2 -> x1, waiting for transfers between devices: 182 us -> 73 us  [local(): lax.all_to_all(a.reshape(device_count, -1, LANES), ('row', 'col'), split_...]
    psum x2 -> x0, waiting for transfers between devices: 82.2 us -> none  [from_root(): return lax.psum(kept, axis)]
    all_to_all x0 -> x1, blocking collectives: none -> 74.7 us  [local(): lax.all_to_all(a.reshape(device_count, -1, LANES), ('row', 'col'), split_...]
  transfers between devices with their start and end apart: 6 -> 12, of which waited for: 5 -> 4; matrix products, arithmetic and copies ran while one was open for 17% -> 4% of each run, Pallas kernels for 0% -> 24%
where the time goes in v1:
time: 603 us; the launch traced here: 602 us
  waiting for transfers between devices  207 us (34%)
  Pallas kernels  196 us (33%)
  blocking collectives  93.8 us (16%)
  between operations  35.8 us (6%)
  starting transfers between devices  26.1 us (4%)
  other arithmetic  25.4 us (4%)
  local copies, waits for them, and re-layouts  18 us (3%)
    pallas_call x5, Pallas kernels, add_rows(): pl.pallas_call(functools.partial(rows_kernel, count, total is None), out_...  127 us
    all_to_all x1, blocking collectives, local(): lax.all_to_all(a.reshape(device_count, -1, LANES), ('row', 'col'), split_...  74.7 us
    all_to_all x1, waiting for transfers between devices, local(): lax.all_to_all(a.reshape(device_count, -1, LANES), ('row', 'col'), split_...  73 us
    ppermute x3, waiting for transfers between devices, local(): up = lax.ppermute(up, 'col', forward)  67.1 us
    ppermute x2, waiting for transfers between devices, row_broadcast(): got = lax.ppermute(value, ('row', 'col'), pairs)  66.2 us
    unnamed x1, blocking collectives  19.1 us
    pallas_call x1, Pallas kernels, first_term(): pl.pallas_call(functools.partial(first_kernel, nd), out_shape=jax.ShapeDt...  17.7 us
    pallas_call x1, Pallas kernels, second_term(): pl.pallas_call(functools.partial(second_kernel, nd), out_shape=jax.ShapeD...  17 us
  transfers between devices with their start and end apart: 12, of which 4 were waited for; matrix products, arithmetic and copies ran while one was open for 4% of the time, Pallas kernels for 24%

profile of v1, /device:TPU:0, one launch (start us, length us, event | category | flops | bytes accessed | tf_op | source)
XLA Modules:
  0.0 602.3 jit_solution(2549450930284182370)
XLA Ops:
  8.3 3.0 pick_tiles.1
  11.4 7.4 %all-to-all-start = ((f32[32,192,128]{2,1,0:T(8,128)}), f32[32,192,128]{2,1,0:T(8,128)}, u32[]{:S(2)}, u32[]{:S(2)}) async-start(f32[32,192,128]{2,1,0:T(8,128)} %bitcast.8), calls=%async_computation | async-start | bytes 6291456 | tf_op jit(solution)/shard_map/all_to_all | solution.py:444
  19.0 73.0 %all-to-all-done = f32[32,192,128]{2,1,0:T(8,128)} async-done(((f32[32,192,128]{2,1,0:T(8,128)}), f32[32,192,128]{2,1,0:T(8,128)}, u32[]{:S(2)}, u32[]{:S(2)}) %all-to-all-start) | async-done | bytes 3145760 | tf_op jit(solution)/shard_map/all_to_all | solution.py:444
  92.0 14.0 %batch_tiles.1 = f32[64,3,32,128]{3,2,1,0:T(8,128)S(1)} custom-call(s32[8]{0:T(128)S(1)} %and_select_fusion.col_ref, f32[64,3,32,128]{3,2,1,0:T(8,128)} %bitcast.9.tiles_ref, f32[512,1024]{1,0:T(8,128)S(1)} %bitcast.63, f32[1,1024]{1,0:T(1,128)S(1)} %copy-done.3, f32[1,1024]{1,0:T(1,128)S(1)} %copy-done.4, f32[3,1,1024]{2,1,0:T(1,128)S(1)} %copy-done.2), custom_call_target="tpu_custom_call" | custom-call | tf_op jit(solution)/shard_map/batch_tiles/pallas_call | solution.py:130
  106.0 74.7 %all_to_all.10 = f32[32,192,128]{2,1,0:T(8,128)S(1)} all-to-all(f32[32,192,128]{2,1,0:T(8,128)S(1)} %bitcast.61), channel_id=1, replica_groups=mesh['row'=4,'col'=8] {'row','col'}, dimensions={0} | all-to-all | bytes 6291456 | tf_op jit(solution)/shard_map/all_to_all | solution.py:444
  184.3 34.0 %collective-permute-done.refs_3_ = f32[32,3,32,128]{3,2,1,0:T(8,128)S(1)} collective-permute-done((f32[32,3,32,128]{3,2,1,0:T(8,128)S(1)}, f32[32,3,32,128]{3,2,1,0:T(8,128)S(1)}, u32[]{:S(2)}, u32[]{:S(2)}) %collective-permute-start) | collective-permute-done | bytes 1572896 | tf_op jit(solution)/shard_map/ppermute | solution.py:477
  220.3 33.2 %collective-permute-done.1.refs_3_ = f32[32,3,32,128]{3,2,1,0:T(8,128)} collective-permute-done((f32[32,3,32,128]{3,2,1,0:T(8,128)S(1)}, f32[32,3,32,128]{3,2,1,0:T(8,128)}, u32[]{:S(2)}, u32[]{:S(2)}) %collective-permute-start.1) | collective-permute-done | bytes 1572896 | tf_op jit(solution)/shard_map/ppermute | solution.py:477
  274.9 19.1 %all-reduce = s32[256]{0:T(256)S(1)} all-reduce(s32[256]{0:T(256)S(1)} %dynamic-update-slice), channel_id=2, replica_groups=mesh['row'=4,'col'=8] {'col'}, use_global_device_ids=true, to_apply=%add | all-reduce | flops 256 | bytes 2048
  296.7 2.1 reshape.46.diag_ref
  319.7 17.0 %add_rows.5.refs_7_ = f32[32,192,512]{2,1,0:T(8,128)} custom-call(s32[1]{0:T(128)} %get-tuple-element.31.refs_0_, s32[32]{0:T(128)} %get-tuple-element.18.refs_1_, s32[32]{0:T(128)} %get-tuple-element.11.refs_2_, f32[32,3,32,128]{3,2,1,0:T(8,128)} %copy-done, f32[8192,512]{1,0:T(8,128)} %all-gather.3.cloned.1.call-done.refs_4_.refs_5_.refs_6_), custom_call_target="tpu_custom_call" | custom-call | tf_op jit(solution)/shard_map/add_rows/pallas_call | solution.py:236
  336.7 29.6 %add_rows.6.refs_7_ = f32[32,192,512]{2,1,0:T(8,128)} custom-call(s32[2]{0:T(128)} %pad_add_fusion.9.refs_0_, s32[64]{0:T(128)} %get-tuple-element.47.refs_1_, s32[64]{0:T(128)} %get-tuple-element.48.refs_2_, f32[32,3,32,128]{3,2,1,0:T(8,128)} %copy-done.7, f32[32,3,32,128]{3,2,1,0:T(8,128)} %copy-done.8, ...), custom_call_target="tpu_custom_call", output_to_operand_aliasing={{}: (7, {})} | custom-call | tf_op jit(solution)/shard_map/add_rows/pallas_call | solution.py:236
  366.3 29.6 %add_rows.7.refs_7_ = f32[32,192,512]{2,1,0:T(8,128)} custom-call(s32[2]{0:T(128)} %pad_add_fusion.6.refs_0_, s32[64]{0:T(128)} %get-tuple-element.45.refs_1_, s32[64]{0:T(128)} %get-tuple-element.46.refs_2_, f32[32,3,32,128]{3,2,1,0:T(8,128)} %collective-permute-done.1.refs_3_, ...), custom_call_target="tpu_custom_call", output_to_operand_aliasing={{}: (7, {})} | custom-call | tf_op jit(solution)/shard_map/add_rows/pallas_call | solution.py:236
  395.9 29.6 %add_rows.8.refs_7_ = f32[32,192,512]{2,1,0:T(8,128)} custom-call(s32[2]{0:T(128)} %pad_add_fusion.3.refs_0_, s32[64]{0:T(128)} %get-tuple-element.43.refs_1_, s32[64]{0:T(128)} %get-tuple-element.44.refs_2_, f32[32,3,32,128]{3,2,1,0:T(8,128)} %copy-done.5, f32[32,3,32,128]{3,2,1,0:T(8,128)} %collective-permute-done.6.refs_4_, ...), custom_call_target="tpu_custom_call", output_to_operand_aliasing={{}: (7, {})} | custom-call | tf_op jit(solution)/shard_map/add_rows/pallas_call | solution.py:236
  425.5 21.1 %add_rows.9.total_ref = f32[32,192,512]{2,1,0:T(8,128)} custom-call(s32[2]{0:T(128)} %pad_add_fusion.refs_0_, s32[32]{0:T(128)} %get-tuple-element.41.refs_1_, s32[32]{0:T(128)} %get-tuple-element.42.refs_2_, f32[16,3,32,128]{3,2,1,0:T(8,128)} %collective-permute-done.3.refs_3_, ...), custom_call_target="tpu_custom_call", output_to_operand_aliasing={{}: (7, {})} | custom-call | tf_op jit(solution)/shard_map/add_rows/pallas_call | solution.py:236
  446.6 16.1 %response_orbitals.1 = (f32[32,192,512]{2,1,0:T(8,128)}, f32[3,16,64,512]{3,2,1,0:T(8,128)}) custom-call(s32[1]{0:T(128)} %bitcast.part_ref, f32[32,192,512]{2,1,0:T(8,128)} %add_rows.9.total_ref, f32[32,64,1]{2,1,0:T(8,128)} %reshape.46.diag_ref, f32[1,512]{1,0:T(1,128)} %bitcast.66), custom_call_target="tpu_custom_call" | custom-call | tf_op jit(solution)/shard_map/response_orbitals/pallas_call | solution.py:285
  462.7 6.6 %collective-permute-start.8 = (f32[3,16,64,512]{3,2,1,0:T(8,128)}, f32[3,16,64,512]{3,2,1,0:T(8,128)}, u32[]{:S(2)}, u32[]{:S(2)}) collective-permute-start(f32[3,16,64,512]{3,2,1,0:T(8,128)} %get-tuple-element.7), channel_id=1, source_target_pairs={{0,16},{1,17},{10,26},{11,27},{20,4},{21,5},{30,14},{31,15}} | collective-permute-start | bytes 18874376 | tf_op jit(solution)/shard_map/ppermute | solution.py:390
  469.2 66.2 %collective-permute-done.8 = f32[3,16,64,512]{3,2,1,0:T(8,128)} collective-permute-done((f32[3,16,64,512]{3,2,1,0:T(8,128)}, f32[3,16,64,512]{3,2,1,0:T(8,128)}, u32[]{:S(2)}, u32[]{:S(2)}) %collective-permute-start.8) | collective-permute-done | bytes 6291488 | tf_op jit(solution)/shard_map/ppermute | solution.py:390
  535.4 7.6 %broadcast_select_fusion = f32[3,16,64,512]{3,2,1,0:T(8,128)} fusion(f32[3,16,64,512]{3,2,1,0:T(8,128)} %collective-permute-done.8, f32[3,16,64,512]{3,2,1,0:T(8,128)} %get-tuple-element.7, pred[]{:T(512)S(6)} %and.101), kind=kLoop, calls=%fused_computation | loop fusion | flops 1572864 | bytes 18874368 | tf_op jit(solution)/shard_map/jit(_where)/select_n | solution.py:393
  543.0 3.9 collective-permute-start.9
  547.5 3.1 constant_dynamic-slice_fusion.orb_ref
  550.6 17.7 %first_term.1.first_ref = f32[3,32,32,128]{3,2,1,0:T(8,128)} custom-call(s32[32]{0:T(128)} %get-tuple-element.40.row_id, s32[32]{0:T(128)} %get-tuple-element.39.col_id, f32[32,192,512]{2,1,0:T(8,128)} %get-tuple-element.8.x_ref, f32[1024,512]{1,0:T(8,128)} %constant_dynamic-slice_fusion.orb_ref), custom_call_target="tpu_custom_call" | custom-call | tf_op jit(solution)/shard_map/first_term/pallas_call | solution.py:329
  568.3 7.6 %broadcast_select_fusion.1.x_ref = f32[3,16,64,512]{3,2,1,0:T(8,128)} fusion(f32[3,16,64,512]{3,2,1,0:T(8,128)} %collective-permute-done.9, f32[3,16,64,512]{3,2,1,0:T(8,128)} %broadcast_select_fusion, pred[]{:T(512)S(6)} %and.98), kind=kLoop, calls=%fused_computation.1 | loop fusion | flops 1572864 | bytes 18874368 | tf_op jit(solution)/shard_map/jit(_where)/select_n | solution.py:393
  575.9 17.0 %second_term.1 = f32[3,32,32,128]{3,2,1,0:T(8,128)} custom-call(s32[32]{0:T(128)} %get-tuple-element.40.row_id, s32[32]{0:T(128)} %get-tuple-element.39.col_id, f32[3,16,64,512]{3,2,1,0:T(8,128)} %broadcast_select_fusion.1.x_ref, f32[2048,512]{1,0:T(8,128)} %orb_ref.1, f32[3,32,32,128]{3,2,1,0:T(8,128)} %first_term.1.first_ref), custom_call_target="tpu_custom_call" | custom-call | tf_op jit(solution)/shard_map/second_term/pallas_call | solution.py:365
  592.9 2.6 reshape.39
  (82 shorter events, 31.0 us)
Async XLA Ops:
  6.5 313.2 %all-gather.3.cloned.1.call-start = ((), (), s32[]{:S(2)}) async-start(), calls=%async_computation.2 | async-start | bytes 20971520 | tf_op jit(solution)/shard_map/all_gather | solution.py:440
  11.3 80.6 %copy-start.1 = (f32[1,512,1024]{2,1,0:T(8,128)S(1)}, f32[1,512,1024]{2,1,0:T(8,128)}, u32[]{:S(2)}) copy-start(f32[1,512,1024]{2,1,0:T(8,128)} %param.15) | copy-start | bytes 6291460
  11.4 80.6 %copy-start.2 = (f32[3,1,1024]{2,1,0:T(1,128)S(1)}, f32[3,1,1024]{2,1,0:T(1,128)}, u32[]{:S(2)}) copy-start(f32[3,1,1024]{2,1,0:T(1,128)} %coord_ref.1) | copy-start | bytes 36868
  11.4 80.6 %copy-start.3 = (f32[1,1024]{1,0:T(1,128)S(1)}, f32[1,1024]{1,0:T(1,128)}, u32[]{:S(2)}) copy-start(f32[1,1024]{1,0:T(1,128)} %weight_ref.1) | copy-start | bytes 12292
  11.4 80.6 %copy-start.4 = (f32[1,1024]{1,0:T(1,128)S(1)}, f32[1,1024]{1,0:T(1,128)}, u32[]{:S(2)}) copy-start(f32[1,1024]{1,0:T(1,128)} %xc_ref.1) | copy-start | bytes 12292
  11.4 80.6 %all-to-all-start = ((f32[32,192,128]{2,1,0:T(8,128)}), f32[32,192,128]{2,1,0:T(8,128)}, u32[]{:S(2)}, u32[]{:S(2)}) async-start(f32[32,192,128]{2,1,0:T(8,128)} %bitcast.8), calls=%async_computation | async-start | bytes 6291456 | tf_op jit(solution)/shard_map/all_to_all | solution.py:444
  180.7 74.8 %copy-start.14 = (s32[8]{0:T(128)S(1)}, s32[8]{0:T(128)}, u32[]{:S(2)}) copy-start(s32[8]{0:T(128)} %constant.164.clone) | copy-start | bytes 100
  180.7 82.0 %copy-start.9 = (s32[8]{0:T(128)S(1)}, s32[8]{0:T(128)}, u32[]{:S(2)}) copy-start(s32[8]{0:T(128)} %constant.163.clone) | copy-start | bytes 100
  180.7 92.7 %copy-start.13 = (u32[32]{0:T(128)S(1)}, u32[32]{0:T(128)}, u32[]{:S(2)}) copy-start(u32[32]{0:T(128)} %constant.171) | copy-start | bytes 388
  180.7 113.4 %copy-start.11 = (f32[2048]{0:T(1024)S(1)}, f32[2048]{0:T(1024)}, u32[]{:S(2)}) copy-start(f32[2048]{0:T(1024)} %param.20) | copy-start | bytes 24580
  182.2 137.5 %copy-start = (f32[32,3,32,128]{3,2,1,0:T(8,128)}, f32[32,3,32,128]{3,2,1,0:T(8,128)S(1)}, u32[]{:S(2)}) copy-start(f32[32,3,32,128]{3,2,1,0:T(8,128)S(1)} %add_tiles.1.refs_3_) | copy-start | bytes 4718596
  182.2 36.0 %collective-permute-start = (f32[32,3,32,128]{3,2,1,0:T(8,128)S(1)}, f32[32,3,32,128]{3,2,1,0:T(8,128)S(1)}, u32[]{:S(2)}, u32[]{:S(2)}) collective-permute-start(f32[32,3,32,128]{3,2,1,0:T(8,128)S(1)} %add_tiles.1.refs_3_), channel_id=1, source_target_pairs={{0,2},{2,4},{4,6},{6,7},{7,5},{5,3},{3,1},{1,0},{8,10},{10,12},{12... | collective-permute-start | bytes 4718600 | tf_op jit(solution)/shard_map/ppermute | solution.py:477
  182.4 36.8 %collective-permute-start.4 = (f32[32,3,32,128]{3,2,1,0:T(8,128)S(1)}, f32[32,3,32,128]{3,2,1,0:T(8,128)S(1)}, u32[]{:S(2)}, u32[]{:S(2)}) collective-permute-start(f32[32,3,32,128]{3,2,1,0:T(8,128)S(1)} %add_tiles.1.refs_3_), channel_id=1, source_target_pairs={{2,0},{4,2},{6,4},{7,6},{5,7},{3,5},{1,3},{0,1},{10,8},{12,10},{14... | collective-permute-start | bytes 4718600 | tf_op jit(solution)/shard_map/ppermute | solution.py:478
  218.3 2.0 copy-start.7
  218.3 35.2 %collective-permute-start.1 = (f32[32,3,32,128]{3,2,1,0:T(8,128)S(1)}, f32[32,3,32,128]{3,2,1,0:T(8,128)}, u32[]{:S(2)}, u32[]{:S(2)}) collective-permute-start(f32[32,3,32,128]{3,2,1,0:T(8,128)S(1)} %collective-permute-done.refs_3_), channel_id=1, source_target_pairs={{0,2},{2,4},{4,6},{6,7},{7,5},{5,3},{3,1},{1,0},{8,10},{10,12},{12... | collective-permute-start | bytes 4718600 | tf_op jit(solution)/shard_map/ppermute | solution.py:477
  219.2 34.3 %copy-start.8 = (f32[32,3,32,128]{3,2,1,0:T(8,128)}, f32[32,3,32,128]{3,2,1,0:T(8,128)S(1)}, u32[]{:S(2)}) copy-start(f32[32,3,32,128]{3,2,1,0:T(8,128)S(1)} %collective-permute-done.4.refs_4_) | copy-start | bytes 4718596
  219.2 36.1 %collective-permute-start.5 = (f32[32,3,32,128]{3,2,1,0:T(8,128)S(1)}, f32[32,3,32,128]{3,2,1,0:T(8,128)}, u32[]{:S(2)}, u32[]{:S(2)}) collective-permute-start(f32[32,3,32,128]{3,2,1,0:T(8,128)S(1)} %collective-permute-done.4.refs_4_), channel_id=1, source_target_pairs={{2,0},{4,2},{6,4},{7,6},{5,7},{3,5},{1,3},{0,1},{10,8},{12,10},{14... | collective-permute-start | bytes 4718600 | tf_op jit(solution)/shard_map/ppermute | solution.py:478
  253.5 52.9 %collective-permute-start.2 = (f32[32,3,32,128]{3,2,1,0:T(8,128)}, f32[32,3,32,128]{3,2,1,0:T(8,128)S(1)}, u32[]{:S(2)}, u32[]{:S(2)}) collective-permute-start(f32[32,3,32,128]{3,2,1,0:T(8,128)} %collective-permute-done.1.refs_3_), channel_id=1, source_target_pairs={{0,2},{2,4},{4,6},{6,7},{7,5},{5,3},{3,1},{1,0},{8,10},{10,12},{12... | collective-permute-start | bytes 4718600 | tf_op jit(solution)/shard_map/ppermute | solution.py:477
  255.3 52.1 %collective-permute-start.6 = (f32[32,3,32,128]{3,2,1,0:T(8,128)}, f32[32,3,32,128]{3,2,1,0:T(8,128)}, u32[]{:S(2)}, u32[]{:S(2)}) collective-permute-start(f32[32,3,32,128]{3,2,1,0:T(8,128)} %collective-permute-done.5.refs_4_), channel_id=1, source_target_pairs={{2,0},{4,2},{6,4},{7,6},{5,7},{3,5},{1,3},{0,1},{10,8},{12,10},{14... | collective-permute-start | bytes 4718600 | tf_op jit(solution)/shard_map/ppermute | solution.py:478
  306.4 30.3 %copy-start.5 = (f32[32,3,32,128]{3,2,1,0:T(8,128)}, f32[32,3,32,128]{3,2,1,0:T(8,128)S(1)}, u32[]{:S(2)}) copy-start(f32[32,3,32,128]{3,2,1,0:T(8,128)S(1)} %collective-permute-done.2.refs_3_) | copy-start | bytes 4718596
  307.4 118.1 %collective-permute-start.3 = (f32[16,3,32,128]{3,2,1,0:T(8,128)}, f32[16,3,32,128]{3,2,1,0:T(8,128)}, u32[]{:S(2)}, u32[]{:S(2)}) collective-permute-start(f32[16,3,32,128]{3,2,1,0:T(8,128)} %slice.8), channel_id=1, source_target_pairs={{0,2},{2,4},{4,6},{6,7},{7,5},{5,3},{3,1},{1,0},{8,10},{10,12},{12... | collective-permute-start | bytes 2359304 | tf_op jit(solution)/shard_map/ppermute | solution.py:481
  309.5 116.0 %collective-permute-start.7 = (f32[16,3,32,128]{3,2,1,0:T(8,128)}, f32[16,3,32,128]{3,2,1,0:T(8,128)}, u32[]{:S(2)}, u32[]{:S(2)}) collective-permute-start(f32[16,3,32,128]{3,2,1,0:T(8,128)} %slice.9), channel_id=1, source_target_pairs={{2,0},{4,2},{6,4},{7,6},{5,7},{3,5},{1,3},{0,1},{10,8},{12,10},{14... | collective-permute-start | bytes 2359304 | tf_op jit(solution)/shard_map/ppermute | solution.py:482
  462.7 72.7 %collective-permute-start.8 = (f32[3,16,64,512]{3,2,1,0:T(8,128)}, f32[3,16,64,512]{3,2,1,0:T(8,128)}, u32[]{:S(2)}, u32[]{:S(2)}) collective-permute-start(f32[3,16,64,512]{3,2,1,0:T(8,128)} %get-tuple-element.7), channel_id=1, source_target_pairs={{0,16},{1,17},{10,26},{11,27},{20,4},{21,5},{30,14},{31,15}} | collective-permute-start | bytes 18874376 | tf_op jit(solution)/shard_map/ppermute | solution.py:390
  543.0 25.3 %collective-permute-start.9 = (f32[3,16,64,512]{3,2,1,0:T(8,128)}, f32[3,16,64,512]{3,2,1,0:T(8,128)}, u32[]{:S(2)}, u32[]{:S(2)}) collective-permute-start(f32[3,16,64,512]{3,2,1,0:T(8,128)} %broadcast_select_fusion), channel_id=1, source_target_pairs={{0,8},{16,24},{1,9},{17,25},{10,2},{26,18},{11,3},{27,19},{4,12},{... | collective-permute-start | bytes 18874376 | tf_op jit(solution)/shard_map/ppermute | solution.py:390
  (3 other events, 3.9 us)
Sparse Core Ops, SparseCore 0:
  8.9 170.9 all-gather.2

commit v2 on v0

v2 whole, which is shorter than its diff:
```python
import functools

import jax
import jax.numpy as jnp
from jax import lax
from jax.experimental import pallas as pl
from jax.experimental.pallas import tpu as pltpu
from jax.sharding import PartitionSpec as P

NB = 8192
TILE = 64
FB = 8
LANES = 2 * TILE
ROWS = TILE * TILE // LANES
F32 = jnp.float32
BF16 = jnp.bfloat16
NT = (((1,), (1,)), ((), ()))


def split(value):
    high = value.astype(BF16)
    return high, (value - high.astype(F32)).astype(BF16)


def dot(a, b):
    return jnp.dot(a, b, preferred_element_type=F32)


def dot_nt(a, b):
    return lax.dot_general(a, b, NT, preferred_element_type=F32)


def low_lanes(shape):
    return lax.broadcasted_iota(jnp.int32, shape, len(shape) - 1) < TILE


def params(mib):
    return pltpu.CompilerParams(vmem_limit_bytes=mib * 2**20)


VMEM = pl.BlockSpec(memory_space=pltpu.VMEM)
SMEM = pl.BlockSpec(memory_space=pltpu.SMEM)


def in_groups(count, body, group=16):
    if count % group:
        group = 1

    def step(g, carry):
        body([g * group + u for u in range(group)])
        return carry

    lax.fori_loop(0, count // group, step, 0)


def pick_kernel(slot_ref, tiles_ref, ids_ref, out_ref, rows):
    nd, slots, area = tiles_ref.shape
    per_range = slot_ref.shape[0] // out_ref.shape[0]
    for d in range(nd):
        for start in range(0, slots, 8):
            for k in range(area // LANES):
                rows[d, pl.ds(start * ROWS + k, 8, stride=ROWS), :] = tiles_ref[
                    d, start : start + 8, k * LANES : (k + 1) * LANES
                ]

    def device(index):
        for n in index:
            for k in range(per_range):
                slot = slot_ref[n * per_range + k]
                first = pl.multiple_of(jnp.maximum(slot, 0) * ROWS, ROWS)
                for d in range(nd):
                    out_ref[n, (k * nd + d) * ROWS : (k * nd + d + 1) * ROWS] = jnp.where(
                        slot >= 0, rows[d, pl.ds(first, ROWS), :], 0.0
                    )
            out_ref[n, per_range * nd * ROWS :] = ids_ref[...]

    in_groups(out_ref.shape[0], device, 2)


def pick_tiles(slots, tiles, ids, device_count):
    nd, count, area = tiles.shape
    rows = slots.shape[0] // device_count * nd * ROWS + ids.shape[0]
    return pl.pallas_call(
        pick_kernel,
        out_shape=jax.ShapeDtypeStruct((device_count, rows, LANES), F32),
        in_specs=[SMEM, VMEM, VMEM],
        out_specs=VMEM,
        scratch_shapes=[pltpu.VMEM((nd, count * ROWS, LANES), F32)],
        compiler_params=params(32),
        name="pick_tiles",
    )(slots, tiles, ids)


def batch_kernel(
    per_range, col_count, col_ref, tiles_ref, basis_ref, weight_ref, xc_ref, coord_ref, out_ref,
    bh, bl, wh, wl, square,
):
    nd = coord_ref.shape[0]
    width, pts = basis_ref.shape
    low = low_lanes((ROWS, LANES))
    if col_count > FB:
        out_ref[...] = jnp.zeros(out_ref.shape, F32)

    def place(i, j, d):
        owner = (i // per_range) * col_count + col_ref[j]
        return owner, pl.ds(pl.multiple_of((i % per_range * nd + d) * ROWS, ROWS), ROWS)

    high, rest = split(basis_ref[...])
    bh[...] = high
    bl[...] = rest

    def direction(d, carry):
        for i in range(FB):
            for jj in range(FB // 2):
                first = tiles_ref[place(i, 2 * jj, d)]
                second = tiles_ref[place(i, 2 * jj + 1, d)]
                square[jj, pl.ds(i * TILE, ROWS, stride=2), :] = jnp.where(
                    low, first, pltpu.roll(second, TILE, 1)
                )
                square[jj, pl.ds(i * TILE + 1, ROWS, stride=2), :] = jnp.where(
                    low, pltpu.roll(first, TILE, 1), second
                )
        eh, el = split(jnp.concatenate([square[jj] for jj in range(FB // 2)], axis=1))
        piece = 256
        for start in range(0, pts, piece):
            cols = slice(start, start + piece)
            projected = dot(eh, bh[:, cols]) + dot(eh, bl[:, cols]) + dot(el, bh[:, cols])
            values = basis_ref[:, cols]
            response = jnp.sum(values * projected, axis=0, keepdims=True)
            potential = xc_ref[:, cols] * response + coord_ref[d, :, cols]
            weighted = values * (weight_ref[:, cols] * potential)
            high, rest = split(weighted)
            wh[:, cols] = high
            wl[:, cols] = rest
        for start in range(0, width, piece):
            rows = slice(start, start + piece)
            value = (
                dot_nt(wh[...], bh[rows]) + dot_nt(wh[...], bl[rows]) + dot_nt(wl[...], bh[rows])
            )
            for lane in range(0, piece, LANES):
                square[(start + lane) // LANES] = value[:, lane : lane + LANES]
        for i in range(FB):
            for jj in range(FB // 2):
                even = square[jj, pl.ds(i * TILE, ROWS, stride=2), :]
                odd = square[jj, pl.ds(i * TILE + 1, ROWS, stride=2), :]
                out_ref[place(i, 2 * jj, d)] = jnp.where(low, even, pltpu.roll(odd, TILE, 1))
                out_ref[place(i, 2 * jj + 1, d)] = jnp.where(low, pltpu.roll(even, TILE, 1), odd)
        return carry

    lax.fori_loop(0, nd, direction, 0)


def batch_tiles(per_range, col_count, cols, tiles, basis, weight, xc, coord):
    width, pts = basis.shape
    return pl.pallas_call(
        functools.partial(batch_kernel, per_range, col_count),
        out_shape=jax.ShapeDtypeStruct(
            (tiles.shape[0], per_range * coord.shape[0] * ROWS, LANES), F32
        ),
        in_specs=[SMEM] + [VMEM] * 5,
        out_specs=VMEM,
        scratch_shapes=[
            pltpu.VMEM((width, pts), BF16),
            pltpu.VMEM((width, pts), BF16),
            pltpu.VMEM((width, pts), BF16),
            pltpu.VMEM((width, pts), BF16),
            pltpu.VMEM((width // LANES, width, LANES), F32),
        ],
        compiler_params=params(48),
        name="batch_tiles",
    )(cols, tiles, basis, weight, xc, coord)


def add_kernel(slot_ref, tiles_ref, *out_refs):
    for out_ref in out_refs:
        out_ref[...] = jnp.zeros(out_ref.shape, F32)

    nd = len(out_refs)
    per_range = slot_ref.shape[0] // tiles_ref.shape[0]

    def step(n, carry):
        for k in range(per_range):
            slot = slot_ref[n * per_range + k]

            @pl.when(slot >= 0)
            def _(slot=slot, k=k):
                for d, out_ref in enumerate(out_refs):
                    start = (k * nd + d) * ROWS
                    out_ref[slot] += tiles_ref[n, start : start + ROWS]

        return carry

    lax.fori_loop(0, tiles_ref.shape[0], step, 0)


def add_tiles(slots, tiles, slot_count, nd):
    return pl.pallas_call(
        add_kernel,
        out_shape=[jax.ShapeDtypeStruct((slot_count, ROWS, LANES), F32)] * nd,
        in_specs=[SMEM, VMEM],
        out_specs=[VMEM] * nd,
        compiler_params=params(32),
        name="add_tiles",
    )(slots, tiles)


def split_kernel(orb_ref, out_ref):
    def blocks(index):
        for b in index:
            high, rest = split(orb_ref[pl.ds(pl.multiple_of(b * TILE, TILE), TILE), :])
            out_ref[b, :TILE] = high
            out_ref[b, TILE:] = rest

    in_groups(out_ref.shape[0], blocks, 2)


def split_orbitals(orbitals, parts):
    count, nocc = orbitals.shape
    return pl.pallas_call(
        split_kernel,
        out_shape=jax.ShapeDtypeStruct((count // TILE, 2 * TILE, nocc), BF16),
        grid=(parts,),
        in_specs=[pl.BlockSpec((count // parts, nocc), lambda g: (g, 0))],
        out_specs=pl.BlockSpec((count // parts // TILE, 2 * TILE, nocc), lambda g: (g, 0, 0)),
        compiler_params=params(32),
        cost_estimate=pl.CostEstimate(
            flops=0, bytes_accessed=8 * count * nocc, transcendentals=0
        ),
        name="split_orbitals",
    )(orbitals)


def accumulate(chunks, orbs, row_id, col_id, sums):
    low = low_lanes((ROWS, LANES))
    nd = len(sums)
    offset = 0
    for chunk, orb in zip(chunks, orbs):

        def tiles(index, chunk=chunk, orb=orb, offset=offset):
            products = []
            for s in index:
                left = []
                for d in range(nd):
                    tile = chunk[d][s]
                    turned = pltpu.roll(tile, TILE, 1)
                    for value in (jnp.where(low, tile, turned), jnp.where(low, turned, tile)):
                        left.append(jnp.concatenate(split(value), axis=1))
                left = jnp.concatenate(left, axis=0)
                pair = orb[col_id[offset + s]]
                products.append(dot(left, jnp.concatenate([pair, pair], axis=0)))
            for s, product in zip(index, products):
                block = row_id[offset + s]
                for d in range(nd):
                    sums[d][block] += product[d * TILE : (d + 1) * TILE]

        in_groups(chunk[0].shape[0], tiles)
        offset += chunk[0].shape[0]


def whole(a):
    return pl.BlockSpec(a.shape, lambda g, *_, n=len(a.shape): (0,) * n)


def orb_spec(blocks, orbs, which):
    return pl.BlockSpec((blocks,) + orbs.shape[1:], lambda g, *t: (which(*t), 0, 0))


def call(kernel, name, tables, args, specs, out, scratch, products, mib=60):
    single = not isinstance(out, (tuple, list))
    return pl.pallas_call(
        kernel,
        out_shape=out,
        grid_spec=pltpu.PrefetchScalarGridSpec(
            num_scalar_prefetch=len(tables),
            grid=(1,),
            in_specs=specs,
            out_specs=whole(out) if single else [whole(o) for o in out],
            scratch_shapes=scratch,
        ),
        compiler_params=params(mib),
        cost_estimate=pl.CostEstimate(
            flops=products * 100_000_000, bytes_accessed=2**23, transcendentals=0
        ),
        name=name,
    )(*tables, *args)


def rows_kernel(count, nd, row_id, col_id, place_ref, *refs):
    chunks = [refs[nd * k : nd * (k + 1)] for k in range(count)]
    orbs, sums = refs[nd * count : (nd + 1) * count], refs[(nd + 1) * count :]
    for total in sums:
        total[...] = jnp.zeros(total.shape, F32)
    accumulate(chunks, orbs, row_id, col_id, sums)


def add_rows(chunks, where, orbs, row_blocks, col_blocks):
    count = len(chunks)
    nd = len(chunks[0])
    flat = [c for chunk in chunks for c in chunk]
    specs = [whole(c) for c in flat]
    specs += [orb_spec(col_blocks, orbs, lambda r, c, p, k=k: p[k]) for k in range(count)]
    out = jax.ShapeDtypeStruct((row_blocks, TILE, orbs.shape[2]), F32)
    return call(
        functools.partial(rows_kernel, count, nd), "add_rows", where, flat + [orbs] * count, specs,
        [out] * nd, [], count * flat[0].shape[0],
    )


def piece_kernel(count, row_id, col_id, place_ref, *refs):
    chunks, orbs, refs = refs[:count], refs[count : 2 * count - 1], refs[2 * count - 1 :]
    in_ref, diag_ref, energy_ref, piece_ref, total_ref, sums, square, sem = refs
    load = pltpu.make_async_copy(in_ref, sums, sem)
    load.start()
    load.wait()
    accumulate([[c] for c in chunks], orbs + orbs[-1:], row_id, col_id, [sums])
    store = pltpu.make_async_copy(sums, total_ref, sem)
    store.start()
    first = place_ref[count - 1] * piece_ref.shape[0]

    def blocks(index):
        for b in index:
            value = sums[first + b] * (-1.0 / (diag_ref[first + b] - energy_ref[...]))
            for k in range(square.shape[1]):
                lanes = slice(k * LANES, (k + 1) * LANES)
                for parity in range(2):
                    square[b % 2, k, pl.ds(parity, ROWS, stride=2), :] = value[
                        parity * ROWS : (parity + 1) * ROWS, lanes
                    ]
                piece_ref[b, :, lanes] = square[b % 2, k]

    in_groups(piece_ref.shape[0], blocks, 2)
    store.wait()


def response_piece(total, chunks, where, orbs, diag, energy, col_blocks):
    count = len(chunks)
    nocc = orbs.shape[2]
    hbm = pl.BlockSpec(memory_space=pl.ANY)
    specs = [whole(c) for c in chunks]
    specs += [orb_spec(col_blocks, orbs, lambda r, c, p, k=k: p[k]) for k in range(count - 1)]
    specs += [hbm, whole(diag), whole(energy)]
    piece = jax.ShapeDtypeStruct((col_blocks, TILE, nocc), F32)
    return pl.pallas_call(
        functools.partial(piece_kernel, count),
        out_shape=(piece, jax.ShapeDtypeStruct(total.shape, F32)),
        grid_spec=pltpu.PrefetchScalarGridSpec(
            num_scalar_prefetch=3,
            grid=(1,),
            in_specs=specs,
            out_specs=(whole(piece), hbm),
            scratch_shapes=[
                pltpu.VMEM(total.shape, F32),
                pltpu.VMEM((2, nocc // LANES, TILE, LANES), F32),
                pltpu.SemaphoreType.DMA,
            ],
        ),
        compiler_params=params(60),
        cost_estimate=pl.CostEstimate(
            flops=20_000_000_000, bytes_accessed=2**23, transcendentals=0
        ),
        name="response_piece",
    )(*where, *chunks, *[orbs] * (count - 1), total, diag, energy)


def first_kernel(nd, row_id, col_id, place_ref, *refs):
    totals, (diag_ref, energy_ref, orb_ref, out_ref) = refs[:nd], refs[nd:]
    low = low_lanes((ROWS, LANES))

    def tiles(index):
        for s in index:
            block = row_id[s]
            inverse = -1.0 / (diag_ref[block] - energy_ref[...])
            left = [part for total in totals for part in split(total[block] * inverse)]
            value = dot_nt(jnp.concatenate(left, axis=0), orb_ref[col_id[s]])
            for d in range(nd):
                start = 2 * d * TILE
                tile = value[start : start + TILE] + value[start + TILE : start + 2 * TILE]
                tile = tile + pltpu.roll(tile, TILE, 1)
                out_ref[d, s] = jnp.where(low, tile[:ROWS], tile[ROWS:])

    in_groups(out_ref.shape[1], tiles, 8)


def first_term(own, places, totals, diag, energy, orbs, col_blocks):
    nd, slots = len(totals), own[0].shape[0]
    specs = [whole(a) for a in [*totals, diag, energy]]
    specs.append(orb_spec(col_blocks, orbs, lambda r, c, p: p[2]))
    return call(
        functools.partial(first_kernel, nd), "first_term", [*own, places],
        [*totals, diag, energy, orbs], specs,
        jax.ShapeDtypeStruct((nd, slots, ROWS, LANES), F32), [], slots,
    )


def second_kernel(directions, way_count, last, row_id, col_id, place_ref, *refs):
    count = len(directions)
    ways = [refs[d * way_count : (d + 1) * way_count] for d in range(count)]
    refs = refs[count * way_count :]
    orb_ref, first_ref, refs = refs[0], refs[1], refs[2:]
    if last:
        done_ref, refs = refs[0], refs[1:]
    out_ref, x_ref, square, sem = refs[:4]
    for d in range(count):
        for k, way in enumerate(ways[d]):

            @pl.when(place_ref[1] == k)
            def _(way=way, d=d):
                pltpu.make_async_copy(way, x_ref.at[d], sem.at[d]).start()

    for d in range(count):
        pltpu.make_async_copy(ways[d][0], x_ref.at[d], sem.at[d]).wait()
    low = low_lanes((ROWS, LANES))
    slots = first_ref.shape[1]

    def tiles(index):
        for u, s in enumerate(index):
            right = [part for d in range(count) for part in split(x_ref[d, col_id[s]])]
            value = dot_nt(orb_ref[row_id[s]], jnp.concatenate(right, axis=0))
            value = value[:TILE] + value[TILE:]
            for d in range(count):
                tile = value[:, d * LANES : (d + 1) * LANES]
                square[d, u] = tile + pltpu.roll(tile, TILE, 1)
        for u, s in enumerate(index):
            for d in range(count):
                even = square[d, u, pl.ds(0, ROWS, stride=2), :]
                odd = square[d, u, pl.ds(1, ROWS, stride=2), :]
                value = first_ref[directions[d], s] + jnp.where(low, even, odd)
                if last:
                    refs[4][d, pl.ds(pl.multiple_of(s * ROWS, ROWS), ROWS), :] = value
                else:
                    out_ref[d, pl.ds(pl.multiple_of(s * ROWS, ROWS), ROWS), :] = value

    in_groups(slots, tiles, square.shape[1])
    if last:
        for d in range(out_ref.shape[0]):
            for start in range(0, slots, 8):
                for k in range(ROWS):
                    rows = pl.ds(start * ROWS + k, 8, stride=ROWS)
                    if d in directions:
                        value = refs[4][directions.index(d), rows, :]
                    else:
                        value = done_ref[d, rows, :]
                    out_ref[d, start : start + 8, k * LANES : (k + 1) * LANES] = value


def second_term(directions, own, places, ways, orbs, first, row_blocks, done=None):
    nd, slots = first.shape[:2]
    count = len(directions)
    last = done is not None
    shape = ways[0][0].shape
    rows = (count, slots * ROWS, LANES)
    scratch = [
        pltpu.VMEM((count,) + shape, F32),
        pltpu.VMEM((count, 8, TILE, LANES), F32),
        pltpu.SemaphoreType.DMA((count,)),
    ]
    if last:
        scratch.append(pltpu.VMEM(rows, F32))
    flat = [way for each in ways for way in each]
    others = [first, done] if last else [first]
    specs = [pl.BlockSpec(memory_space=pl.ANY)] * len(flat)
    specs.append(orb_spec(row_blocks, orbs, lambda r, c, p: p[0]))
    specs += [whole(a) for a in others]
    out = jax.ShapeDtypeStruct((nd, slots, ROWS * LANES) if last else rows, F32)
    return call(
        functools.partial(second_kernel, directions, len(ways[0]), last), "second_term",
        [*own, places], [*flat, orbs, *others], specs, out, scratch, slots,
    )


def after(value, other):
    hbm = pl.BlockSpec(memory_space=pl.ANY)
    return pl.pallas_call(
        lambda value_ref, other_ref, out_ref: None,
        out_shape=jax.ShapeDtypeStruct(value.shape, value.dtype),
        in_specs=[hbm, hbm],
        out_specs=hbm,
        input_output_aliases={0: 0},
        name="after",
    )(value, other)


def ring_order(count):
    return list(range(0, count, 2)) + list(range(count - 1, 0, -2))


def row_broadcast(value, row_count, col_count, ratio, held=None):
    ways = [value]
    for k in range(1, row_count):
        parent = k & (k - 1)
        sent = ways[parent]
        if k & 1:
            rows = [[(r, r ^ 1) for r in range(row_count)]] * col_count
        else:
            rows = [[(c // ratio ^ parent, c // ratio ^ k)] for c in range(col_count)]
        if held is not None and parent:
            sent = after(sent, held(ways))
        pairs = [(a * col_count + c, b * col_count + c) for c in range(col_count) for a, b in rows[c]]
        ways.append(lax.ppermute(sent, ("row", "col"), pairs))
    return ways


def local(
    density_tiles,
    tile_ids,
    batch_blocks,
    basis_values,
    grid_weight,
    xc_kernel,
    grid_coord,
    orbitals,
    precond_diag,
    orbital_energy,
):
    row_count = lax.axis_size("row")
    col_count = lax.axis_size("col")
    device_count = row_count * col_count
    own_row = lax.axis_index("row")
    own_col = lax.axis_index("col")
    own_index = own_row * col_count + own_col
    block_count = NB // TILE
    row_blocks = block_count // row_count
    col_blocks = block_count // col_count
    per_range = FB // row_count
    slot_count = tile_ids.shape[0]
    ratio = col_count // row_count
    col_width = col_blocks * TILE
    nd = density_tiles.shape[0]
    nocc = orbitals.shape[1]

    ask = batch_blocks
    match = ask // col_blocks == own_col
    ask_col = jnp.sum(jnp.where(match, ask, 0), axis=1)
    ask_row = lax.dynamic_slice_in_dim(ask, own_row * per_range, per_range, 1)
    wanted = jnp.where(jnp.any(match, axis=1)[:, None], ask_row * block_count + ask_col[:, None], -1)
    hit = wanted.reshape(-1)[:, None] == tile_ids[None, :]
    slots = jnp.max(jnp.where(hit, jnp.arange(slot_count, dtype=jnp.int32)[None, :], -1), axis=1)
    own_cols = lax.dynamic_slice_in_dim(ask, own_index, 1, 0)[0] // col_blocks

    local_rows = tile_ids // block_count - own_row * row_blocks
    local_cols = tile_ids % col_blocks

    order = ring_order(col_count)
    place = [order.index(c) for c in range(col_count)]
    forward = [(order[i], order[(i + 1) % col_count]) for i in range(col_count)]
    backward = [(b, a) for a, b in forward]
    ring = jnp.asarray(order, jnp.int32)
    at = jnp.asarray(place, jnp.int32)[own_col]
    part = own_col % ratio
    half = slot_count // 2
    steps = col_count // 2 - 1

    diag = precond_diag.reshape(row_blocks, ROWS, 2).swapaxes(1, 2).reshape(row_blocks, TILE, 1)
    term_place = jnp.stack([own_row, own_row ^ (own_col // ratio), own_col])

    all_orbitals = lax.all_gather(orbitals, "row", axis=0, tiled=True)
    pad = -slot_count % (8 * LANES)
    ids = jnp.pad(tile_ids, (0, pad)).reshape(-1, LANES).astype(F32)
    picked = pick_tiles(slots, density_tiles, ids, device_count)
    exchange = lambda a: lax.all_to_all(
        a, ("row", "col"), split_axis=0, concat_axis=0, tiled=True
    )
    arrived = exchange(picked)
    listed = lax.dynamic_slice(
        arrived, (own_row * col_count, arrived.shape[1] - ids.shape[0], 0), (col_count,) + ids.shape
    )
    listed = listed.reshape(col_count, -1)[:, :slot_count].astype(jnp.int32)
    listed_rows = listed // block_count - own_row * row_blocks
    listed_cols = listed % col_blocks

    def plan(offsets):
        cols = ring[(at + jnp.asarray(offsets, jnp.int32)) % col_count]
        rows = listed_rows[cols].reshape(-1)
        blocks = listed_cols[cols].reshape(-1)
        return rows, blocks, jnp.append(cols, part)

    near = plan((0, -1, 1))
    far = plan([o for step in range(2, steps + 1) for o in (-step, step)] + [col_count // 2])
    tables = (diag, local_rows, local_cols, term_place)
    arrived, tables = lax.optimization_barrier((arrived, tables))
    diag, local_rows, local_cols, term_place = tables
    built = batch_tiles(
        per_range, col_count, own_cols, arrived, basis_values[0], grid_weight, xc_kernel, grid_coord
    )
    returned = exchange(built)
    hams = add_tiles(slots, returned, slot_count, nd)

    orbs = split_orbitals(all_orbitals, col_count)

    own = (local_rows, local_cols)
    energy = orbital_energy[None]
    send_up = lambda a: lax.ppermute(a, "col", forward)
    send_down = lambda a: lax.ppermute(a, "col", backward)

    ups = [send_up(ham) for ham in hams]
    downs = [send_down(ham) for ham in hams]
    ups[0] = after(ups[0], orbs)
    totals = add_rows([hams, ups, downs], near, orbs, row_blocks, col_blocks)

    early = tuple(range(nd - 1))
    ways = []
    ends = []
    sums = []

    def finished(last_ways):
        sums.append(first_term(own, term_place, ends, diag, energy, orbs, col_blocks))
        sums.append(second_term(early, own, term_place, ways, orbs, sums[0], row_blocks))
        return sums[1]

    for d in range(nd):
        up, down = ups[d], downs[d]
        chunks = []
        for step in range(2, steps + 1):
            if step == 2 and d == nd - 1 or step == 3 and d == 0:
                up, down = after(up, totals[0]), after(down, totals[0])
            if step == 3 and d == nd - 1:
                up, down = after(up, ends[0]), after(down, ends[0])
            up, down = send_up(up), send_down(down)
            chunks += [up, down]
        if d:
            up, down = after(up, ends[d - 1]), after(down, ends[d - 1])
            chunks[-2:] = [up, down]
        chunks += [send_up(up[:half]), send_down(down[half:])]
        total = totals[d]
        if d == nd - 1:
            total = after(total, ways[0][row_count // 2])
        piece, end = response_piece(total, chunks, far, orbs, diag, energy, col_blocks)
        ends.append(end)
        held = None
        if d == nd - 1:
            held = lambda last: sums[1] if sums else finished(last)
        ways.append(row_broadcast(piece, row_count, col_count, ratio, held))
    return second_term((nd - 1,), own, term_place, ways[-1:], orbs, sums[0], row_blocks, sums[1])


def solution(mesh):
    placed = (
        P(None, ("row", "col"), None),
        P(("row", "col")),
        P(),
        P(("row", "col"), None, None),
        P(("row", "col"), None),
        P(("row", "col"), None),
        P(None, ("row", "col"), None),
        P("row", None),
        P("row"),
        P(),
    )
    return jax.shard_map(
        local, mesh=mesh, in_specs=placed, out_specs=P(None, ("row", "col"), None), check_vma=False
    )
```

time: 1090 us -> 438 us (0.40); the launches traced: 1080 us -> 437 us
  waiting for transfers between devices: 644 us -> 129 us
  local copies, waits for them, and re-layouts: 228 us -> 38.2 us
  matrix products: 153 us -> 0 us
  Pallas kernels: 0 us -> 136 us
  blocking collectives: 0 us -> 74.6 us
  starting transfers between devices: 11.2 us -> 41.4 us
  other arithmetic: 24.8 us -> 3.73 us
    reduce_scatter x1 -> x0, waiting for transfers between devices: 204 us -> none  [local(): lax.psum_scatter(partial_rows, 'col', scatter_dimension=2, tiled=True)]
    all_gather x1, waiting for transfers between devices: 176 us -> 0.01 us  [local(): all_orbitals = lax.all_gather(orbitals, 'row', axis=0, tiled=True)]
    dot_general x8 -> x0, matrix products: 153 us -> none  [the longest x1 45.9 us: local(): jnp.einsum('drc,co->dro', block_matrix, orbital_cols, precision=PRECISE)]
    pallas_call x0 -> x24, Pallas kernels: none -> 136 us  [the longest x3 60.4 us: response_piece(): pl.pallas_call(functools.partial(piece_kernel, count), out_shape=(piece,...]
    all_to_all x2 -> x1, waiting for transfers between devices: 182 us -> 73.8 us  [local(): lax.all_to_all(a, ('row', 'col'), split_axis=0, concat_axis=0, tiled=True)]
    psum x2 -> x0, waiting for transfers between devices: 82.2 us -> none  [from_root(): return lax.psum(kept, axis)]
    reshape x8 -> x6, local copies, waits for them, and re-layouts: 78.7 us -> 3.15 us  [the longest x2 1.33 us: plan(): blocks = listed_cols[cols].reshape(-1)]
    all_to_all x0 -> x1, blocking collectives: none -> 74.6 us  [local(): lax.all_to_all(a, ('row', 'col'), split_axis=0, concat_axis=0, tiled=True)]
  transfers between devices with their start and end apart: 6 -> 35, of which waited for: 5 -> 13; matrix products, arithmetic and copies ran while one was open for 17% -> 6% of each run, Pallas kernels for 0% -> 29%
where the time goes in v2:
time: 438 us; the launch traced here: 437 us
  Pallas kernels  136 us (31%)
  waiting for transfers between devices  129 us (29%)
  blocking collectives  74.6 us (17%)
  starting transfers between devices  41.4 us (9%)
  local copies, waits for them, and re-layouts  38.2 us (9%)
  between operations  13.8 us (3%)
    all_to_all x1, blocking collectives, local(): lax.all_to_all(a, ('row', 'col'), split_axis=0, concat_axis=0, tiled=True)  74.6 us
    all_to_all x1, waiting for transfers between devices, local(): lax.all_to_all(a, ('row', 'col'), split_axis=0, concat_axis=0, tiled=True)  73.8 us
    pallas_call x3, Pallas kernels, response_piece(): pl.pallas_call(functools.partial(piece_kernel, count), out_shape=(piece,...  60.4 us
    pallas_call x4, Pallas kernels, call(): pl.pallas_call(kernel, out_shape=out, grid_spec=pltpu.PrefetchScalarGridS...  48.2 us
    ppermute x12, waiting for transfers between devices, local(): send_down = lambda a: lax.ppermute(a, 'col', backward)  34.8 us
    unnamed x77, local copies, waits for them, and re-layouts  22.8 us
    ppermute x12, starting transfers between devices, local(): send_up = lambda a: lax.ppermute(a, 'col', forward)  14.9 us
    pallas_call x1, Pallas kernels, batch_tiles(): pl.pallas_call(functools.partial(batch_kernel, per_range, col_count), out...  14.1 us
  transfers between devices with their start and end apart: 35, of which 13 were waited for; matrix products, arithmetic and copies ran while one was open for 6% of the time, Pallas kernels for 29%

profile of v2, /device:TPU:0, one launch (start us, length us, event | category | flops | bytes accessed | tf_op | source)
XLA Modules:
  0.0 436.8 jit_solution(9764170119415019419)
XLA Ops:
  8.0 3.7 pick_tiles.1
  11.7 7.4 %all-to-all-start = ((f32[32,200,128]{2,1,0:T(8,128)}), f32[32,200,128]{2,1,0:T(8,128)}, u32[]{:S(2)}, u32[]{:S(2)}) async-start(f32[32,200,128]{2,1,0:T(8,128)} %pick_tiles.1), calls=%async_computation | async-start | bytes 6553600 | tf_op jit(solution)/shard_map/all_to_all | solution.py:560
  21.3 73.8 %all-to-all-done.tiles_ref = f32[32,200,128]{2,1,0:T(8,128)} async-done(((f32[32,200,128]{2,1,0:T(8,128)}), f32[32,200,128]{2,1,0:T(8,128)}, u32[]{:S(2)}, u32[]{:S(2)}) %all-to-all-start) | async-done | bytes 3276832 | tf_op jit(solution)/shard_map/all_to_all | solution.py:560
  95.1 14.1 %batch_tiles.1 = f32[32,192,128]{2,1,0:T(8,128)S(1)} custom-call(s32[8]{0:T(128)S(1)} %and_select_fusion.1.col_ref, f32[32,200,128]{2,1,0:T(8,128)} %all-to-all-done.tiles_ref, f32[512,1024]{1,0:T(8,128)S(1)} %bitcast.23, f32[1,1024]{1,0:T(1,128)S(1)} %copy-done.7, f32[1,1024]{1,0:T(1,128)S(1)} %copy-done.8, f32[3,1,1024]{2,1,0:T(1,128)S(1)} %copy-done.6), custom_call_target="tpu_custom_call" | custom-call | tf_op jit(solution)/shard_map/batch_tiles/pallas_call | solution.py:155
  109.2 74.6 %all_to_all.10.tiles_ref = f32[32,192,128]{2,1,0:T(8,128)S(1)} all-to-all(f32[32,192,128]{2,1,0:T(8,128)S(1)} %batch_tiles.1), channel_id=1, replica_groups=mesh['row'=4,'col'=8] {'row','col'}, dimensions={0} | all-to-all | bytes 6291456 | tf_op jit(solution)/shard_map/all_to_all | solution.py:560
  186.5 12.2 %collective-permute-done.3.refs_6_ = f32[32,32,128]{2,1,0:T(8,128)S(1)} collective-permute-done((f32[32,32,128]{2,1,0:T(8,128)S(1)}, f32[32,32,128]{2,1,0:T(8,128)S(1)}, u32[]{:S(2)}, u32[]{:S(2)}) %collective-permute-start.3) | collective-permute-done | bytes 524320 | tf_op jit(solution)/shard_map/ppermute | solution.py:593
  205.1 8.7 %collective-permute-done.9.refs_1_ = f32[32,32,128]{2,1,0:T(8,128)} collective-permute-done((f32[32,32,128]{2,1,0:T(8,128)S(1)}, f32[32,32,128]{2,1,0:T(8,128)}, u32[]{:S(2)}, u32[]{:S(2)}) %collective-permute-start.9) | collective-permute-done | bytes 524320 | tf_op jit(solution)/shard_map/ppermute | solution.py:593
  220.5 8.6 %split_orbitals.1.other_ref.refs_9_.refs_10_.refs_11_.refs_6_.refs_7_.refs_8_.refs_5_.refs_4_ = bf16[128,128,512]{2,1,0:T(8,128)(2,1)S(1)} custom-call(f32[8192,512]{1,0:T(8,128)} %all-gather.2.cloned.1.call-done.orb_ref), custom_call_target="tpu_custom_call" | custom-call | bytes 33554432 | tf_op jit(solution)/shard_map/split_orbitals/pallas_call | solution.py:219
  229.2 5.8 %copy-done = bf16[128,128,512]{2,1,0:T(8,128)(2,1)} copy-done((bf16[128,128,512]{2,1,0:T(8,128)(2,1)}, bf16[128,128,512]{2,1,0:T(8,128)(2,1)S(1)}, u32[]{:S(2)}) %copy-start) | copy-done | bytes 16777240
  239.8 16.5 %add_rows.1 = (f32[32,64,512]{2,1,0:T(8,128)}, f32[32,64,512]{2,1,0:T(8,128)}, f32[32,64,512]{2,1,0:T(8,128)}) custom-call(s32[96]{0:T(128)} %reshape.65.row_id, s32[96]{0:T(128)} %reshape.66.col_id, s32[4]{0:T(128)} %pad_add_fusion.2.place_ref, f32[32,32,128]{2,1,0:T(8,128)} %copy-done.3, f32[32,32,128]{2,1,0:T(8,128)} %copy-done.4, ...), custom_call_target="tpu_custom_call" | custom-call | flops 9600000000 | bytes 8388608 | tf_op jit(solution)/shard_map/add_rows/pallas_call | solution.py:270
  262.6 8.7 %collective-permute-done.11.refs_3_ = f32[32,32,128]{2,1,0:T(8,128)S(1)} collective-permute-done((f32[32,32,128]{2,1,0:T(8,128)}, f32[32,32,128]{2,1,0:T(8,128)S(1)}, u32[]{:S(2)}, u32[]{:S(2)}) %collective-permute-start.11) | collective-permute-done | bytes 524320 | tf_op jit(solution)/shard_map/ppermute | solution.py:593
  279.5 3.1 collective-permute-done.16.refs_1_
  290.1 20.1 %response_piece.3 = (f32[16,64,512]{2,1,0:T(8,128)}, f32[32,64,512]{2,1,0:T(8,128)}) custom-call(s32[160]{0:T(256)} %reshape.62.row_id, s32[160]{0:T(256)} %reshape.63.col_id, s32[6]{0:T(128)} %pad_add_fusion.1.place_ref, f32[32,32,128]{2,1,0:T(8,128)} %copy-done.18, f32[32,32,128]{2,1,0:T(8,128)} %collective-permute-done.9.refs_1_, ...), custom_call_target="tpu_custom_call" | custom-call | flops 20000000000 | bytes 8388608 | tf_op jit(solution)/shard_map/response_piece/pallas_call | solution.py:343
  317.4 2.8 collective-permute-start.24
  323.1 20.1 %response_piece.4 = (f32[16,64,512]{2,1,0:T(8,128)}, f32[32,64,512]{2,1,0:T(8,128)}) custom-call(s32[160]{0:T(256)} %reshape.62.row_id, s32[160]{0:T(256)} %reshape.63.col_id, s32[6]{0:T(128)} %pad_add_fusion.1.place_ref, f32[32,32,128]{2,1,0:T(8,128)} %collective-permute-done.15.refs_0_, f32[32,32,128]{2,1,0:T(8,128)} %copy-done.23, ...), custom_call_target="tpu_custom_call" | custom-call | flops 20000000000 | bytes 8388608 | tf_op jit(solution)/shard_map/response_piece/pallas_call | solution.py:343
  348.1 2.6 collective-permute-start.30
  353.8 20.2 %response_piece.5 = (f32[16,64,512]{2,1,0:T(8,128)}, f32[32,64,512]{2,1,0:T(8,128)}) custom-call(s32[160]{0:T(256)} %reshape.62.row_id, s32[160]{0:T(256)} %reshape.63.col_id, s32[6]{0:T(128)} %pad_add_fusion.1.place_ref, f32[32,32,128]{2,1,0:T(8,128)} %copy-done.19, f32[32,32,128]{2,1,0:T(8,128)} %copy-done.17, f32[32,32,128]{2,1,0:T(8,128)} %after.21.refs_2_, ...), custom_call_target="tpu_custom_call" | custom-call | flops 20000000000 | bytes 8388608 | tf_op jit(solution)/shard_map/response_piece/pallas_call | solution.py:343
  374.0 4.5 %collective-permute-start.26 = (f32[16,64,512]{2,1,0:T(8,128)}, f32[16,64,512]{2,1,0:T(8,128)}, u32[]{:S(2)}, u32[]{:S(2)}) collective-permute-start(f32[16,64,512]{2,1,0:T(8,128)} %get-tuple-element.36.refs_0_), channel_id=1, source_target_pairs={{0,16},{1,17},{10,26},{11,27},{20,4},{21,5},{30,14},{31,15}} | collective-permute-start | bytes 6291464 | tf_op jit(solution)/shard_map/ppermute | solution.py:499
  379.5 12.0 %first_term.1.refs_9_.refs_5_ = f32[3,32,32,128]{3,2,1,0:T(8,128)} custom-call(s32[32]{0:T(128)} %get-tuple-element.22.row_id, s32[32]{0:T(128)} %get-tuple-element.23.col_id, s32[3]{0:T(128)} %pad_add_fusion.place_ref, f32[32,64,512]{2,1,0:T(8,128)} %get-tuple-element.31.other_ref.refs_0_, f32[32,64,512]{2,1,0:T(8,128)} %get-tuple-element.33.other_ref.refs_1_, ...), custom_call_target="tpu_custom_call" | custom-call | flops 3200000000 | bytes 8388608 | tf_op jit(solution)/shard_map/first_term/pallas_call | solution.py:270
  391.5 9.5 %collective-permute-done.26.refs_2_ = f32[16,64,512]{2,1,0:T(8,128)} collective-permute-done((f32[16,64,512]{2,1,0:T(8,128)}, f32[16,64,512]{2,1,0:T(8,128)}, u32[]{:S(2)}, u32[]{:S(2)}) %collective-permute-start.26) | collective-permute-done | bytes 2097184 | tf_op jit(solution)/shard_map/ppermute | solution.py:499
  401.0 3.2 copy.56.value_ref
  404.2 10.4 %second_term.2.other_ref.refs_6_ = f32[2,1024,128]{2,1,0:T(8,128)} custom-call(s32[32]{0:T(128)} %get-tuple-element.22.row_id, s32[32]{0:T(128)} %get-tuple-element.23.col_id, s32[3]{0:T(128)} %pad_add_fusion.place_ref, f32[16,64,512]{2,1,0:T(8,128)} %get-tuple-element.35.refs_0_, f32[16,64,512]{2,1,0:T(8,128)} %collective-permute-done.27.refs_1_, ...), custom_call_target="tpu_custom_call" | custom-call | flops 3200000000 | bytes 8388608 | tf_op jit(solution)/shard_map/second_term/pallas_call | solution.py:270
  415.2 4.0 collective-permute-done.32.refs_3_
  420.5 9.4 %second_term.3 = f32[3,32,4096]{2,1,0:T(8,128)} custom-call(s32[32]{0:T(128)} %get-tuple-element.22.row_id, s32[32]{0:T(128)} %get-tuple-element.23.col_id, s32[3]{0:T(128)} %pad_add_fusion.place_ref, f32[16,64,512]{2,1,0:T(8,128)} %get-tuple-element.36.refs_0_, f32[16,64,512]{2,1,0:T(8,128)} %collective-permute-done.25.refs_1_, ...), custom_call_target="tpu_custom_call" | custom-call | flops 3200000000 | bytes 8388608 | tf_op jit(solution)/shard_map/second_term/pallas_call | solution.py:270
  (192 shorter events, 67.2 us)
Async XLA Ops:
  6.5 214.0 %all-gather.2.cloned.1.call-start = ((), (), s32[]{:S(2)}) async-start(), calls=%async_computation.2 | async-start | bytes 20971520 | tf_op jit(solution)/shard_map/all_gather | solution.py:556
  11.7 83.4 %all-to-all-start = ((f32[32,200,128]{2,1,0:T(8,128)}), f32[32,200,128]{2,1,0:T(8,128)}, u32[]{:S(2)}, u32[]{:S(2)}) async-start(f32[32,200,128]{2,1,0:T(8,128)} %pick_tiles.1), calls=%async_computation | async-start | bytes 6553600 | tf_op jit(solution)/shard_map/all_to_all | solution.py:560
  201.2 33.7 %collective-permute-start.1 = (f32[32,32,128]{2,1,0:T(8,128)S(1)}, f32[32,32,128]{2,1,0:T(8,128)S(1)}, u32[]{:S(2)}, u32[]{:S(2)}) collective-permute-start(f32[32,32,128]{2,1,0:T(8,128)S(1)} %get-tuple-element.27.refs_0_), channel_id=1, source_target_pairs={{0,2},{2,4},{4,6},{6,7},{7,5},{5,3},{3,1},{1,0},{8,10},{10,12},{12... | collective-permute-start | bytes 1572872 | tf_op jit(solution)/shard_map/ppermute | solution.py:592
  202.1 36.0 %collective-permute-start.2 = (f32[32,32,128]{2,1,0:T(8,128)S(1)}, f32[32,32,128]{2,1,0:T(8,128)}, u32[]{:S(2)}, u32[]{:S(2)}) collective-permute-start(f32[32,32,128]{2,1,0:T(8,128)S(1)} %get-tuple-element.28.refs_1_), channel_id=1, source_target_pairs={{0,2},{2,4},{4,6},{6,7},{7,5},{5,3},{3,1},{1,0},{8,10},{10,12},{12... | collective-permute-start | bytes 1572872 | tf_op jit(solution)/shard_map/ppermute | solution.py:592
  203.1 35.1 %collective-permute-start.4 = (f32[32,32,128]{2,1,0:T(8,128)S(1)}, f32[32,32,128]{2,1,0:T(8,128)}, u32[]{:S(2)}, u32[]{:S(2)}) collective-permute-start(f32[32,32,128]{2,1,0:T(8,128)S(1)} %get-tuple-element.28.refs_1_), channel_id=1, source_target_pairs={{2,0},{4,2},{6,4},{7,6},{5,7},{3,5},{1,3},{0,1},{10,8},{12,10},{14... | collective-permute-start | bytes 1572872 | tf_op jit(solution)/shard_map/ppermute | solution.py:593
  204.1 34.0 %collective-permute-start = (f32[32,32,128]{2,1,0:T(8,128)S(1)}, f32[32,32,128]{2,1,0:T(8,128)S(1)}, u32[]{:S(2)}, u32[]{:S(2)}) collective-permute-start(f32[32,32,128]{2,1,0:T(8,128)S(1)} %get-tuple-element.26.refs_2_), channel_id=1, source_target_pairs={{0,2},{2,4},{4,6},{6,7},{7,5},{5,3},{3,1},{1,0},{8,10},{10,12},{12... | collective-permute-start | bytes 1572872 | tf_op jit(solution)/shard_map/ppermute | solution.py:592
  213.7 24.4 %collective-permute-start.5 = (f32[32,32,128]{2,1,0:T(8,128)S(1)}, f32[32,32,128]{2,1,0:T(8,128)S(1)}, u32[]{:S(2)}, u32[]{:S(2)}) collective-permute-start(f32[32,32,128]{2,1,0:T(8,128)S(1)} %get-tuple-element.26.refs_2_), channel_id=1, source_target_pairs={{2,0},{4,2},{6,4},{7,6},{5,7},{3,5},{1,3},{0,1},{10,8},{12,10},{14... | collective-permute-start | bytes 1572872 | tf_op jit(solution)/shard_map/ppermute | solution.py:593
  235.7 20.7 %collective-permute-start.8 = (f32[32,32,128]{2,1,0:T(8,128)}, f32[32,32,128]{2,1,0:T(8,128)S(1)}, u32[]{:S(2)}, u32[]{:S(2)}) collective-permute-start(f32[32,32,128]{2,1,0:T(8,128)} %after.13.refs_3_), channel_id=1, source_target_pairs={{0,2},{2,4},{4,6},{6,7},{7,5},{5,3},{3,1},{1,0},{8,10},{10,12},{12... | collective-permute-start | bytes 1572872 | tf_op jit(solution)/shard_map/ppermute | solution.py:592
  259.9 22.7 %collective-permute-start.16 = (f32[32,32,128]{2,1,0:T(8,128)}, f32[32,32,128]{2,1,0:T(8,128)S(1)}, u32[]{:S(2)}, u32[]{:S(2)}) collective-permute-start(f32[32,32,128]{2,1,0:T(8,128)} %collective-permute-done.4.refs_7_), channel_id=1, source_target_pairs={{2,0},{4,2},{6,4},{7,6},{5,7},{3,5},{1,3},{0,1},{10,8},{12,10},{14... | collective-permute-start | bytes 1572872 | tf_op jit(solution)/shard_map/ppermute | solution.py:593
  260.2 23.7 %collective-permute-start.15 = (f32[32,32,128]{2,1,0:T(8,128)}, f32[32,32,128]{2,1,0:T(8,128)}, u32[]{:S(2)}, u32[]{:S(2)}) collective-permute-start(f32[32,32,128]{2,1,0:T(8,128)} %collective-permute-done.2.refs_4_), channel_id=1, source_target_pairs={{0,2},{2,4},{4,6},{6,7},{7,5},{5,3},{3,1},{1,0},{8,10},{10,12},{12... | collective-permute-start | bytes 1572872 | tf_op jit(solution)/shard_map/ppermute | solution.py:592
  271.3 16.8 %collective-permute-start.13 = (f32[16,32,128]{2,1,0:T(8,128)S(1)}, f32[16,32,128]{2,1,0:T(8,128)S(1)}, u32[]{:S(2)}, u32[]{:S(2)}) collective-permute-start(f32[16,32,128]{2,1,0:T(8,128)S(1)} %slice.42), channel_id=1, source_target_pairs={{2,0},{4,2},{6,4},{7,6},{5,7},{3,5},{1,3},{0,1},{10,8},{12,10},{14... | collective-permute-start | bytes 786440 | tf_op jit(solution)/shard_map/ppermute | solution.py:593
  282.5 27.7 %collective-permute-start.18 = (f32[32,32,128]{2,1,0:T(8,128)S(1)}, f32[32,32,128]{2,1,0:T(8,128)}, u32[]{:S(2)}, u32[]{:S(2)}) collective-permute-start(f32[32,32,128]{2,1,0:T(8,128)S(1)} %collective-permute-done.16.refs_1_), channel_id=1, source_target_pairs={{2,0},{4,2},{6,4},{7,6},{5,7},{3,5},{1,3},{0,1},{10,8},{12,10},{14... | collective-permute-start | bytes 1572872 | tf_op jit(solution)/shard_map/ppermute | solution.py:593
  283.9 28.9 %collective-permute-start.17 = (f32[32,32,128]{2,1,0:T(8,128)}, f32[32,32,128]{2,1,0:T(8,128)}, u32[]{:S(2)}, u32[]{:S(2)}) collective-permute-start(f32[32,32,128]{2,1,0:T(8,128)} %collective-permute-done.15.refs_0_), channel_id=1, source_target_pairs={{0,2},{2,4},{4,6},{6,7},{7,5},{5,3},{3,1},{1,0},{8,10},{10,12},{12... | collective-permute-start | bytes 1572872 | tf_op jit(solution)/shard_map/ppermute | solution.py:592
  285.7 29.9 %collective-permute-start.7 = (f32[32,32,128]{2,1,0:T(8,128)}, f32[32,32,128]{2,1,0:T(8,128)S(1)}, u32[]{:S(2)}, u32[]{:S(2)}) collective-permute-start(f32[32,32,128]{2,1,0:T(8,128)} %after.15), channel_id=1, source_target_pairs={{2,0},{4,2},{6,4},{7,6},{5,7},{3,5},{1,3},{0,1},{10,8},{12,10},{14... | collective-permute-start | bytes 1572872 | tf_op jit(solution)/shard_map/ppermute | solution.py:593
  288.2 28.3 %collective-permute-start.6 = (f32[32,32,128]{2,1,0:T(8,128)}, f32[32,32,128]{2,1,0:T(8,128)S(1)}, u32[]{:S(2)}, u32[]{:S(2)}) collective-permute-start(f32[32,32,128]{2,1,0:T(8,128)} %after.14), channel_id=1, source_target_pairs={{0,2},{2,4},{4,6},{6,7},{7,5},{5,3},{3,1},{1,0},{8,10},{10,12},{12... | collective-permute-start | bytes 1572872 | tf_op jit(solution)/shard_map/ppermute | solution.py:592
  317.4 33.3 %collective-permute-start.24 = (f32[16,64,512]{2,1,0:T(8,128)}, f32[16,64,512]{2,1,0:T(8,128)S(1)}, u32[]{:S(2)}, u32[]{:S(2)}) collective-permute-start(f32[16,64,512]{2,1,0:T(8,128)} %get-tuple-element.35.refs_0_), channel_id=1, source_target_pairs={{0,16},{1,17},{10,26},{11,27},{20,4},{21,5},{30,14},{31,15}} | collective-permute-start | bytes 6291464 | tf_op jit(solution)/shard_map/ppermute | solution.py:499
  320.3 22.9 %collective-permute-start.21 = (f32[32,32,128]{2,1,0:T(8,128)}, f32[32,32,128]{2,1,0:T(8,128)S(1)}, u32[]{:S(2)}, u32[]{:S(2)}) collective-permute-start(f32[32,32,128]{2,1,0:T(8,128)} %after.22), channel_id=1, source_target_pairs={{2,0},{4,2},{6,4},{7,6},{5,7},{3,5},{1,3},{0,1},{10,8},{12,10},{14... | collective-permute-start | bytes 1572872 | tf_op jit(solution)/shard_map/ppermute | solution.py:593
  320.9 24.9 %collective-permute-start.14 = (f32[32,32,128]{2,1,0:T(8,128)}, f32[32,32,128]{2,1,0:T(8,128)}, u32[]{:S(2)}, u32[]{:S(2)}) collective-permute-start(f32[32,32,128]{2,1,0:T(8,128)} %after.18), channel_id=1, source_target_pairs={{0,2},{2,4},{4,6},{6,7},{7,5},{5,3},{3,1},{1,0},{8,10},{10,12},{12... | collective-permute-start | bytes 1572872 | tf_op jit(solution)/shard_map/ppermute | solution.py:592
  348.1 30.9 %collective-permute-start.30 = (f32[16,64,512]{2,1,0:T(8,128)}, f32[16,64,512]{2,1,0:T(8,128)}, u32[]{:S(2)}, u32[]{:S(2)}) collective-permute-start(f32[16,64,512]{2,1,0:T(8,128)} %get-tuple-element.37.refs_4_), channel_id=1, source_target_pairs={{0,16},{1,17},{10,26},{11,27},{20,4},{21,5},{30,14},{31,15}} | collective-permute-start | bytes 6291464 | tf_op jit(solution)/shard_map/ppermute | solution.py:499
  374.0 27.0 %collective-permute-start.26 = (f32[16,64,512]{2,1,0:T(8,128)}, f32[16,64,512]{2,1,0:T(8,128)}, u32[]{:S(2)}, u32[]{:S(2)}) collective-permute-start(f32[16,64,512]{2,1,0:T(8,128)} %get-tuple-element.36.refs_0_), channel_id=1, source_target_pairs={{0,16},{1,17},{10,26},{11,27},{20,4},{21,5},{30,14},{31,15}} | collective-permute-start | bytes 6291464 | tf_op jit(solution)/shard_map/ppermute | solution.py:499
  378.5 25.7 %collective-permute-start.27 = (f32[16,64,512]{2,1,0:T(8,128)}, f32[16,64,512]{2,1,0:T(8,128)}, u32[]{:S(2)}, u32[]{:S(2)}) collective-permute-start(f32[16,64,512]{2,1,0:T(8,128)} %get-tuple-element.35.refs_0_), channel_id=1, source_target_pairs={{0,8},{8,0},{16,24},{24,16},{1,9},{9,1},{17,25},{25,17},{2,10},{10... | collective-permute-start | bytes 6291464 | tf_op jit(solution)/shard_map/ppermute | solution.py:499
  378.5 25.7 %collective-permute-start.29 = (f32[16,64,512]{2,1,0:T(8,128)}, f32[16,64,512]{2,1,0:T(8,128)}, u32[]{:S(2)}, u32[]{:S(2)}) collective-permute-start(f32[16,64,512]{2,1,0:T(8,128)} %get-tuple-element.37.refs_4_), channel_id=1, source_target_pairs={{0,8},{8,0},{16,24},{24,16},{1,9},{9,1},{17,25},{25,17},{2,10},{10... | collective-permute-start | bytes 6291464 | tf_op jit(solution)/shard_map/ppermute | solution.py:499
  379.0 25.2 %collective-permute-start.28 = (f32[16,64,512]{2,1,0:T(8,128)S(1)}, f32[16,64,512]{2,1,0:T(8,128)}, u32[]{:S(2)}, u32[]{:S(2)}) collective-permute-start(f32[16,64,512]{2,1,0:T(8,128)S(1)} %copy-done.11), channel_id=1, source_target_pairs={{0,8},{8,0},{16,24},{24,16},{1,9},{9,1},{17,25},{25,17},{2,10},{10... | collective-permute-start | bytes 6291464 | tf_op jit(solution)/shard_map/ppermute | solution.py:499
  379.0 25.2 %collective-permute-start.31 = (f32[16,64,512]{2,1,0:T(8,128)}, f32[16,64,512]{2,1,0:T(8,128)}, u32[]{:S(2)}, u32[]{:S(2)}) collective-permute-start(f32[16,64,512]{2,1,0:T(8,128)} %collective-permute-done.30.refs_6_), channel_id=1, source_target_pairs={{0,8},{8,0},{16,24},{24,16},{1,9},{9,1},{17,25},{25,17},{2,10},{10... | collective-permute-start | bytes 6291464 | tf_op jit(solution)/shard_map/ppermute | solution.py:499
  (46 other events, 725.5 us)
Sparse Core Ops, SparseCore 0:
  8.9 172.3 all-gather.1

commit v3 on v2

--- a/solution.py
+++ b/solution.py
@@ -171,12 +171,10 @@
     )(cols, tiles, basis, weight, xc, coord)
 
 
-def add_kernel(slot_ref, tiles_ref, *out_refs):
-    for out_ref in out_refs:
-        out_ref[...] = jnp.zeros(out_ref.shape, F32)
-
-    nd = len(out_refs)
+def add_kernel(slot_ref, tiles_ref, out_ref):
+    nd = out_ref.shape[0]
     per_range = slot_ref.shape[0] // tiles_ref.shape[0]
+    out_ref[...] = jnp.zeros(out_ref.shape, F32)
 
     def step(n, carry):
         for k in range(per_range):
@@ -184,9 +182,9 @@
 
             @pl.when(slot >= 0)
             def _(slot=slot, k=k):
-                for d, out_ref in enumerate(out_refs):
+                for d in range(nd):
                     start = (k * nd + d) * ROWS
-                    out_ref[slot] += tiles_ref[n, start : start + ROWS]
+                    out_ref[d, slot] += tiles_ref[n, start : start + ROWS]
 
         return carry
 
@@ -196,15 +194,17 @@
 def add_tiles(slots, tiles, slot_count, nd):
     return pl.pallas_call(
         add_kernel,
-        out_shape=[jax.ShapeDtypeStruct((slot_count, ROWS, LANES), F32)] * nd,
+        out_shape=jax.ShapeDtypeStruct((nd, slot_count, ROWS, LANES), F32),
         in_specs=[SMEM, VMEM],
-        out_specs=[VMEM] * nd,
+        out_specs=VMEM,
         compiler_params=params(32),
         name="add_tiles",
     )(slots, tiles)
 
 
-def split_kernel(orb_ref, out_ref):
+def split_kernel(orb_ref, out_ref, mark_ref):
+    mark_ref[...] = jnp.zeros(mark_ref.shape, F32)
+
     def blocks(index):
         for b in index:
             high, rest = split(orb_ref[pl.ds(pl.multiple_of(b * TILE, TILE), TILE), :])
@@ -218,11 +218,17 @@
     count, nocc = orbitals.shape
     return pl.pallas_call(
         split_kernel,
-        out_shape=jax.ShapeDtypeStruct((count // TILE, 2 * TILE, nocc), BF16),
+        out_shape=(
+            jax.ShapeDtypeStruct((count // TILE, 2 * TILE, nocc), BF16),
+            jax.ShapeDtypeStruct((8, LANES), F32),
+        ),
         grid=(parts,),
         in_specs=[pl.BlockSpec((count // parts, nocc), lambda g: (g, 0))],
-        out_specs=pl.BlockSpec((count // parts // TILE, 2 * TILE, nocc), lambda g: (g, 0, 0)),
-        compiler_params=params(32),
+        out_specs=(
+            pl.BlockSpec((count // parts // TILE, 2 * TILE, nocc), lambda g: (g, 0, 0)),
+            pl.BlockSpec((8, LANES), lambda g: (0, 0)),
+        ),
+        compiler_params=params(60),
         cost_estimate=pl.CostEstimate(
             flops=0, bytes_accessed=8 * count * nocc, transcendentals=0
         ),
@@ -230,31 +236,32 @@
     )(orbitals)
 
 
-def accumulate(chunks, orbs, row_id, col_id, sums):
+def accumulate(chunk, orb, row_id, col_id, offset, sums):
     low = low_lanes((ROWS, LANES))
     nd = len(sums)
-    offset = 0
-    for chunk, orb in zip(chunks, orbs):
-
-        def tiles(index, chunk=chunk, orb=orb, offset=offset):
-            products = []
-            for s in index:
-                left = []
-                for d in range(nd):
-                    tile = chunk[d][s]
-                    turned = pltpu.roll(tile, TILE, 1)
-                    for value in (jnp.where(low, tile, turned), jnp.where(low, turned, tile)):
-                        left.append(jnp.concatenate(split(value), axis=1))
-                left = jnp.concatenate(left, axis=0)
-                pair = orb[col_id[offset + s]]
+
+    def tiles(index):
+        products = []
+        for s in index:
+            left = []
+            for d in range(nd):
+                tile = chunk[d, s]
+                turned = pltpu.roll(tile, TILE, 1)
+                left += [split(jnp.where(low, tile, turned)), split(jnp.where(low, turned, tile))]
+            pair = orb[col_id[offset + s]]
+            if nd > 1:
+                left = jnp.concatenate([jnp.concatenate(parts, axis=1) for parts in left], axis=0)
                 products.append(dot(left, jnp.concatenate([pair, pair], axis=0)))
-            for s, product in zip(index, products):
-                block = row_id[offset + s]
-                for d in range(nd):
-                    sums[d][block] += product[d * TILE : (d + 1) * TILE]
-
-        in_groups(chunk[0].shape[0], tiles)
-        offset += chunk[0].shape[0]
+            else:
+                left = jnp.concatenate([parts[k] for k in range(2) for parts in left], axis=0)
+                product = dot(left, pair)
+                products.append(product[:TILE] + product[TILE:])
+        for s, product in zip(index, products):
+            block = row_id[offset + s]
+            for d in range(nd):
+                sums[d][block] += product[d * TILE : (d + 1) * TILE]
+
+    in_groups(chunk.shape[1], tiles, 16 if nd > 1 else 32)
 
 
 def whole(a):
@@ -285,73 +292,114 @@
     )(*tables, *args)
 
 
-def rows_kernel(count, nd, row_id, col_id, place_ref, *refs):
-    chunks = [refs[nd * k : nd * (k + 1)] for k in range(count)]
-    orbs, sums = refs[nd * count : (nd + 1) * count], refs[(nd + 1) * count :]
-    for total in sums:
-        total[...] = jnp.zeros(total.shape, F32)
-    accumulate(chunks, orbs, row_id, col_id, sums)
-
-
-def add_rows(chunks, where, orbs, row_blocks, col_blocks):
+def rows_kernel(count, nd, fresh, row_id, col_id, place_ref, *refs):
+    chunks, orbs, refs = refs[:count], refs[count : 2 * count], refs[2 * count :]
+    if fresh:
+        sums = refs
+        for total in sums:
+            total[...] = jnp.zeros(total.shape, F32)
+    else:
+        before, sums, sem = refs[:nd], refs[nd : 2 * nd], refs[2 * nd]
+        loads = [pltpu.make_async_copy(before[d], sums[d], sem.at[d]) for d in range(nd)]
+        for load in loads:
+            load.start()
+        for load in loads:
+            load.wait()
+    offset = 0
+    for chunk, orb in zip(chunks, orbs):
+        accumulate(chunk, orb, row_id, col_id, offset, sums)
+        offset += chunk.shape[1]
+
+
+def add_rows(totals, chunks, where, orbs, row_blocks, col_blocks):
     count = len(chunks)
-    nd = len(chunks[0])
-    flat = [c for chunk in chunks for c in chunk]
-    specs = [whole(c) for c in flat]
+    nd, slots = chunks[0].shape[:2]
+    args = list(chunks)
+    specs = [whole(c) for c in args]
     specs += [orb_spec(col_blocks, orbs, lambda r, c, p, k=k: p[k]) for k in range(count)]
+    args += [orbs] * count
+    scratch = []
+    if totals is not None:
+        specs += [pl.BlockSpec(memory_space=pl.ANY)] * nd
+        args += totals
+        scratch.append(pltpu.SemaphoreType.DMA((nd,)))
     out = jax.ShapeDtypeStruct((row_blocks, TILE, orbs.shape[2]), F32)
     return call(
-        functools.partial(rows_kernel, count, nd), "add_rows", where, flat + [orbs] * count, specs,
-        [out] * nd, [], count * flat[0].shape[0],
-    )
-
-
-def piece_kernel(count, row_id, col_id, place_ref, *refs):
-    chunks, orbs, refs = refs[:count], refs[count : 2 * count - 1], refs[2 * count - 1 :]
-    in_ref, diag_ref, energy_ref, piece_ref, total_ref, sums, square, sem = refs
+        functools.partial(rows_kernel, count, nd, totals is None), "add_rows", where, args, specs,
+        [out] * nd, scratch, count * slots,
+    )
+
+
+def piece_kernel(count, halves, row_id, col_id, place_ref, *refs):
+    chunks, refs = refs[:count], refs[count:]
+    orbs_ref, in_ref, diag_ref, energy_ref, piece_ref, total_ref, sums, square, chunk_buf, orb_buf = refs[:10]
+    sem, chunk_sem, orb_sem = refs[10:]
+    ranges = count - halves
+    col_blocks = orb_buf.shape[1]
     load = pltpu.make_async_copy(in_ref, sums, sem)
     load.start()
+    moves = []
+    for k in range(count):
+        size = chunks[k].shape[1]
+        start = chunks[0].shape[1] if halves and k == count - 1 else 0
+        start = start // 2
+        target = chunk_buf.at[min(k, ranges - 1), pl.ds(start, size)]
+        moves.append(pltpu.make_async_copy(chunks[k].at[0], target, chunk_sem.at[k]))
+        moves[-1].start()
+        if k < ranges:
+            source = orbs_ref.at[pl.ds(place_ref[k] * col_blocks, col_blocks)]
+            moves.append(pltpu.make_async_copy(source, orb_buf.at[k], orb_sem.at[k]))
+            moves[-1].start()
     load.wait()
-    accumulate([[c] for c in chunks], orbs + orbs[-1:], row_id, col_id, [sums])
+    offset = 0
+    for k in range(ranges):
+        for move in moves[2 * k : 2 * k + 2 + (halves if k == ranges - 1 else 0)]:
+            move.wait()
+        accumulate(chunk_buf.at[pl.ds(k, 1)], orb_buf.at[k], row_id, col_id, offset, [sums])
+        offset += chunk_buf.shape[1]
     store = pltpu.make_async_copy(sums, total_ref, sem)
     store.start()
-    first = place_ref[count - 1] * piece_ref.shape[0]
+    first = place_ref[ranges] * piece_ref.shape[0]
+    energy = energy_ref[...]
 
     def blocks(index):
         for b in index:
-            value = sums[first + b] * (-1.0 / (diag_ref[first + b] - energy_ref[...]))
+            value = sums[first + b] * (-1.0 / (diag_ref[first + b] - energy))
             for k in range(square.shape[1]):
                 lanes = slice(k * LANES, (k + 1) * LANES)
                 for parity in range(2):
-                    square[b % 2, k, pl.ds(parity, ROWS, stride=2), :] = value[
+                    square[b % 4, k, pl.ds(parity, ROWS, stride=2), :] = value[
                         parity * ROWS : (parity + 1) * ROWS, lanes
                     ]
-                piece_ref[b, :, lanes] = square[b % 2, k]
-
-    in_groups(piece_ref.shape[0], blocks, 2)
+                piece_ref[b, :, lanes] = square[b % 4, k]
+
+    in_groups(piece_ref.shape[0], blocks, 4)
     store.wait()
 
 
 def response_piece(total, chunks, where, orbs, diag, energy, col_blocks):
     count = len(chunks)
+    halves = int(chunks[-1].shape != chunks[0].shape)
+    ranges = count - halves
     nocc = orbs.shape[2]
     hbm = pl.BlockSpec(memory_space=pl.ANY)
-    specs = [whole(c) for c in chunks]
-    specs += [orb_spec(col_blocks, orbs, lambda r, c, p, k=k: p[k]) for k in range(count - 1)]
-    specs += [hbm, whole(diag), whole(energy)]
     piece = jax.ShapeDtypeStruct((col_blocks, TILE, nocc), F32)
     return pl.pallas_call(
-        functools.partial(piece_kernel, count),
+        functools.partial(piece_kernel, count, halves),
         out_shape=(piece, jax.ShapeDtypeStruct(total.shape, F32)),
         grid_spec=pltpu.PrefetchScalarGridSpec(
             num_scalar_prefetch=3,
             grid=(1,),
-            in_specs=specs,
+            in_specs=[hbm] * (count + 2) + [whole(diag), whole(energy)],
             out_specs=(whole(piece), hbm),
             scratch_shapes=[
                 pltpu.VMEM(total.shape, F32),
-                pltpu.VMEM((2, nocc // LANES, TILE, LANES), F32),
+                pltpu.VMEM((4, nocc // LANES, TILE, LANES), F32),
+                pltpu.VMEM((ranges,) + chunks[0].shape[1:], F32),
+                pltpu.VMEM((ranges, col_blocks) + orbs.shape[1:], BF16),
                 pltpu.SemaphoreType.DMA,
+                pltpu.SemaphoreType.DMA((count,)),
+                pltpu.SemaphoreType.DMA((ranges,)),
             ],
         ),
         compiler_params=params(60),
@@ -359,11 +407,10 @@
             flops=20_000_000_000, bytes_accessed=2**23, transcendentals=0
         ),
         name="response_piece",
-    )(*where, *chunks, *[orbs] * (count - 1), total, diag, energy)
-
-
-def first_kernel(nd, row_id, col_id, place_ref, *refs):
-    totals, (diag_ref, energy_ref, orb_ref, out_ref) = refs[:nd], refs[nd:]
+    )(*where, *chunks, orbs, total, diag, energy)
+
+
+def first_tiles(totals, diag_ref, energy_ref, orb_ref, row_id, col_id, out_ref):
     low = low_lanes((ROWS, LANES))
 
     def tiles(index):
@@ -372,45 +419,19 @@
             inverse = -1.0 / (diag_ref[block] - energy_ref[...])
             left = [part for total in totals for part in split(total[block] * inverse)]
             value = dot_nt(jnp.concatenate(left, axis=0), orb_ref[col_id[s]])
-            for d in range(nd):
+            for d in range(len(totals)):
                 start = 2 * d * TILE
                 tile = value[start : start + TILE] + value[start + TILE : start + 2 * TILE]
                 tile = tile + pltpu.roll(tile, TILE, 1)
-                out_ref[d, s] = jnp.where(low, tile[:ROWS], tile[ROWS:])
-
-    in_groups(out_ref.shape[1], tiles, 8)
-
-
-def first_term(own, places, totals, diag, energy, orbs, col_blocks):
-    nd, slots = len(totals), own[0].shape[0]
-    specs = [whole(a) for a in [*totals, diag, energy]]
-    specs.append(orb_spec(col_blocks, orbs, lambda r, c, p: p[2]))
-    return call(
-        functools.partial(first_kernel, nd), "first_term", [*own, places],
-        [*totals, diag, energy, orbs], specs,
-        jax.ShapeDtypeStruct((nd, slots, ROWS, LANES), F32), [], slots,
-    )
-
-
-def second_kernel(directions, way_count, last, row_id, col_id, place_ref, *refs):
-    count = len(directions)
-    ways = [refs[d * way_count : (d + 1) * way_count] for d in range(count)]
-    refs = refs[count * way_count :]
-    orb_ref, first_ref, refs = refs[0], refs[1], refs[2:]
-    if last:
-        done_ref, refs = refs[0], refs[1:]
-    out_ref, x_ref, square, sem = refs[:4]
-    for d in range(count):
-        for k, way in enumerate(ways[d]):
-
-            @pl.when(place_ref[1] == k)
-            def _(way=way, d=d):
-                pltpu.make_async_copy(way, x_ref.at[d], sem.at[d]).start()
-
-    for d in range(count):
-        pltpu.make_async_copy(ways[d][0], x_ref.at[d], sem.at[d]).wait()
+                rows = pl.ds(pl.multiple_of(s * ROWS, ROWS), ROWS)
+                out_ref[d, rows, :] = jnp.where(low, tile[:ROWS], tile[ROWS:])
+
+    in_groups(out_ref.shape[1] // ROWS, tiles, 8)
+
+
+def second_tiles(x_ref, orb_ref, row_id, col_id, square, read, write):
     low = low_lanes((ROWS, LANES))
-    slots = first_ref.shape[1]
+    count = x_ref.shape[0]
 
     def tiles(index):
         for u, s in enumerate(index):
@@ -421,63 +442,120 @@
                 tile = value[:, d * LANES : (d + 1) * LANES]
                 square[d, u] = tile + pltpu.roll(tile, TILE, 1)
         for u, s in enumerate(index):
+            rows = pl.ds(pl.multiple_of(s * ROWS, ROWS), ROWS)
             for d in range(count):
                 even = square[d, u, pl.ds(0, ROWS, stride=2), :]
                 odd = square[d, u, pl.ds(1, ROWS, stride=2), :]
-                value = first_ref[directions[d], s] + jnp.where(low, even, odd)
-                if last:
-                    refs[4][d, pl.ds(pl.multiple_of(s * ROWS, ROWS), ROWS), :] = value
-                else:
-                    out_ref[d, pl.ds(pl.multiple_of(s * ROWS, ROWS), ROWS), :] = value
-
-    in_groups(slots, tiles, square.shape[1])
-    if last:
-        for d in range(out_ref.shape[0]):
-            for start in range(0, slots, 8):
-                for k in range(ROWS):
-                    rows = pl.ds(start * ROWS + k, 8, stride=ROWS)
-                    if d in directions:
-                        value = refs[4][directions.index(d), rows, :]
-                    else:
-                        value = done_ref[d, rows, :]
-                    out_ref[d, start : start + 8, k * LANES : (k + 1) * LANES] = value
-
-
-def second_term(directions, own, places, ways, orbs, first, row_blocks, done=None):
-    nd, slots = first.shape[:2]
-    count = len(directions)
-    last = done is not None
+                write(d, rows, read(d, rows) + jnp.where(low, even, odd))
+
+    in_groups(row_id.shape[0], tiles, square.shape[1])
+
+
+def fetch(place_ref, ways, x_ref, sem):
+    for k, way in enumerate(ways):
+
+        @pl.when(place_ref[1] == k)
+        def _(way=way):
+            pltpu.make_async_copy(way, x_ref, sem).start()
+
+    return pltpu.make_async_copy(ways[0], x_ref, sem).wait
+
+
+def early_kernel(nd, way_count, row_id, col_id, place_ref, *refs):
+    ways = [refs[d * way_count : (d + 1) * way_count] for d in range(nd - 1)]
+    refs = refs[(nd - 1) * way_count :]
+    totals, refs = refs[:nd], refs[nd:]
+    diag_ref, energy_ref, orb_cols, orb_rows, out_ref, x_ref, square, sem = refs
+    waits = [fetch(place_ref, ways[d], x_ref.at[d], sem.at[d]) for d in range(nd - 1)]
+    first_tiles(totals, diag_ref, energy_ref, orb_cols, row_id, col_id, out_ref)
+    for wait in waits:
+        wait()
+
+    def write(d, rows, value):
+        out_ref[d, rows, :] = value
+
+    second_tiles(
+        x_ref, orb_rows, row_id, col_id, square, lambda d, rows: out_ref[d, rows, :], write
+    )
+
+
+def early_terms(own, places, ways, totals, diag, energy, orbs, row_blocks, col_blocks):
+    nd, slots = len(totals), own[0].shape[0]
     shape = ways[0][0].shape
-    rows = (count, slots * ROWS, LANES)
-    scratch = [
-        pltpu.VMEM((count,) + shape, F32),
-        pltpu.VMEM((count, 8, TILE, LANES), F32),
-        pltpu.SemaphoreType.DMA((count,)),
-    ]
-    if last:
-        scratch.append(pltpu.VMEM(rows, F32))
     flat = [way for each in ways for way in each]
-    others = [first, done] if last else [first]
     specs = [pl.BlockSpec(memory_space=pl.ANY)] * len(flat)
+    specs += [whole(a) for a in [*totals, diag, energy]]
+    specs.append(orb_spec(col_blocks, orbs, lambda r, c, p: p[2]))
     specs.append(orb_spec(row_blocks, orbs, lambda r, c, p: p[0]))
-    specs += [whole(a) for a in others]
-    out = jax.ShapeDtypeStruct((nd, slots, ROWS * LANES) if last else rows, F32)
     return call(
-        functools.partial(second_kernel, directions, len(ways[0]), last), "second_term",
-        [*own, places], [*flat, orbs, *others], specs, out, scratch, slots,
-    )
-
-
-def after(value, other):
+        functools.partial(early_kernel, nd, len(ways[0])), "early_terms", [*own, places],
+        [*flat, *totals, diag, energy, orbs, orbs], specs,
+        jax.ShapeDtypeStruct((nd, slots * ROWS, LANES), F32),
+        [
+            pltpu.VMEM((nd - 1,) + shape, F32),
+            pltpu.VMEM((nd - 1, 8, TILE, LANES), F32),
+            pltpu.SemaphoreType.DMA((nd - 1,)),
+        ],
+        1,
+    )
+
+
+def last_kernel(way_count, row_id, col_id, place_ref, *refs):
+    ways, refs = refs[:way_count], refs[way_count:]
+    orb_rows, done_ref, out_ref, x_ref, square, rows_ref, sem = refs
+    wait = fetch(place_ref, ways, x_ref.at[0], sem)
+    nd, slots, area = out_ref.shape
+
+    def layout(d, source):
+        for start in range(0, slots, 8):
+            for k in range(area // LANES):
+                out_ref[d, start : start + 8, k * LANES : (k + 1) * LANES] = source[
+                    pl.ds(start * ROWS + k, 8, stride=ROWS), :
+                ]
+
+    for d in range(nd - 1):
+        layout(d, done_ref.at[d])
+    wait()
+
+    def write(d, rows, value):
+        rows_ref[rows, :] = value
+
+    second_tiles(
+        x_ref, orb_rows, row_id, col_id, square, lambda d, rows: done_ref[nd - 1, rows, :], write
+    )
+    layout(nd - 1, rows_ref)
+
+
+def last_terms(own, places, ways, done, orbs, row_blocks):
+    slots = own[0].shape[0]
+    nd = done.shape[0]
+    specs = [pl.BlockSpec(memory_space=pl.ANY)] * len(ways)
+    specs += [orb_spec(row_blocks, orbs, lambda r, c, p: p[0]), whole(done)]
+    return call(
+        functools.partial(last_kernel, len(ways)), "last_terms", [*own, places],
+        [*ways, orbs, done], specs,
+        jax.ShapeDtypeStruct((nd, slots, ROWS * LANES), F32),
+        [
+            pltpu.VMEM((1,) + ways[0].shape, F32),
+            pltpu.VMEM((1, 8, TILE, LANES), F32),
+            pltpu.VMEM((slots * ROWS, LANES), F32),
+            pltpu.SemaphoreType.DMA,
+        ],
+        slots,
+    )
+
+
+def tie(values, others=()):
     hbm = pl.BlockSpec(memory_space=pl.ANY)
+    count = len(values)
     return pl.pallas_call(
-        lambda value_ref, other_ref, out_ref: None,
-        out_shape=jax.ShapeDtypeStruct(value.shape, value.dtype),
-        in_specs=[hbm, hbm],
-        out_specs=hbm,
-        input_output_aliases={0: 0},
-        name="after",
-    )(value, other)
+        lambda *refs: None,
+        out_shape=[jax.ShapeDtypeStruct(v.shape, v.dtype) for v in values],
+        in_specs=[hbm] * (count + len(others)),
+        out_specs=[hbm] * count,
+        input_output_aliases={k: k for k in range(count)},
+        name="tie",
+    )(*values, *others)
 
 
 def ring_order(count):
@@ -485,18 +563,24 @@
 
 
 def row_broadcast(value, row_count, col_count, ratio, held=None):
-    ways = [value]
-    for k in range(1, row_count):
+    def send(k):
         parent = k & (k - 1)
-        sent = ways[parent]
         if k & 1:
             rows = [[(r, r ^ 1) for r in range(row_count)]] * col_count
         else:
             rows = [[(c // ratio ^ parent, c // ratio ^ k)] for c in range(col_count)]
-        if held is not None and parent:
-            sent = after(sent, held(ways))
         pairs = [(a * col_count + c, b * col_count + c) for c in range(col_count) for a, b in rows[c]]
-        ways.append(lax.ppermute(sent, ("row", "col"), pairs))
+        return lax.ppermute(ways[parent], ("row", "col"), pairs)
+
+    ways = [value] + [None] * (row_count - 1)
+    for k in range(2, row_count, 2):
+        ways[k] = send(k)
+    if held is not None:
+        mark = held()
+        for k in range(2, row_count, 2):
+            ways[k] = tie([ways[k]], [mark])[0]
+    for k in range(1, row_count, 2):
+        ways[k] = send(k)
     return ways
 
 
@@ -574,8 +658,9 @@
         blocks = listed_cols[cols].reshape(-1)
         return rows, blocks, jnp.append(cols, part)
 
-    near = plan((0, -1, 1))
-    far = plan([o for step in range(2, steps + 1) for o in (-step, step)] + [col_count // 2])
+    plans = [plan((0, -1, 1))]
+    plans += [plan((-step, step)) for step in range(2, steps)]
+    plans[-1:] = [plan((-steps + 1, steps - 1, -steps, steps, col_count // 2))]
     tables = (diag, local_rows, local_cols, term_place)
     arrived, tables = lax.optimization_barrier((arrived, tables))
     diag, local_rows, local_cols, term_place = tables
@@ -583,54 +668,73 @@
         per_range, col_count, own_cols, arrived, basis_values[0], grid_weight, xc_kernel, grid_coord
     )
     returned = exchange(built)
-    hams = add_tiles(slots, returned, slot_count, nd)
-
-    orbs = split_orbitals(all_orbitals, col_count)
+    ham = add_tiles(slots, returned, slot_count, nd)
+
+    orbs, mark = split_orbitals(all_orbitals, col_count)
 
     own = (local_rows, local_cols)
     energy = orbital_energy[None]
     send_up = lambda a: lax.ppermute(a, "col", forward)
     send_down = lambda a: lax.ppermute(a, "col", backward)
 
-    ups = [send_up(ham) for ham in hams]
-    downs = [send_down(ham) for ham in hams]
-    ups[0] = after(ups[0], orbs)
-    totals = add_rows([hams, ups, downs], near, orbs, row_blocks, col_blocks)
-
-    early = tuple(range(nd - 1))
-    ways = []
-    ends = []
-    sums = []
-
-    def finished(last_ways):
-        sums.append(first_term(own, term_place, ends, diag, energy, orbs, col_blocks))
-        sums.append(second_term(early, own, term_place, ways, orbs, sums[0], row_blocks))
-        return sums[1]
-
-    for d in range(nd):
-        up, down = ups[d], downs[d]
-        chunks = []
-        for step in range(2, steps + 1):
-            if step == 2 and d == nd - 1 or step == 3 and d == 0:
-                up, down = after(up, totals[0]), after(down, totals[0])
-            if step == 3 and d == nd - 1:
-                up, down = after(up, ends[0]), after(down, ends[0])
-            up, down = send_up(up), send_down(down)
-            chunks += [up, down]
-        if d:
-            up, down = after(up, ends[d - 1]), after(down, ends[d - 1])
-            chunks[-2:] = [up, down]
-        chunks += [send_up(up[:half]), send_down(down[half:])]
-        total = totals[d]
+    marks = [mark, diag, *(table for where in plans for table in where)]
+    up, down = tie([send_up(ham), send_down(ham)], marks)
+    totals = None
+    for step in range(2, steps):
+        chunks = [ham, up, down] if totals is None else [up, down]
+        sums = add_rows(totals, chunks, plans[step - 2], orbs, row_blocks, col_blocks)
+        up, down, *totals = tie([send_up(up), send_down(down), *sums])
+
+    def go(d):
+        ups[d], downs[d] = send_up(ups[d]), send_down(downs[d])
+
+    def opposite(d):
+        return [send_up(ups[d][:, :half]), send_down(downs[d][:, half:])]
+
+    def finish(d, ends):
+        chunks = [up2[d], down2[d], ups[d], downs[d], *ends]
+        return response_piece(totals[d], chunks, plans[-1], orbs, diag, energy, col_blocks)
+
+    def spread(piece, held=None):
+        return row_broadcast(piece, row_count, col_count, ratio, held)
+
+    def wait(value, moving, *others):
+        kept = [a[k] for a in (ups, downs, totals) for k in moving]
+        held = tie([*value, *kept], others)
+        kept = list(held[len(value) :])
+        for a in (ups, downs, totals):
+            for k in moving:
+                a[k] = kept.pop(0)
+        return list(held[: len(value)])
+
+    ups = [up[d : d + 1] for d in range(nd)]
+    downs = [down[d : d + 1] for d in range(nd)]
+    up2, down2 = list(ups), list(downs)
+    everything = range(nd)
+    go(0)
+    wait([], everything)
+    ends = wait(opposite(0), everything)
+    for d in everything[1:]:
+        go(d)
+    pieces, sums, ways = [], [], []
+    for d in everything:
         if d == nd - 1:
-            total = after(total, ways[0][row_count // 2])
-        piece, end = response_piece(total, chunks, far, orbs, diag, energy, col_blocks)
-        ends.append(end)
-        held = None
-        if d == nd - 1:
-            held = lambda last: sums[1] if sums else finished(last)
-        ways.append(row_broadcast(piece, row_count, col_count, ratio, held))
-    return second_term((nd - 1,), own, term_place, ways[-1:], orbs, sums[0], row_blocks, sums[1])
+            totals[d] = tie([totals[d]], [ways[0][row_count // 2]])[0]
+        piece, total = finish(d, ends)
+        pieces.append(piece)
+        sums.append(total)
+        if d == 0:
+            ways.append(spread(piece))
+            wait([], [1], total)
+            ends = wait(opposite(1), everything[1:])
+        elif d < nd - 1:
+            ends = wait(opposite(d + 1), [d + 1], total)
+    for d in range(1, nd - 1):
+        ways.append(spread(pieces[d], lambda: sums[-1]))
+    piece = tie([piece], [way[row_count // 2] for way in ways])[0]
+    done = early_terms(own, term_place, ways, sums, diag, energy, orbs, row_blocks, col_blocks)
+    ways.append(spread(piece, lambda: done))
+    return last_terms(own, term_place, ways[-1], done, orbs, row_blocks)
 
 
 def solution(mesh):

time: 438 us -> 421 us (0.961)
  blocking collectives: 74.6 us -> 0 us
  waiting for transfers between devices: 129 us -> 199 us
  Pallas kernels: 136 us -> 129 us
  local copies, waits for them, and re-layouts: 38.2 us -> 32.4 us
    all_to_all x1 -> x0, blocking collectives: 74.6 us -> none  [local(): lax.all_to_all(a, ('row', 'col'), split_axis=0, concat_axis=0, tiled=True)]
    all_to_all x1 -> x2, waiting for transfers between devices: 73.8 us -> 145 us  [local(): lax.all_to_all(a, ('row', 'col'), split_axis=0, concat_axis=0, tiled=True)]
    ppermute x12 -> x8, waiting for transfers between devices: 5.81 us -> 38.4 us  [local(): send_up = lambda a: lax.ppermute(a, 'col', forward)]
    ppermute x12 -> x8, waiting for transfers between devices: 34.8 us -> 2.77 us  [local(): send_down = lambda a: lax.ppermute(a, 'col', backward)]
    ppermute x12 -> x8, starting transfers between devices: 14.9 us -> 5.89 us  [local(): send_up = lambda a: lax.ppermute(a, 'col', forward)]
    unnamed x77 -> x80, local copies, waits for them, and re-layouts: 22.8 us -> 15.7 us
    pallas_call x4 -> x3, Pallas kernels: 48.2 us -> 42 us  [call(): pl.pallas_call(kernel, out_shape=out, grid_spec=pltpu.PrefetchScalarGridS...]
    ppermute x12 -> x8, starting transfers between devices: 7.54 us -> 10.6 us  [local(): send_down = lambda a: lax.ppermute(a, 'col', backward)]
  transfers between devices with their start and end apart: 35 -> 28, of which waited for: 13 -> 12; matrix products, arithmetic and copies ran while one was open for 6% -> 5% of each run, Pallas kernels for 29% -> 29%
where the time goes in v3:
time: 421 us; the launch traced here: 420 us
  waiting for transfers between devices  199 us (47%)
  Pallas kernels  129 us (31%)
  starting transfers between devices  41.6 us (10%)
  local copies, waits for them, and re-layouts  32.4 us (8%)
  between operations  13.9 us (3%)
    all_to_all x2, waiting for transfers between devices, local(): lax.all_to_all(a, ('row', 'col'), split_axis=0, concat_axis=0, tiled=True)  145 us
    pallas_call x3, Pallas kernels, response_piece(): pl.pallas_call(functools.partial(piece_kernel, count, halves), out_shape=...  51.9 us
    pallas_call x3, Pallas kernels, call(): pl.pallas_call(kernel, out_shape=out, grid_spec=pltpu.PrefetchScalarGridS...  42 us
    ppermute x8, waiting for transfers between devices, local(): send_up = lambda a: lax.ppermute(a, 'col', forward)  38.4 us
    unnamed x80, local copies, waits for them, and re-layouts  15.7 us
    ppermute x9, starting transfers between devices, send(): return lax.ppermute(ways[parent], ('row', 'col'), pairs)  14.8 us
    pallas_call x1, Pallas kernels, batch_tiles(): pl.pallas_call(functools.partial(batch_kernel, per_range, col_count), out...  14.3 us
    pallas_call x1, Pallas kernels, split_orbitals(): pl.pallas_call(split_kernel, out_shape=(jax.ShapeDtypeStruct((count // TI...  14.2 us
  transfers between devices with their start and end apart: 28, of which 12 were waited for; matrix products, arithmetic and copies ran while one was open for 5% of the time, Pallas kernels for 29%

profile of v3, /device:TPU:0, one launch (start us, length us, event | category | flops | bytes accessed | tf_op | source)
XLA Modules:
  0.0 419.9 jit_solution(11707657385959916340)
XLA Ops:
  8.0 3.6 pick_tiles.1
  11.6 7.4 %all-to-all-start = ((f32[32,200,128]{2,1,0:T(8,128)}), f32[32,200,128]{2,1,0:T(8,128)}, u32[]{:S(2)}, u32[]{:S(2)}) async-start(f32[32,200,128]{2,1,0:T(8,128)} %pick_tiles.1), calls=%async_computation | async-start | bytes 6553600 | tf_op jit(solution)/shard_map/all_to_all | solution.py:644
  21.3 73.8 %all-to-all-done.tiles_ref = f32[32,200,128]{2,1,0:T(8,128)} async-done(((f32[32,200,128]{2,1,0:T(8,128)}), f32[32,200,128]{2,1,0:T(8,128)}, u32[]{:S(2)}, u32[]{:S(2)}) %all-to-all-start) | async-done | bytes 3276832 | tf_op jit(solution)/shard_map/all_to_all | solution.py:644
  95.1 14.3 %batch_tiles.1 = f32[32,192,128]{2,1,0:T(8,128)S(1)} custom-call(s32[8]{0:T(128)S(1)} %and_select_fusion.1.col_ref, f32[32,200,128]{2,1,0:T(8,128)} %all-to-all-done.tiles_ref, f32[512,1024]{1,0:T(8,128)S(1)} %bitcast.23, f32[1,1024]{1,0:T(1,128)S(1)} %copy-done.4, f32[1,1024]{1,0:T(1,128)S(1)} %copy-done.5, f32[3,1,1024]{2,1,0:T(1,128)S(1)} %copy-done.3), custom_call_target="tpu_custom_call" | custom-call | tf_op jit(solution)/shard_map/batch_tiles/pallas_call | solution.py:155
  111.1 2.9 all-to-all-start.1
  115.2 71.6 %all-to-all-done.1.tiles_ref = f32[32,192,128]{2,1,0:T(8,128)S(1)} async-done(((f32[32,192,128]{2,1,0:T(8,128)}), f32[32,192,128]{2,1,0:T(8,128)S(1)}, u32[]{:S(2)}, u32[]{:S(2)}) %all-to-all-start.1) | async-done | bytes 3145760 | tf_op jit(solution)/shard_map/all_to_all | solution.py:644
  186.8 2.6 add_tiles.1.refs_0_
  201.6 14.2 %split_orbitals.1 = (bf16[128,128,512]{2,1,0:T(8,128)(2,1)}, f32[8,128]{1,0:T(8,128)}) custom-call(f32[8192,512]{1,0:T(8,128)} %all-gather.2.cloned.1.call-done.orb_ref), custom_call_target="tpu_custom_call" | custom-call | bytes 33554432 | tf_op jit(solution)/shard_map/split_orbitals/pallas_call | solution.py:219
  215.8 9.8 %collective-permute-done.refs_0_ = f32[3,32,32,128]{3,2,1,0:T(8,128)S(1)} collective-permute-done((f32[3,32,32,128]{3,2,1,0:T(8,128)}, f32[3,32,32,128]{3,2,1,0:T(8,128)S(1)}, u32[]{:S(2)}, u32[]{:S(2)}) %collective-permute-start) | collective-permute-done | bytes 1572896 | tf_op jit(solution)/shard_map/ppermute | solution.py:677
  228.8 16.5 %add_rows.1 = (f32[32,64,512]{2,1,0:T(8,128)}, f32[32,64,512]{2,1,0:T(8,128)}, f32[32,64,512]{2,1,0:T(8,128)}) custom-call(s32[96]{0:T(128)} %reshape.65.refs_4_.row_id, s32[96]{0:T(128)} %reshape.66.refs_5_.col_id, s32[4]{0:T(128)} %pad_add_fusion.2.refs_6_.place_ref, f32[3,32,32,128]{3,2,1,0:T(8,128)} %add_tiles.1.refs_0_, ...), custom_call_target="tpu_custom_call" | custom-call | flops 9600000000 | bytes 8388608 | tf_op jit(solution)/shard_map/add_rows/pallas_call | solution.py:277
  245.2 17.4 %collective-permute-done.2.refs_0_ = f32[3,32,32,128]{3,2,1,0:T(8,128)S(1)} collective-permute-done((f32[3,32,32,128]{3,2,1,0:T(8,128)}, f32[3,32,32,128]{3,2,1,0:T(8,128)S(1)}, u32[]{:S(2)}, u32[]{:S(2)}) %collective-permute-start.2) | collective-permute-done | bytes 1572896 | tf_op jit(solution)/shard_map/ppermute | solution.py:677
  271.5 7.6 %collective-permute-done.4.refs_0_ = f32[1,32,32,128]{3,2,1,0:T(8,128)S(1)} collective-permute-done((f32[1,32,32,128]{3,2,1,0:T(8,128)S(1)}, f32[1,32,32,128]{3,2,1,0:T(8,128)S(1)}, u32[]{:S(2)}, u32[]{:S(2)}) %collective-permute-start.4) | collective-permute-done | bytes 524320 | tf_op jit(solution)/shard_map/ppermute | solution.py:677
  284.2 3.6 collective-permute-done.6.refs_0_
  293.6 17.2 %response_piece.3 = (f32[16,64,512]{2,1,0:T(8,128)}, f32[32,64,512]{2,1,0:T(8,128)}) custom-call(s32[160]{0:T(256)} %reshape.62.refs_7_.row_id, s32[160]{0:T(256)} %reshape.63.refs_8_.col_id, s32[6]{0:T(128)} %pad_add_fusion.1.refs_9_.place_ref, f32[1,32,32,128]{3,2,1,0:T(8,128)} %copy-done.23, f32[1,32,32,128]{3,2,1,0:T(8,128)} %copy-done.24, ...), custom_call_target="tpu_custom_call" | custom-call | flops 20000000000 | bytes 8388608 | tf_op jit(solution)/shard_map/response_piece/pallas_call | solution.py:387
  315.8 3.8 collective-permute-start.16
  326.1 17.3 %response_piece.4 = (f32[16,64,512]{2,1,0:T(8,128)}, f32[32,64,512]{2,1,0:T(8,128)}) custom-call(s32[160]{0:T(256)} %reshape.62.refs_7_.row_id, s32[160]{0:T(256)} %reshape.63.refs_8_.col_id, s32[6]{0:T(128)} %pad_add_fusion.1.refs_9_.place_ref, f32[1,32,32,128]{3,2,1,0:T(8,128)} %copy-done.21, f32[1,32,32,128]{3,2,1,0:T(8,128)} %copy-done.22, ...), custom_call_target="tpu_custom_call" | custom-call | flops 20000000000 | bytes 8388608 | tf_op jit(solution)/shard_map/response_piece/pallas_call | solution.py:387
  343.4 4.7 %collective-permute-start.17 = (f32[16,64,512]{2,1,0:T(8,128)}, f32[16,64,512]{2,1,0:T(8,128)}, u32[]{:S(2)}, u32[]{:S(2)}) collective-permute-start(f32[16,64,512]{2,1,0:T(8,128)} %get-tuple-element.121.refs_4_), channel_id=1, source_target_pairs={{0,16},{1,17},{10,26},{11,27},{20,4},{21,5},{30,14},{31,15}} | collective-permute-start | bytes 6291464 | tf_op jit(solution)/shard_map/ppermute | solution.py:573
  350.6 17.4 %response_piece.5 = (f32[16,64,512]{2,1,0:T(8,128)}, f32[32,64,512]{2,1,0:T(8,128)}) custom-call(s32[160]{0:T(256)} %reshape.62.refs_7_.row_id, s32[160]{0:T(256)} %reshape.63.refs_8_.col_id, s32[6]{0:T(128)} %pad_add_fusion.1.refs_9_.place_ref, f32[1,32,32,128]{3,2,1,0:T(8,128)} %copy-done.19, f32[1,32,32,128]{3,2,1,0:T(8,128)} %copy-done.20, ...), custom_call_target="tpu_custom_call" | custom-call | flops 20000000000 | bytes 8388608 | tf_op jit(solution)/shard_map/response_piece/pallas_call | solution.py:387
  368.2 2.4 collective-permute-done.17.refs_0_
  370.6 5.7 %collective-permute-start.19 = (f32[16,64,512]{2,1,0:T(8,128)}, f32[16,64,512]{2,1,0:T(8,128)}, u32[]{:S(2)}, u32[]{:S(2)}) collective-permute-start(f32[16,64,512]{2,1,0:T(8,128)} %tie.20.refs_0_), channel_id=1, source_target_pairs={{0,16},{1,17},{10,26},{11,27},{20,4},{21,5},{30,14},{31,15}} | collective-permute-start | bytes 6291464 | tf_op jit(solution)/shard_map/ppermute | solution.py:573
  376.3 17.1 %early_terms.1.refs_1_.refs_5_ = f32[3,1024,128]{2,1,0:T(8,128)} custom-call(s32[32]{0:T(128)} %get-tuple-element.64.row_id, s32[32]{0:T(128)} %get-tuple-element.65.col_id, s32[3]{0:T(128)} %pad_add_fusion.place_ref, f32[16,64,512]{2,1,0:T(8,128)} %get-tuple-element.119.refs_0_, f32[16,64,512]{2,1,0:T(8,128)} %collective-permute-done.20.refs_1_, ...), custom_call_target="tpu_custom_call" | custom-call | flops 100000000 | bytes 8388608 | tf_op jit(solution)/shard_map/early_terms/pallas_call | solution.py:277
  393.4 5.4 %collective-permute-done.19.refs_0_ = f32[16,64,512]{2,1,0:T(8,128)} collective-permute-done((f32[16,64,512]{2,1,0:T(8,128)}, f32[16,64,512]{2,1,0:T(8,128)}, u32[]{:S(2)}, u32[]{:S(2)}) %collective-permute-start.19) | collective-permute-done | bytes 2097184 | tf_op jit(solution)/shard_map/ppermute | solution.py:573
  398.8 4.4 %collective-permute-done.24.refs_3_ = f32[16,64,512]{2,1,0:T(8,128)S(1)} collective-permute-done((f32[16,64,512]{2,1,0:T(8,128)}, f32[16,64,512]{2,1,0:T(8,128)S(1)}, u32[]{:S(2)}, u32[]{:S(2)}) %collective-permute-start.24) | collective-permute-done | bytes 2097184 | tf_op jit(solution)/shard_map/ppermute | solution.py:573
  404.5 8.5 %last_terms.1 = f32[3,32,4096]{2,1,0:T(8,128)} custom-call(s32[32]{0:T(128)} %get-tuple-element.64.row_id, s32[32]{0:T(128)} %get-tuple-element.65.col_id, s32[3]{0:T(128)} %pad_add_fusion.place_ref, f32[16,64,512]{2,1,0:T(8,128)} %tie.20.refs_0_, f32[16,64,512]{2,1,0:T(8,128)} %collective-permute-done.18.refs_1_, f32[16,64,512]{2,1,0:T(8,128)} %tie.21.refs_2_, ...), custom_call_target="tpu_custom_call" | custom-call | flops 3200000000 | bytes 8388608 | tf_op jit(solution)/shard_map/last_terms/pallas_call | solution.py:277
  (179 shorter events, 57.0 us)
Async XLA Ops:
  6.5 195.0 %all-gather.2.cloned.1.call-start = ((), (), s32[]{:S(2)}) async-start(), calls=%async_computation.2 | async-start | bytes 20971520 | tf_op jit(solution)/shard_map/all_gather | solution.py:640
  11.6 83.4 %all-to-all-start = ((f32[32,200,128]{2,1,0:T(8,128)}), f32[32,200,128]{2,1,0:T(8,128)}, u32[]{:S(2)}, u32[]{:S(2)}) async-start(f32[32,200,128]{2,1,0:T(8,128)} %pick_tiles.1), calls=%async_computation | async-start | bytes 6553600 | tf_op jit(solution)/shard_map/all_to_all | solution.py:644
  111.1 75.8 %all-to-all-start.1 = ((f32[32,192,128]{2,1,0:T(8,128)}), f32[32,192,128]{2,1,0:T(8,128)S(1)}, u32[]{:S(2)}, u32[]{:S(2)}) async-start(f32[32,192,128]{2,1,0:T(8,128)} %copy-done), calls=%async_computation.1 | async-start | bytes 6291456 | tf_op jit(solution)/shard_map/all_to_all | solution.py:644
  189.4 36.2 %collective-permute-start = (f32[3,32,32,128]{3,2,1,0:T(8,128)}, f32[3,32,32,128]{3,2,1,0:T(8,128)S(1)}, u32[]{:S(2)}, u32[]{:S(2)}) collective-permute-start(f32[3,32,32,128]{3,2,1,0:T(8,128)} %add_tiles.1.refs_0_), channel_id=1, source_target_pairs={{0,2},{2,4},{4,6},{6,7},{7,5},{5,3},{3,1},{1,0},{8,10},{10,12},{12... | collective-permute-start | bytes 4718600 | tf_op jit(solution)/shard_map/ppermute | solution.py:677
  189.4 36.3 %collective-permute-start.1 = (f32[3,32,32,128]{3,2,1,0:T(8,128)}, f32[3,32,32,128]{3,2,1,0:T(8,128)}, u32[]{:S(2)}, u32[]{:S(2)}) collective-permute-start(f32[3,32,32,128]{3,2,1,0:T(8,128)} %add_tiles.1.refs_0_), channel_id=1, source_target_pairs={{2,0},{4,2},{6,4},{7,6},{5,7},{3,5},{1,3},{0,1},{10,8},{12,10},{14... | collective-permute-start | bytes 4718600 | tf_op jit(solution)/shard_map/ppermute | solution.py:678
  226.8 35.9 %collective-permute-start.2 = (f32[3,32,32,128]{3,2,1,0:T(8,128)}, f32[3,32,32,128]{3,2,1,0:T(8,128)S(1)}, u32[]{:S(2)}, u32[]{:S(2)}) collective-permute-start(f32[3,32,32,128]{3,2,1,0:T(8,128)} %get-tuple-element.70.refs_1_), channel_id=1, source_target_pairs={{0,2},{2,4},{4,6},{6,7},{7,5},{5,3},{3,1},{1,0},{8,10},{10,12},{12... | collective-permute-start | bytes 4718600 | tf_op jit(solution)/shard_map/ppermute | solution.py:677
  227.0 35.6 %collective-permute-start.3 = (f32[3,32,32,128]{3,2,1,0:T(8,128)}, f32[3,32,32,128]{3,2,1,0:T(8,128)S(1)}, u32[]{:S(2)}, u32[]{:S(2)}) collective-permute-start(f32[3,32,32,128]{3,2,1,0:T(8,128)} %get-tuple-element.71.refs_2_), channel_id=1, source_target_pairs={{2,0},{4,2},{6,4},{7,6},{5,7},{3,5},{1,3},{0,1},{10,8},{12,10},{14... | collective-permute-start | bytes 4718600 | tf_op jit(solution)/shard_map/ppermute | solution.py:678
  266.0 13.1 %collective-permute-start.4 = (f32[1,32,32,128]{3,2,1,0:T(8,128)S(1)}, f32[1,32,32,128]{3,2,1,0:T(8,128)S(1)}, u32[]{:S(2)}, u32[]{:S(2)}) collective-permute-start(f32[1,32,32,128]{3,2,1,0:T(8,128)S(1)} %get-tuple-element.129.refs_0_), channel_id=1, source_target_pairs={{0,2},{2,4},{4,6},{6,7},{7,5},{5,3},{3,1},{1,0},{8,10},{10,12},{12... | collective-permute-start | bytes 1572872 | tf_op jit(solution)/shard_map/ppermute | solution.py:677
  266.4 12.7 %collective-permute-start.5 = (f32[1,32,32,128]{3,2,1,0:T(8,128)S(1)}, f32[1,32,32,128]{3,2,1,0:T(8,128)S(1)}, u32[]{:S(2)}, u32[]{:S(2)}) collective-permute-start(f32[1,32,32,128]{3,2,1,0:T(8,128)S(1)} %get-tuple-element.126.refs_1_), channel_id=1, source_target_pairs={{2,0},{4,2},{6,4},{7,6},{5,7},{3,5},{1,3},{0,1},{10,8},{12,10},{14... | collective-permute-start | bytes 1572872 | tf_op jit(solution)/shard_map/ppermute | solution.py:678
  281.1 6.7 %collective-permute-start.6 = (f32[1,16,32,128]{3,2,1,0:T(8,128)S(1)}, f32[1,16,32,128]{3,2,1,0:T(8,128)S(1)}, u32[]{:S(2)}, u32[]{:S(2)}) collective-permute-start(f32[1,16,32,128]{3,2,1,0:T(8,128)S(1)} %slice.46), channel_id=1, source_target_pairs={{0,2},{2,4},{4,6},{6,7},{7,5},{5,3},{3,1},{1,0},{8,10},{10,12},{12... | collective-permute-start | bytes 786440 | tf_op jit(solution)/shard_map/ppermute | solution.py:677
  289.5 21.2 %collective-permute-start.8 = (f32[1,32,32,128]{3,2,1,0:T(8,128)}, f32[1,32,32,128]{3,2,1,0:T(8,128)S(1)}, u32[]{:S(2)}, u32[]{:S(2)}) collective-permute-start(f32[1,32,32,128]{3,2,1,0:T(8,128)} %get-tuple-element.90), channel_id=1, source_target_pairs={{0,2},{2,4},{4,6},{6,7},{7,5},{5,3},{3,1},{1,0},{8,10},{10,12},{12... | collective-permute-start | bytes 1572872 | tf_op jit(solution)/shard_map/ppermute | solution.py:677
  290.6 20.2 %collective-permute-start.9 = (f32[1,32,32,128]{3,2,1,0:T(8,128)}, f32[1,32,32,128]{3,2,1,0:T(8,128)S(1)}, u32[]{:S(2)}, u32[]{:S(2)}) collective-permute-start(f32[1,32,32,128]{3,2,1,0:T(8,128)} %get-tuple-element.91), channel_id=1, source_target_pairs={{2,0},{4,2},{6,4},{7,6},{5,7},{3,5},{1,3},{0,1},{10,8},{12,10},{14... | collective-permute-start | bytes 1572872 | tf_op jit(solution)/shard_map/ppermute | solution.py:678
  291.6 28.0 %collective-permute-start.12 = (f32[1,32,32,128]{3,2,1,0:T(8,128)}, f32[1,32,32,128]{3,2,1,0:T(8,128)S(1)}, u32[]{:S(2)}, u32[]{:S(2)}) collective-permute-start(f32[1,32,32,128]{3,2,1,0:T(8,128)} %get-tuple-element.101), channel_id=1, source_target_pairs={{0,2},{2,4},{4,6},{6,7},{7,5},{5,3},{3,1},{1,0},{8,10},{10,12},{12... | collective-permute-start | bytes 1572872 | tf_op jit(solution)/shard_map/ppermute | solution.py:677
  292.7 27.0 %collective-permute-start.13 = (f32[1,32,32,128]{3,2,1,0:T(8,128)}, f32[1,32,32,128]{3,2,1,0:T(8,128)}, u32[]{:S(2)}, u32[]{:S(2)}) collective-permute-start(f32[1,32,32,128]{3,2,1,0:T(8,128)} %get-tuple-element.102), channel_id=1, source_target_pairs={{2,0},{4,2},{6,4},{7,6},{5,7},{3,5},{1,3},{0,1},{10,8},{12,10},{14... | collective-permute-start | bytes 1572872 | tf_op jit(solution)/shard_map/ppermute | solution.py:678
  312.7 6.9 %collective-permute-start.10 = (f32[1,16,32,128]{3,2,1,0:T(8,128)S(1)}, f32[1,16,32,128]{3,2,1,0:T(8,128)S(1)}, u32[]{:S(2)}, u32[]{:S(2)}) collective-permute-start(f32[1,16,32,128]{3,2,1,0:T(8,128)S(1)} %slice.48), channel_id=1, source_target_pairs={{0,2},{2,4},{4,6},{6,7},{7,5},{5,3},{3,1},{1,0},{8,10},{10,12},{12... | collective-permute-start | bytes 786440 | tf_op jit(solution)/shard_map/ppermute | solution.py:677
  315.8 33.4 %collective-permute-start.16 = (f32[16,64,512]{2,1,0:T(8,128)}, f32[16,64,512]{2,1,0:T(8,128)S(1)}, u32[]{:S(2)}, u32[]{:S(2)}) collective-permute-start(f32[16,64,512]{2,1,0:T(8,128)} %get-tuple-element.119.refs_0_), channel_id=1, source_target_pairs={{0,16},{1,17},{10,26},{11,27},{20,4},{21,5},{30,14},{31,15}} | collective-permute-start | bytes 6291464 | tf_op jit(solution)/shard_map/ppermute | solution.py:573
  323.0 25.0 %collective-permute-start.14 = (f32[1,16,32,128]{3,2,1,0:T(8,128)S(1)}, f32[1,16,32,128]{3,2,1,0:T(8,128)S(1)}, u32[]{:S(2)}, u32[]{:S(2)}) collective-permute-start(f32[1,16,32,128]{3,2,1,0:T(8,128)S(1)} %slice.50), channel_id=1, source_target_pairs={{0,2},{2,4},{4,6},{6,7},{7,5},{5,3},{3,1},{1,0},{8,10},{10,12},{12... | collective-permute-start | bytes 786440 | tf_op jit(solution)/shard_map/ppermute | solution.py:677
  325.7 22.8 %collective-permute-start.15 = (f32[1,16,32,128]{3,2,1,0:T(8,128)S(1)}, f32[1,16,32,128]{3,2,1,0:T(8,128)S(1)}, u32[]{:S(2)}, u32[]{:S(2)}) collective-permute-start(f32[1,16,32,128]{3,2,1,0:T(8,128)S(1)} %slice.51), channel_id=1, source_target_pairs={{2,0},{4,2},{6,4},{7,6},{5,7},{3,5},{1,3},{0,1},{10,8},{12,10},{14... | collective-permute-start | bytes 786440 | tf_op jit(solution)/shard_map/ppermute | solution.py:678
  343.4 27.2 %collective-permute-start.17 = (f32[16,64,512]{2,1,0:T(8,128)}, f32[16,64,512]{2,1,0:T(8,128)}, u32[]{:S(2)}, u32[]{:S(2)}) collective-permute-start(f32[16,64,512]{2,1,0:T(8,128)} %get-tuple-element.121.refs_4_), channel_id=1, source_target_pairs={{0,16},{1,17},{10,26},{11,27},{20,4},{21,5},{30,14},{31,15}} | collective-permute-start | bytes 6291464 | tf_op jit(solution)/shard_map/ppermute | solution.py:573
  348.0 28.2 %collective-permute-start.20 = (f32[16,64,512]{2,1,0:T(8,128)}, f32[16,64,512]{2,1,0:T(8,128)}, u32[]{:S(2)}, u32[]{:S(2)}) collective-permute-start(f32[16,64,512]{2,1,0:T(8,128)} %get-tuple-element.119.refs_0_), channel_id=1, source_target_pairs={{0,8},{8,0},{16,24},{24,16},{1,9},{9,1},{17,25},{25,17},{2,10},{10... | collective-permute-start | bytes 6291464 | tf_op jit(solution)/shard_map/ppermute | solution.py:573
  348.0 28.2 %collective-permute-start.22 = (f32[16,64,512]{2,1,0:T(8,128)}, f32[16,64,512]{2,1,0:T(8,128)}, u32[]{:S(2)}, u32[]{:S(2)}) collective-permute-start(f32[16,64,512]{2,1,0:T(8,128)} %get-tuple-element.121.refs_4_), channel_id=1, source_target_pairs={{0,8},{8,0},{16,24},{24,16},{1,9},{9,1},{17,25},{25,17},{2,10},{10... | collective-permute-start | bytes 6291464 | tf_op jit(solution)/shard_map/ppermute | solution.py:573
  368.0 8.2 %collective-permute-start.21 = (f32[16,64,512]{2,1,0:T(8,128)S(1)}, f32[16,64,512]{2,1,0:T(8,128)}, u32[]{:S(2)}, u32[]{:S(2)}) collective-permute-start(f32[16,64,512]{2,1,0:T(8,128)S(1)} %copy-done.8), channel_id=1, source_target_pairs={{0,8},{8,0},{16,24},{24,16},{1,9},{9,1},{17,25},{25,17},{2,10},{10... | collective-permute-start | bytes 6291464 | tf_op jit(solution)/shard_map/ppermute | solution.py:573
  370.6 28.2 %collective-permute-start.19 = (f32[16,64,512]{2,1,0:T(8,128)}, f32[16,64,512]{2,1,0:T(8,128)}, u32[]{:S(2)}, u32[]{:S(2)}) collective-permute-start(f32[16,64,512]{2,1,0:T(8,128)} %tie.20.refs_0_), channel_id=1, source_target_pairs={{0,16},{1,17},{10,26},{11,27},{20,4},{21,5},{30,14},{31,15}} | collective-permute-start | bytes 6291464 | tf_op jit(solution)/shard_map/ppermute | solution.py:573
  376.3 22.6 %collective-permute-start.18 = (f32[16,64,512]{2,1,0:T(8,128)}, f32[16,64,512]{2,1,0:T(8,128)}, u32[]{:S(2)}, u32[]{:S(2)}) collective-permute-start(f32[16,64,512]{2,1,0:T(8,128)} %tie.20.refs_0_), channel_id=1, source_target_pairs={{0,8},{8,0},{16,24},{24,16},{1,9},{9,1},{17,25},{25,17},{2,10},{10... | collective-permute-start | bytes 6291464 | tf_op jit(solution)/shard_map/ppermute | solution.py:573
  (41 other events, 590.2 us)
Sparse Core Ops, SparseCore 0:
  8.9 169.5 all-gather.1

commit v4 on v3

--- a/solution.py
+++ b/solution.py
@@ -171,10 +171,11 @@
     )(cols, tiles, basis, weight, xc, coord)
 
 
-def add_kernel(slot_ref, tiles_ref, out_ref):
-    nd = out_ref.shape[0]
+def add_kernel(slot_ref, tiles_ref, head_ref, rest_ref):
+    nd = head_ref.shape[0] + 1
     per_range = slot_ref.shape[0] // tiles_ref.shape[0]
-    out_ref[...] = jnp.zeros(out_ref.shape, F32)
+    head_ref[...] = jnp.zeros(head_ref.shape, F32)
+    rest_ref[...] = jnp.zeros(rest_ref.shape, F32)
 
     def step(n, carry):
         for k in range(per_range):
@@ -184,7 +185,8 @@
             def _(slot=slot, k=k):
                 for d in range(nd):
                     start = (k * nd + d) * ROWS
-                    out_ref[d, slot] += tiles_ref[n, start : start + ROWS]
+                    ref, at = (head_ref, d) if d < nd - 1 else (rest_ref, 0)
+                    ref[at, slot] += tiles_ref[n, start : start + ROWS]
 
         return carry
 
@@ -194,9 +196,9 @@
 def add_tiles(slots, tiles, slot_count, nd):
     return pl.pallas_call(
         add_kernel,
-        out_shape=jax.ShapeDtypeStruct((nd, slot_count, ROWS, LANES), F32),
+        out_shape=[jax.ShapeDtypeStruct((n, slot_count, ROWS, LANES), F32) for n in (nd - 1, 1)],
         in_specs=[SMEM, VMEM],
-        out_specs=VMEM,
+        out_specs=[VMEM, VMEM],
         compiler_params=params(32),
         name="add_tiles",
     )(slots, tiles)
@@ -236,7 +238,7 @@
     )(orbitals)
 
 
-def accumulate(chunk, orb, row_id, col_id, offset, sums):
+def accumulate(read, count, orb, row_id, col_id, offset, sums):
     low = low_lanes((ROWS, LANES))
     nd = len(sums)
 
@@ -245,7 +247,7 @@
         for s in index:
             left = []
             for d in range(nd):
-                tile = chunk[d, s]
+                tile = read(d, s)
                 turned = pltpu.roll(tile, TILE, 1)
                 left += [split(jnp.where(low, tile, turned)), split(jnp.where(low, turned, tile))]
             pair = orb[col_id[offset + s]]
@@ -261,7 +263,7 @@
             for d in range(nd):
                 sums[d][block] += product[d * TILE : (d + 1) * TILE]
 
-    in_groups(chunk.shape[1], tiles, 16 if nd > 1 else 32)
+    in_groups(count, tiles, 16 if nd > 1 else 32)
 
 
 def whole(a):
@@ -293,7 +295,8 @@
 
 
 def rows_kernel(count, nd, fresh, row_id, col_id, place_ref, *refs):
-    chunks, orbs, refs = refs[:count], refs[count : 2 * count], refs[2 * count :]
+    chunks = [refs[2 * k : 2 * k + 2] for k in range(count)]
+    orbs, refs = refs[2 * count : 3 * count], refs[3 * count :]
     if fresh:
         sums = refs
         for total in sums:
@@ -306,15 +309,16 @@
         for load in loads:
             load.wait()
     offset = 0
-    for chunk, orb in zip(chunks, orbs):
-        accumulate(chunk, orb, row_id, col_id, offset, sums)
-        offset += chunk.shape[1]
+    for (head, rest), orb in zip(chunks, orbs):
+        read = lambda d, s, head=head, rest=rest: head[d, s] if d < nd - 1 else rest[0, s]
+        accumulate(read, head.shape[1], orb, row_id, col_id, offset, sums)
+        offset += head.shape[1]
 
 
 def add_rows(totals, chunks, where, orbs, row_blocks, col_blocks):
     count = len(chunks)
-    nd, slots = chunks[0].shape[:2]
-    args = list(chunks)
+    nd, slots = chunks[0][0].shape[0] + 1, chunks[0][0].shape[1]
+    args = [part for chunk in chunks for part in chunk]
     specs = [whole(c) for c in args]
     specs += [orb_spec(col_blocks, orbs, lambda r, c, p, k=k: p[k]) for k in range(count)]
     args += [orbs] * count
@@ -330,7 +334,7 @@
     )
 
 
-def piece_kernel(count, halves, row_id, col_id, place_ref, *refs):
+def piece_kernel(count, halves, at, row_id, col_id, place_ref, *refs):
     chunks, refs = refs[:count], refs[count:]
     orbs_ref, in_ref, diag_ref, energy_ref, piece_ref, total_ref, sums, square, chunk_buf, orb_buf = refs[:10]
     sem, chunk_sem, orb_sem = refs[10:]
@@ -344,7 +348,8 @@
         start = chunks[0].shape[1] if halves and k == count - 1 else 0
         start = start // 2
         target = chunk_buf.at[min(k, ranges - 1), pl.ds(start, size)]
-        moves.append(pltpu.make_async_copy(chunks[k].at[0], target, chunk_sem.at[k]))
+        source = chunks[k].at[min(at, chunks[k].shape[0] - 1)]
+        moves.append(pltpu.make_async_copy(source, target, chunk_sem.at[k]))
         moves[-1].start()
         if k < ranges:
             source = orbs_ref.at[pl.ds(place_ref[k] * col_blocks, col_blocks)]
@@ -355,7 +360,8 @@
     for k in range(ranges):
         for move in moves[2 * k : 2 * k + 2 + (halves if k == ranges - 1 else 0)]:
             move.wait()
-        accumulate(chunk_buf.at[pl.ds(k, 1)], orb_buf.at[k], row_id, col_id, offset, [sums])
+        read = lambda d, s, k=k: chunk_buf[k, s]
+        accumulate(read, chunk_buf.shape[1], orb_buf.at[k], row_id, col_id, offset, [sums])
         offset += chunk_buf.shape[1]
     store = pltpu.make_async_copy(sums, total_ref, sem)
     store.start()
@@ -377,15 +383,15 @@
     store.wait()
 
 
-def response_piece(total, chunks, where, orbs, diag, energy, col_blocks):
+def response_piece(total, chunks, at, where, orbs, diag, energy, col_blocks):
     count = len(chunks)
-    halves = int(chunks[-1].shape != chunks[0].shape)
+    halves = int(chunks[-1].shape[1] != chunks[0].shape[1])
     ranges = count - halves
     nocc = orbs.shape[2]
     hbm = pl.BlockSpec(memory_space=pl.ANY)
     piece = jax.ShapeDtypeStruct((col_blocks, TILE, nocc), F32)
     return pl.pallas_call(
-        functools.partial(piece_kernel, count, halves),
+        functools.partial(piece_kernel, count, halves, at),
         out_shape=(piece, jax.ShapeDtypeStruct(total.shape, F32)),
         grid_spec=pltpu.PrefetchScalarGridSpec(
             num_scalar_prefetch=3,
@@ -542,6 +548,7 @@
             pltpu.SemaphoreType.DMA,
         ],
         slots,
+        mib=32,
     )
 
 
@@ -668,7 +675,7 @@
         per_range, col_count, own_cols, arrived, basis_values[0], grid_weight, xc_kernel, grid_coord
     )
     returned = exchange(built)
-    ham = add_tiles(slots, returned, slot_count, nd)
+    hams = add_tiles(slots, returned, slot_count, nd)
 
     orbs, mark = split_orbitals(all_orbitals, col_count)
 
@@ -678,57 +685,55 @@
     send_down = lambda a: lax.ppermute(a, "col", backward)
 
     marks = [mark, diag, *(table for where in plans for table in where)]
-    up, down = tie([send_up(ham), send_down(ham)], marks)
+    held = tie([send_up(a) for a in hams] + [send_down(a) for a in hams], marks)
+    ups, downs = list(held[:2]), list(held[2:])
     totals = None
     for step in range(2, steps):
-        chunks = [ham, up, down] if totals is None else [up, down]
+        chunks = [hams, ups, downs] if totals is None else [ups, downs]
         sums = add_rows(totals, chunks, plans[step - 2], orbs, row_blocks, col_blocks)
-        up, down, *totals = tie([send_up(up), send_down(down), *sums])
-
-    def go(d):
-        ups[d], downs[d] = send_up(ups[d]), send_down(downs[d])
-
-    def opposite(d):
-        return [send_up(ups[d][:, :half]), send_down(downs[d][:, half:])]
-
-    def finish(d, ends):
-        chunks = [up2[d], down2[d], ups[d], downs[d], *ends]
-        return response_piece(totals[d], chunks, plans[-1], orbs, diag, energy, col_blocks)
+        up, down = send_up(ups[0]), send_down(downs[0])
+        if step < steps - 1:
+            ups[1], downs[1] = send_up(ups[1]), send_down(downs[1])
+        ups[0], downs[0], ups[1], downs[1], *totals = tie([up, down, ups[1], downs[1], *sums])
+
+    def opposite(up, down):
+        return [send_up(up[:, :half]), send_down(down[:, half:])]
+
+    def finish(d, chunks):
+        return response_piece(
+            totals[d], chunks, d % (nd - 1), plans[-1], orbs, diag, energy, col_blocks
+        )
 
     def spread(piece, held=None):
         return row_broadcast(piece, row_count, col_count, ratio, held)
 
-    def wait(value, moving, *others):
-        kept = [a[k] for a in (ups, downs, totals) for k in moving]
-        held = tie([*value, *kept], others)
-        kept = list(held[len(value) :])
-        for a in (ups, downs, totals):
-            for k in moving:
-                a[k] = kept.pop(0)
-        return list(held[: len(value)])
-
-    ups = [up[d : d + 1] for d in range(nd)]
-    downs = [down[d : d + 1] for d in range(nd)]
-    up2, down2 = list(ups), list(downs)
-    everything = range(nd)
-    go(0)
-    wait([], everything)
-    ends = wait(opposite(0), everything)
-    for d in everything[1:]:
-        go(d)
+    up3, down3, *totals = tie([send_up(ups[0]), send_down(downs[0]), *totals])
     pieces, sums, ways = [], [], []
-    for d in everything:
-        if d == nd - 1:
-            totals[d] = tie([totals[d]], [ways[0][row_count // 2]])[0]
-        piece, total = finish(d, ends)
+    held = tie([*opposite(up3[:1], down3[:1]), up3, down3, ups[1], downs[1], *totals])
+    for d in range(nd - 1):
+        up_end, down_end, up3, down3, ups[1], downs[1], *totals[d:] = held
+        later = [up_end, down_end]
+        if d < nd - 2:
+            later = opposite(up3[d + 1 : d + 2], down3[d + 1 : d + 2])
+        if d == 0:
+            last2 = [send_up(ups[1]), send_down(downs[1])]
+        if d == nd - 2:
+            last3 = [send_up(last2[0]), send_down(last2[1])]
+        piece, total = finish(d, [ups[0], downs[0], up3, down3, up_end, down_end])
         pieces.append(piece)
         sums.append(total)
-        if d == 0:
-            ways.append(spread(piece))
-            wait([], [1], total)
-            ends = wait(opposite(1), everything[1:])
-        elif d < nd - 1:
-            ends = wait(opposite(d + 1), [d + 1], total)
+        ways.append(spread(piece) if d == 0 else None)
+        if d < nd - 2:
+            held = tie([*later, up3, down3, *last2, *totals[d + 1 :]], [total])
+            last2 = held[4:6]
+    last2 = list(last2)
+    last3[0], last3[1], last2[0], last2[1], totals[-1] = tie([*last3, *last2, totals[-1]], [sums[-1]])
+    up_end, down_end, *last3, last2[0], last2[1], totals[-1] = tie(
+        [*opposite(*last3), *last3, *last2, totals[-1]], [ways[0][row_count // 2]]
+    )
+    piece, total = finish(nd - 1, [*last2, *last3, up_end, down_end])
+    sums.append(total)
+    ways = ways[:1]
     for d in range(1, nd - 1):
         ways.append(spread(pieces[d], lambda: sums[-1]))
     piece = tie([piece], [way[row_count // 2] for way in ways])[0]

time: 421 us -> 418 us (level)
    unnamed x80 -> x78, local copies, waits for them, and re-layouts: 15.7 us -> 13.5 us
    ppermute x8 -> x9, waiting for transfers between devices: 38.4 us -> 40 us  [local(): send_up = lambda a: lax.ppermute(a, 'col', forward)]
    ppermute x8 -> x9, starting transfers between devices: 10.6 us -> 11.8 us  [local(): send_down = lambda a: lax.ppermute(a, 'col', backward)]
  transfers between devices with their start and end apart: 28 -> 30, of which waited for: 12 -> 12; matrix products, arithmetic and copies ran while one was open for 5% -> 4% of each run, Pallas kernels for 29% -> 29%
where the time goes in v4:
time: 418 us; the launch traced here: 416 us
  waiting for transfers between devices  200 us (48%)
  Pallas kernels  127 us (30%)
  starting transfers between devices  41.9 us (10%)
  local copies, waits for them, and re-layouts  29.2 us (7%)
  between operations  13.9 us (3%)
    all_to_all x2, waiting for transfers between devices, local(): lax.all_to_all(a, ('row', 'col'), split_axis=0, concat_axis=0, tiled=True)  144 us
    pallas_call x3, Pallas kernels, response_piece(): pl.pallas_call(functools.partial(piece_kernel, count, halves, at), out_sh...  51.9 us
    pallas_call x3, Pallas kernels, call(): pl.pallas_call(kernel, out_shape=out, grid_spec=pltpu.PrefetchScalarGridS...  40.6 us
    ppermute x9, waiting for transfers between devices, local(): send_up = lambda a: lax.ppermute(a, 'col', forward)  40 us
    pallas_call x1, Pallas kernels, batch_tiles(): pl.pallas_call(functools.partial(batch_kernel, per_range, col_count), out...  14.3 us
    pallas_call x1, Pallas kernels, split_orbitals(): pl.pallas_call(split_kernel, out_shape=(jax.ShapeDtypeStruct((count // TI...  14.2 us
    unnamed x78, local copies, waits for them, and re-layouts  13.5 us
    ppermute x9, starting transfers between devices, send(): return lax.ppermute(ways[parent], ('row', 'col'), pairs)  13 us
  transfers between devices with their start and end apart: 30, of which 12 were waited for; matrix products, arithmetic and copies ran while one was open for 4% of the time, Pallas kernels for 29%

profile of v4, /device:TPU:0, one launch (start us, length us, event | category | flops | bytes accessed | tf_op | source)
XLA Modules:
  0.0 416.2 jit_solution(15768652445765874681)
XLA Ops:
  8.0 3.7 pick_tiles.1
  11.7 7.4 %all-to-all-start = ((f32[32,200,128]{2,1,0:T(8,128)}), f32[32,200,128]{2,1,0:T(8,128)}, u32[]{:S(2)}, u32[]{:S(2)}) async-start(f32[32,200,128]{2,1,0:T(8,128)} %pick_tiles.1), calls=%async_computation | async-start | bytes 6553600 | tf_op jit(solution)/shard_map/all_to_all | solution.py:651
  21.4 73.7 %all-to-all-done.tiles_ref = f32[32,200,128]{2,1,0:T(8,128)} async-done(((f32[32,200,128]{2,1,0:T(8,128)}), f32[32,200,128]{2,1,0:T(8,128)}, u32[]{:S(2)}, u32[]{:S(2)}) %all-to-all-start) | async-done | bytes 3276832 | tf_op jit(solution)/shard_map/all_to_all | solution.py:651
  95.1 14.3 %batch_tiles.1 = f32[32,192,128]{2,1,0:T(8,128)S(1)} custom-call(s32[8]{0:T(128)S(1)} %and_select_fusion.1.col_ref, f32[32,200,128]{2,1,0:T(8,128)} %all-to-all-done.tiles_ref, f32[512,1024]{1,0:T(8,128)S(1)} %bitcast.23, f32[1,1024]{1,0:T(1,128)S(1)} %copy-done.10, f32[1,1024]{1,0:T(1,128)S(1)} %copy-done.11, f32[3,1,1024]{2,1,0:T(1,128)S(1)} %copy-done.6), custom_call_target="tpu_custom_call" | custom-call | tf_op jit(solution)/shard_map/batch_tiles/pallas_call | solution.py:155
  111.1 2.9 all-to-all-start.1
  116.6 70.3 %all-to-all-done.1.tiles_ref = f32[32,192,128]{2,1,0:T(8,128)S(1)} async-done(((f32[32,192,128]{2,1,0:T(8,128)}), f32[32,192,128]{2,1,0:T(8,128)S(1)}, u32[]{:S(2)}, u32[]{:S(2)}) %all-to-all-start.1) | async-done | bytes 3145760 | tf_op jit(solution)/shard_map/all_to_all | solution.py:651
  203.1 14.2 %split_orbitals.1 = (bf16[128,128,512]{2,1,0:T(8,128)(2,1)}, f32[8,128]{1,0:T(8,128)}) custom-call(f32[8192,512]{1,0:T(8,128)} %all-gather.2.cloned.1.call-done.orb_ref), custom_call_target="tpu_custom_call" | custom-call | bytes 33554432 | tf_op jit(solution)/shard_map/split_orbitals/pallas_call | solution.py:221
  217.3 8.9 %collective-permute-done.1.refs_1_ = f32[1,32,32,128]{3,2,1,0:T(8,128)S(1)} collective-permute-done((f32[1,32,32,128]{3,2,1,0:T(8,128)}, f32[1,32,32,128]{3,2,1,0:T(8,128)S(1)}, u32[]{:S(2)}, u32[]{:S(2)}) %collective-permute-start.1) | collective-permute-done | bytes 524320 | tf_op jit(solution)/shard_map/ppermute | solution.py:684
  229.6 16.5 %add_rows.1 = (f32[32,64,512]{2,1,0:T(8,128)}, f32[32,64,512]{2,1,0:T(8,128)}, f32[32,64,512]{2,1,0:T(8,128)}) custom-call(s32[96]{0:T(128)} %reshape.65.refs_6_.row_id, s32[96]{0:T(128)} %reshape.66.refs_7_.col_id, s32[4]{0:T(128)} %pad_add_fusion.2.refs_8_.place_ref, f32[2,32,32,128]{3,2,1,0:T(8,128)} %get-tuple-element.72.refs_0_, ...), custom_call_target="tpu_custom_call" | custom-call | flops 9600000000 | bytes 8388608 | tf_op jit(solution)/shard_map/add_rows/pallas_call | solution.py:279
  246.1 6.0 %collective-permute-done.4.refs_0_ = f32[2,32,32,128]{3,2,1,0:T(8,128)S(1)} collective-permute-done((f32[2,32,32,128]{3,2,1,0:T(8,128)}, f32[2,32,32,128]{3,2,1,0:T(8,128)S(1)}, u32[]{:S(2)}, u32[]{:S(2)}) %collective-permute-start.4) | collective-permute-done | bytes 1048608 | tf_op jit(solution)/shard_map/ppermute | solution.py:684
  255.4 21.8 %collective-permute-done.6.refs_0_ = f32[2,32,32,128]{3,2,1,0:T(8,128)S(1)} collective-permute-done((f32[2,32,32,128]{3,2,1,0:T(8,128)}, f32[2,32,32,128]{3,2,1,0:T(8,128)S(1)}, u32[]{:S(2)}, u32[]{:S(2)}) %collective-permute-start.6) | collective-permute-done | bytes 1048608 | tf_op jit(solution)/shard_map/ppermute | solution.py:684
  282.6 3.3 collective-permute-done.8.refs_0_
  285.9 2.4 collective-permute-done.9.refs_1_
  295.8 17.2 %response_piece.3 = (f32[16,64,512]{2,1,0:T(8,128)}, f32[32,64,512]{2,1,0:T(8,128)}) custom-call(s32[160]{0:T(256)} %reshape.62.refs_9_.row_id, s32[160]{0:T(256)} %reshape.63.refs_10_.col_id, s32[6]{0:T(128)} %pad_add_fusion.1.refs_11_.place_ref, f32[2,32,32,128]{3,2,1,0:T(8,128)} %get-tuple-element.84.refs_0_, ...), custom_call_target="tpu_custom_call" | custom-call | flops 20000000000 | bytes 8388608 | tf_op jit(solution)/shard_map/response_piece/pallas_call | solution.py:393
  313.0 2.8 collective-permute-start.18
  319.4 17.3 %response_piece.4 = (f32[16,64,512]{2,1,0:T(8,128)}, f32[32,64,512]{2,1,0:T(8,128)}) custom-call(s32[160]{0:T(256)} %reshape.62.refs_9_.row_id, s32[160]{0:T(256)} %reshape.63.refs_10_.col_id, s32[6]{0:T(128)} %pad_add_fusion.1.refs_11_.place_ref, f32[2,32,32,128]{3,2,1,0:T(8,128)} %get-tuple-element.84.refs_0_, ...), custom_call_target="tpu_custom_call" | custom-call | flops 20000000000 | bytes 8388608 | tf_op jit(solution)/shard_map/response_piece/pallas_call | solution.py:393
  341.8 3.8 collective-permute-start.19
  347.5 17.4 %response_piece.5 = (f32[16,64,512]{2,1,0:T(8,128)}, f32[32,64,512]{2,1,0:T(8,128)}) custom-call(s32[160]{0:T(256)} %reshape.62.refs_9_.row_id, s32[160]{0:T(256)} %reshape.63.refs_10_.col_id, s32[6]{0:T(128)} %pad_add_fusion.1.refs_11_.place_ref, f32[1,32,32,128]{3,2,1,0:T(8,128)} %get-tuple-element.121.refs_0_, ...), custom_call_target="tpu_custom_call" | custom-call | flops 20000000000 | bytes 8388608 | tf_op jit(solution)/shard_map/response_piece/pallas_call | solution.py:393
  365.1 2.9 collective-permute-done.19.refs_0_
  368.1 5.7 %collective-permute-start.21 = (f32[16,64,512]{2,1,0:T(8,128)}, f32[16,64,512]{2,1,0:T(8,128)}, u32[]{:S(2)}, u32[]{:S(2)}) collective-permute-start(f32[16,64,512]{2,1,0:T(8,128)} %tie.18.refs_0_), channel_id=1, source_target_pairs={{0,16},{1,17},{10,26},{11,27},{20,4},{21,5},{30,14},{31,15}} | collective-permute-start | bytes 6291464 | tf_op jit(solution)/shard_map/ppermute | solution.py:580
  373.8 17.0 %early_terms.1.refs_1_.refs_5_ = f32[3,1024,128]{2,1,0:T(8,128)} custom-call(s32[32]{0:T(128)} %get-tuple-element.68.row_id, s32[32]{0:T(128)} %get-tuple-element.69.col_id, s32[3]{0:T(128)} %pad_add_fusion.place_ref, f32[16,64,512]{2,1,0:T(8,128)} %get-tuple-element.120.refs_0_, f32[16,64,512]{2,1,0:T(8,128)} %collective-permute-done.22.refs_1_, ...), custom_call_target="tpu_custom_call" | custom-call | flops 100000000 | bytes 8388608 | tf_op jit(solution)/shard_map/early_terms/pallas_call | solution.py:279
  390.9 5.4 %collective-permute-done.21.refs_0_ = f32[16,64,512]{2,1,0:T(8,128)} collective-permute-done((f32[16,64,512]{2,1,0:T(8,128)}, f32[16,64,512]{2,1,0:T(8,128)}, u32[]{:S(2)}, u32[]{:S(2)}) %collective-permute-start.21) | collective-permute-done | bytes 2097184 | tf_op jit(solution)/shard_map/ppermute | solution.py:580
  396.3 4.4 %collective-permute-done.26.refs_3_ = f32[16,64,512]{2,1,0:T(8,128)S(1)} collective-permute-done((f32[16,64,512]{2,1,0:T(8,128)}, f32[16,64,512]{2,1,0:T(8,128)S(1)}, u32[]{:S(2)}, u32[]{:S(2)}) %collective-permute-start.26) | collective-permute-done | bytes 2097184 | tf_op jit(solution)/shard_map/ppermute | solution.py:580
  402.3 7.1 %last_terms.1 = f32[3,32,4096]{2,1,0:T(8,128)} custom-call(s32[32]{0:T(128)S(1)} %copy-done.9, s32[32]{0:T(128)S(1)} %copy-done.8, s32[3]{0:T(128)S(1)} %copy-done.7, f32[16,64,512]{2,1,0:T(8,128)S(1)} %copy-done.2, f32[16,64,512]{2,1,0:T(8,128)} %collective-permute-done.20.refs_1_, f32[16,64,512]{2,1,0:T(8,128)} %tie.19.refs_2_, ...), custom_call_target="tpu_custom_call" | custom-call | flops 3200000000 | bytes 8388608 | tf_op jit(solution)/shard_map/last_terms/pallas_call | solution.py:279
  (178 shorter events, 55.9 us)
Async XLA Ops:
  6.5 196.5 %all-gather.2.cloned.1.call-start = ((), (), s32[]{:S(2)}) async-start(), calls=%async_computation.2 | async-start | bytes 20971520 | tf_op jit(solution)/shard_map/all_gather | solution.py:647
  11.7 83.4 %all-to-all-start = ((f32[32,200,128]{2,1,0:T(8,128)}), f32[32,200,128]{2,1,0:T(8,128)}, u32[]{:S(2)}, u32[]{:S(2)}) async-start(f32[32,200,128]{2,1,0:T(8,128)} %pick_tiles.1), calls=%async_computation | async-start | bytes 6553600 | tf_op jit(solution)/shard_map/all_to_all | solution.py:651
  111.1 75.8 %all-to-all-start.1 = ((f32[32,192,128]{2,1,0:T(8,128)}), f32[32,192,128]{2,1,0:T(8,128)S(1)}, u32[]{:S(2)}, u32[]{:S(2)}) async-start(f32[32,192,128]{2,1,0:T(8,128)} %copy-done.1), calls=%async_computation.1 | async-start | bytes 6291456 | tf_op jit(solution)/shard_map/all_to_all | solution.py:651
  190.1 36.2 %collective-permute-start = (f32[2,32,32,128]{3,2,1,0:T(8,128)}, f32[2,32,32,128]{3,2,1,0:T(8,128)S(1)}, u32[]{:S(2)}, u32[]{:S(2)}) collective-permute-start(f32[2,32,32,128]{3,2,1,0:T(8,128)} %get-tuple-element.72.refs_0_), channel_id=1, source_target_pairs={{0,2},{2,4},{4,6},{6,7},{7,5},{5,3},{3,1},{1,0},{8,10},{10,12},{12... | collective-permute-start | bytes 3145736 | tf_op jit(solution)/shard_map/ppermute | solution.py:684
  190.1 36.2 %collective-permute-start.2 = (f32[2,32,32,128]{3,2,1,0:T(8,128)}, f32[2,32,32,128]{3,2,1,0:T(8,128)}, u32[]{:S(2)}, u32[]{:S(2)}) collective-permute-start(f32[2,32,32,128]{3,2,1,0:T(8,128)} %get-tuple-element.72.refs_0_), channel_id=1, source_target_pairs={{2,0},{4,2},{6,4},{7,6},{5,7},{3,5},{1,3},{0,1},{10,8},{12,10},{14... | collective-permute-start | bytes 3145736 | tf_op jit(solution)/shard_map/ppermute | solution.py:685
  193.4 32.8 %collective-permute-start.1 = (f32[1,32,32,128]{3,2,1,0:T(8,128)}, f32[1,32,32,128]{3,2,1,0:T(8,128)S(1)}, u32[]{:S(2)}, u32[]{:S(2)}) collective-permute-start(f32[1,32,32,128]{3,2,1,0:T(8,128)} %copy-done.5), channel_id=1, source_target_pairs={{0,2},{2,4},{4,6},{6,7},{7,5},{5,3},{3,1},{1,0},{8,10},{10,12},{12... | collective-permute-start | bytes 1572872 | tf_op jit(solution)/shard_map/ppermute | solution.py:684
  193.5 32.8 %collective-permute-start.3 = (f32[1,32,32,128]{3,2,1,0:T(8,128)}, f32[1,32,32,128]{3,2,1,0:T(8,128)S(1)}, u32[]{:S(2)}, u32[]{:S(2)}) collective-permute-start(f32[1,32,32,128]{3,2,1,0:T(8,128)} %copy-done.5), channel_id=1, source_target_pairs={{2,0},{4,2},{6,4},{7,6},{5,7},{3,5},{1,3},{0,1},{10,8},{12,10},{14... | collective-permute-start | bytes 1572872 | tf_op jit(solution)/shard_map/ppermute | solution.py:685
  227.6 24.5 %collective-permute-start.4 = (f32[2,32,32,128]{3,2,1,0:T(8,128)}, f32[2,32,32,128]{3,2,1,0:T(8,128)S(1)}, u32[]{:S(2)}, u32[]{:S(2)}) collective-permute-start(f32[2,32,32,128]{3,2,1,0:T(8,128)} %get-tuple-element.76.refs_2_), channel_id=1, source_target_pairs={{0,2},{2,4},{4,6},{6,7},{7,5},{5,3},{3,1},{1,0},{8,10},{10,12},{12... | collective-permute-start | bytes 3145736 | tf_op jit(solution)/shard_map/ppermute | solution.py:684
  228.0 24.2 %collective-permute-start.5 = (f32[2,32,32,128]{3,2,1,0:T(8,128)}, f32[2,32,32,128]{3,2,1,0:T(8,128)S(1)}, u32[]{:S(2)}, u32[]{:S(2)}) collective-permute-start(f32[2,32,32,128]{3,2,1,0:T(8,128)} %get-tuple-element.77.refs_4_), channel_id=1, source_target_pairs={{2,0},{4,2},{6,4},{7,6},{5,7},{3,5},{1,3},{0,1},{10,8},{12,10},{14... | collective-permute-start | bytes 3145736 | tf_op jit(solution)/shard_map/ppermute | solution.py:685
  253.4 23.8 %collective-permute-start.6 = (f32[2,32,32,128]{3,2,1,0:T(8,128)}, f32[2,32,32,128]{3,2,1,0:T(8,128)S(1)}, u32[]{:S(2)}, u32[]{:S(2)}) collective-permute-start(f32[2,32,32,128]{3,2,1,0:T(8,128)} %get-tuple-element.84.refs_0_), channel_id=1, source_target_pairs={{0,2},{2,4},{4,6},{6,7},{7,5},{5,3},{3,1},{1,0},{8,10},{10,12},{12... | collective-permute-start | bytes 3145736 | tf_op jit(solution)/shard_map/ppermute | solution.py:684
  254.6 22.7 %collective-permute-start.7 = (f32[2,32,32,128]{3,2,1,0:T(8,128)}, f32[2,32,32,128]{3,2,1,0:T(8,128)S(1)}, u32[]{:S(2)}, u32[]{:S(2)}) collective-permute-start(f32[2,32,32,128]{3,2,1,0:T(8,128)} %get-tuple-element.85.refs_1_), channel_id=1, source_target_pairs={{2,0},{4,2},{6,4},{7,6},{5,7},{3,5},{1,3},{0,1},{10,8},{12,10},{14... | collective-permute-start | bytes 3145736 | tf_op jit(solution)/shard_map/ppermute | solution.py:685
  290.0 25.8 %collective-permute-start.10 = (f32[1,16,32,128]{3,2,1,0:T(8,128)S(1)}, f32[1,16,32,128]{3,2,1,0:T(8,128)S(1)}, u32[]{:S(2)}, u32[]{:S(2)}) collective-permute-start(f32[1,16,32,128]{3,2,1,0:T(8,128)S(1)} %slice.32), channel_id=1, source_target_pairs={{0,2},{2,4},{4,6},{6,7},{7,5},{5,3},{3,1},{1,0},{8,10},{10,12},{12... | collective-permute-start | bytes 786440 | tf_op jit(solution)/shard_map/ppermute | solution.py:684
  293.5 22.4 %collective-permute-start.11 = (f32[1,16,32,128]{3,2,1,0:T(8,128)}, f32[1,16,32,128]{3,2,1,0:T(8,128)S(1)}, u32[]{:S(2)}, u32[]{:S(2)}) collective-permute-start(f32[1,16,32,128]{3,2,1,0:T(8,128)} %slice.33), channel_id=1, source_target_pairs={{2,0},{4,2},{6,4},{7,6},{5,7},{3,5},{1,3},{0,1},{10,8},{12,10},{14... | collective-permute-start | bytes 786440 | tf_op jit(solution)/shard_map/ppermute | solution.py:685
  293.8 22.1 %collective-permute-start.12 = (f32[1,32,32,128]{3,2,1,0:T(8,128)}, f32[1,32,32,128]{3,2,1,0:T(8,128)S(1)}, u32[]{:S(2)}, u32[]{:S(2)}) collective-permute-start(f32[1,32,32,128]{3,2,1,0:T(8,128)} %get-tuple-element.98), channel_id=1, source_target_pairs={{0,2},{2,4},{4,6},{6,7},{7,5},{5,3},{3,1},{1,0},{8,10},{10,12},{12... | collective-permute-start | bytes 1572872 | tf_op jit(solution)/shard_map/ppermute | solution.py:684
  295.6 20.4 %collective-permute-start.13 = (f32[1,32,32,128]{3,2,1,0:T(8,128)}, f32[1,32,32,128]{3,2,1,0:T(8,128)S(1)}, u32[]{:S(2)}, u32[]{:S(2)}) collective-permute-start(f32[1,32,32,128]{3,2,1,0:T(8,128)} %get-tuple-element.99), channel_id=1, source_target_pairs={{2,0},{4,2},{6,4},{7,6},{5,7},{3,5},{1,3},{0,1},{10,8},{12,10},{14... | collective-permute-start | bytes 1572872 | tf_op jit(solution)/shard_map/ppermute | solution.py:685
  313.0 33.1 %collective-permute-start.18 = (f32[16,64,512]{2,1,0:T(8,128)}, f32[16,64,512]{2,1,0:T(8,128)S(1)}, u32[]{:S(2)}, u32[]{:S(2)}) collective-permute-start(f32[16,64,512]{2,1,0:T(8,128)} %get-tuple-element.120.refs_0_), channel_id=1, source_target_pairs={{0,16},{1,17},{10,26},{11,27},{20,4},{21,5},{30,14},{31,15}} | collective-permute-start | bytes 6291464 | tf_op jit(solution)/shard_map/ppermute | solution.py:580
  317.4 19.3 %collective-permute-start.14 = (f32[1,32,32,128]{3,2,1,0:T(8,128)}, f32[1,32,32,128]{3,2,1,0:T(8,128)S(1)}, u32[]{:S(2)}, u32[]{:S(2)}) collective-permute-start(f32[1,32,32,128]{3,2,1,0:T(8,128)} %get-tuple-element.106.refs_2_), channel_id=1, source_target_pairs={{0,2},{2,4},{4,6},{6,7},{7,5},{5,3},{3,1},{1,0},{8,10},{10,12},{12... | collective-permute-start | bytes 1572872 | tf_op jit(solution)/shard_map/ppermute | solution.py:684
  317.4 19.3 %collective-permute-start.15 = (f32[1,32,32,128]{3,2,1,0:T(8,128)}, f32[1,32,32,128]{3,2,1,0:T(8,128)S(1)}, u32[]{:S(2)}, u32[]{:S(2)}) collective-permute-start(f32[1,32,32,128]{3,2,1,0:T(8,128)} %get-tuple-element.107.refs_3_), channel_id=1, source_target_pairs={{2,0},{4,2},{6,4},{7,6},{5,7},{3,5},{1,3},{0,1},{10,8},{12,10},{14... | collective-permute-start | bytes 1572872 | tf_op jit(solution)/shard_map/ppermute | solution.py:685
  341.8 26.3 %collective-permute-start.19 = (f32[16,64,512]{2,1,0:T(8,128)}, f32[16,64,512]{2,1,0:T(8,128)}, u32[]{:S(2)}, u32[]{:S(2)}) collective-permute-start(f32[16,64,512]{2,1,0:T(8,128)} %get-tuple-element.129.refs_4_), channel_id=1, source_target_pairs={{0,16},{1,17},{10,26},{11,27},{20,4},{21,5},{30,14},{31,15}} | collective-permute-start | bytes 6291464 | tf_op jit(solution)/shard_map/ppermute | solution.py:580
  345.6 28.2 %collective-permute-start.22 = (f32[16,64,512]{2,1,0:T(8,128)}, f32[16,64,512]{2,1,0:T(8,128)}, u32[]{:S(2)}, u32[]{:S(2)}) collective-permute-start(f32[16,64,512]{2,1,0:T(8,128)} %get-tuple-element.120.refs_0_), channel_id=1, source_target_pairs={{0,8},{8,0},{16,24},{24,16},{1,9},{9,1},{17,25},{25,17},{2,10},{10... | collective-permute-start | bytes 6291464 | tf_op jit(solution)/shard_map/ppermute | solution.py:580
  345.6 28.2 %collective-permute-start.24 = (f32[16,64,512]{2,1,0:T(8,128)}, f32[16,64,512]{2,1,0:T(8,128)}, u32[]{:S(2)}, u32[]{:S(2)}) collective-permute-start(f32[16,64,512]{2,1,0:T(8,128)} %get-tuple-element.129.refs_4_), channel_id=1, source_target_pairs={{0,8},{8,0},{16,24},{24,16},{1,9},{9,1},{17,25},{25,17},{2,10},{10... | collective-permute-start | bytes 6291464 | tf_op jit(solution)/shard_map/ppermute | solution.py:580
  365.0 8.8 %collective-permute-start.23 = (f32[16,64,512]{2,1,0:T(8,128)S(1)}, f32[16,64,512]{2,1,0:T(8,128)}, u32[]{:S(2)}, u32[]{:S(2)}) collective-permute-start(f32[16,64,512]{2,1,0:T(8,128)S(1)} %copy-done.14), channel_id=1, source_target_pairs={{0,8},{8,0},{16,24},{24,16},{1,9},{9,1},{17,25},{25,17},{2,10},{10... | collective-permute-start | bytes 6291464 | tf_op jit(solution)/shard_map/ppermute | solution.py:580
  368.1 28.2 %collective-permute-start.21 = (f32[16,64,512]{2,1,0:T(8,128)}, f32[16,64,512]{2,1,0:T(8,128)}, u32[]{:S(2)}, u32[]{:S(2)}) collective-permute-start(f32[16,64,512]{2,1,0:T(8,128)} %tie.18.refs_0_), channel_id=1, source_target_pairs={{0,16},{1,17},{10,26},{11,27},{20,4},{21,5},{30,14},{31,15}} | collective-permute-start | bytes 6291464 | tf_op jit(solution)/shard_map/ppermute | solution.py:580
  373.8 22.5 %collective-permute-start.20 = (f32[16,64,512]{2,1,0:T(8,128)}, f32[16,64,512]{2,1,0:T(8,128)}, u32[]{:S(2)}, u32[]{:S(2)}) collective-permute-start(f32[16,64,512]{2,1,0:T(8,128)} %tie.18.refs_0_), channel_id=1, source_target_pairs={{0,8},{8,0},{16,24},{24,16},{1,9},{9,1},{17,25},{25,17},{2,10},{10... | collective-permute-start | bytes 6291464 | tf_op jit(solution)/shard_map/ppermute | solution.py:580
  (44 other events, 475.8 us)
Sparse Core Ops, SparseCore 0:
  8.9 169.5 all-gather.1

commit v5 on v4

--- a/solution.py
+++ b/solution.py
@@ -467,12 +467,12 @@
     return pltpu.make_async_copy(ways[0], x_ref, sem).wait
 
 
-def early_kernel(nd, way_count, row_id, col_id, place_ref, *refs):
-    ways = [refs[d * way_count : (d + 1) * way_count] for d in range(nd - 1)]
-    refs = refs[(nd - 1) * way_count :]
+def early_kernel(nd, count, way_count, row_id, col_id, place_ref, *refs):
+    ways = [refs[d * way_count : (d + 1) * way_count] for d in range(count)]
+    refs = refs[count * way_count :]
     totals, refs = refs[:nd], refs[nd:]
     diag_ref, energy_ref, orb_cols, orb_rows, out_ref, x_ref, square, sem = refs
-    waits = [fetch(place_ref, ways[d], x_ref.at[d], sem.at[d]) for d in range(nd - 1)]
+    waits = [fetch(place_ref, ways[d], x_ref.at[d], sem.at[d]) for d in range(count)]
     first_tiles(totals, diag_ref, energy_ref, orb_cols, row_id, col_id, out_ref)
     for wait in waits:
         wait()
@@ -494,23 +494,25 @@
     specs.append(orb_spec(col_blocks, orbs, lambda r, c, p: p[2]))
     specs.append(orb_spec(row_blocks, orbs, lambda r, c, p: p[0]))
     return call(
-        functools.partial(early_kernel, nd, len(ways[0])), "early_terms", [*own, places],
+        functools.partial(early_kernel, nd, len(ways), len(ways[0])), "early_terms", [*own, places],
         [*flat, *totals, diag, energy, orbs, orbs], specs,
         jax.ShapeDtypeStruct((nd, slots * ROWS, LANES), F32),
         [
-            pltpu.VMEM((nd - 1,) + shape, F32),
-            pltpu.VMEM((nd - 1, 8, TILE, LANES), F32),
-            pltpu.SemaphoreType.DMA((nd - 1,)),
+            pltpu.VMEM((len(ways),) + shape, F32),
+            pltpu.VMEM((len(ways), 8, TILE, LANES), F32),
+            pltpu.SemaphoreType.DMA((len(ways),)),
         ],
         1,
     )
 
 
-def last_kernel(way_count, row_id, col_id, place_ref, *refs):
-    ways, refs = refs[:way_count], refs[way_count:]
+def last_kernel(count, way_count, row_id, col_id, place_ref, *refs):
+    ways = [refs[d * way_count : (d + 1) * way_count] for d in range(count)]
+    refs = refs[count * way_count :]
     orb_rows, done_ref, out_ref, x_ref, square, rows_ref, sem = refs
-    wait = fetch(place_ref, ways, x_ref.at[0], sem)
+    waits = [fetch(place_ref, ways[d], x_ref.at[d], sem.at[d]) for d in range(count)]
     nd, slots, area = out_ref.shape
+    early = nd - count
 
     def layout(d, source):
         for start in range(0, slots, 8):
@@ -519,36 +521,40 @@
                     pl.ds(start * ROWS + k, 8, stride=ROWS), :
                 ]
 
-    for d in range(nd - 1):
+    for d in range(early):
         layout(d, done_ref.at[d])
-    wait()
+    for wait in waits:
+        wait()
 
     def write(d, rows, value):
-        rows_ref[rows, :] = value
+        rows_ref[d, rows, :] = value
 
     second_tiles(
-        x_ref, orb_rows, row_id, col_id, square, lambda d, rows: done_ref[nd - 1, rows, :], write
-    )
-    layout(nd - 1, rows_ref)
+        x_ref, orb_rows, row_id, col_id, square, lambda d, rows: done_ref[early + d, rows, :], write
+    )
+    for d in range(count):
+        layout(early + d, rows_ref.at[d])
 
 
 def last_terms(own, places, ways, done, orbs, row_blocks):
     slots = own[0].shape[0]
     nd = done.shape[0]
-    specs = [pl.BlockSpec(memory_space=pl.ANY)] * len(ways)
+    count = len(ways)
+    flat = [way for each in ways for way in each]
+    specs = [pl.BlockSpec(memory_space=pl.ANY)] * len(flat)
     specs += [orb_spec(row_blocks, orbs, lambda r, c, p: p[0]), whole(done)]
     return call(
-        functools.partial(last_kernel, len(ways)), "last_terms", [*own, places],
-        [*ways, orbs, done], specs,
+        functools.partial(last_kernel, count, len(ways[0])), "last_terms", [*own, places],
+        [*flat, orbs, done], specs,
         jax.ShapeDtypeStruct((nd, slots, ROWS * LANES), F32),
         [
-            pltpu.VMEM((1,) + ways[0].shape, F32),
-            pltpu.VMEM((1, 8, TILE, LANES), F32),
-            pltpu.VMEM((slots * ROWS, LANES), F32),
-            pltpu.SemaphoreType.DMA,
+            pltpu.VMEM((count,) + ways[0][0].shape, F32),
+            pltpu.VMEM((count, 8, TILE, LANES), F32),
+            pltpu.VMEM((count, slots * ROWS, LANES), F32),
+            pltpu.SemaphoreType.DMA((count,)),
         ],
         slots,
-        mib=32,
+        mib=40,
     )
 
 
@@ -734,12 +740,11 @@
     piece, total = finish(nd - 1, [*last2, *last3, up_end, down_end])
     sums.append(total)
     ways = ways[:1]
-    for d in range(1, nd - 1):
-        ways.append(spread(pieces[d], lambda: sums[-1]))
-    piece = tie([piece], [way[row_count // 2] for way in ways])[0]
+    piece = tie([piece], [ways[0][row_count // 2]])[0]
     done = early_terms(own, term_place, ways, sums, diag, energy, orbs, row_blocks, col_blocks)
-    ways.append(spread(piece, lambda: done))
-    return last_terms(own, term_place, ways[-1], done, orbs, row_blocks)
+    for value in [*pieces[1:], piece]:
+        ways.append(spread(value, lambda: done))
+    return last_terms(own, term_place, ways[1:], done, orbs, row_blocks)
 
 
 def solution(mesh):

time: 418 us -> 439 us (1.050)
  waiting for transfers between devices: 200 us -> 222 us
    ppermute x9, waiting for transfers between devices: 12.8 us -> 30.8 us  [send(): return lax.ppermute(ways[parent], ('row', 'col'), pairs)]
    unnamed x78 -> x76, local copies, waits for them, and re-layouts: 13.5 us -> 12.7 us
  transfers between devices with their start and end apart: 30 -> 30, of which waited for: 12 -> 14; matrix products, arithmetic and copies ran while one was open for 4% -> 4% of each run, Pallas kernels for 29% -> 27%
where the time goes in v5:
time: 439 us; the launch traced here: 438 us
  waiting for transfers between devices  222 us (51%)
  Pallas kernels  128 us (29%)
  starting transfers between devices  41.4 us (9%)
  local copies, waits for them, and re-layouts  28.4 us (6%)
  between operations  13.9 us (3%)
    all_to_all x2, waiting for transfers between devices, local(): lax.all_to_all(a, ('row', 'col'), split_axis=0, concat_axis=0, tiled=True)  144 us
    pallas_call x3, Pallas kernels, response_piece(): pl.pallas_call(functools.partial(piece_kernel, count, halves, at), out_sh...  51.7 us
    ppermute x9, waiting for transfers between devices, local(): send_up = lambda a: lax.ppermute(a, 'col', forward)  42.7 us
    pallas_call x3, Pallas kernels, call(): pl.pallas_call(kernel, out_shape=out, grid_spec=pltpu.PrefetchScalarGridS...  41.7 us
    ppermute x9, waiting for transfers between devices, send(): return lax.ppermute(ways[parent], ('row', 'col'), pairs)  30.8 us
    pallas_call x1, Pallas kernels, batch_tiles(): pl.pallas_call(functools.partial(batch_kernel, per_range, col_count), out...  14.3 us
    pallas_call x1, Pallas kernels, split_orbitals(): pl.pallas_call(split_kernel, out_shape=(jax.ShapeDtypeStruct((count // TI...  14.2 us
    unnamed x76, local copies, waits for them, and re-layouts  12.7 us
  transfers between devices with their start and end apart: 30, of which 14 were waited for; matrix products, arithmetic and copies ran while one was open for 4% of the time, Pallas kernels for 27%

profile of v5, /device:TPU:0, one launch (start us, length us, event | category | flops | bytes accessed | tf_op | source)
XLA Modules:
  0.0 437.8 jit_solution(15095321524352997109)
XLA Ops:
  8.0 3.6 pick_tiles.1
  11.6 7.4 %all-to-all-start = ((f32[32,200,128]{2,1,0:T(8,128)}), f32[32,200,128]{2,1,0:T(8,128)}, u32[]{:S(2)}, u32[]{:S(2)}) async-start(f32[32,200,128]{2,1,0:T(8,128)} %pick_tiles.1), calls=%async_computation | async-start | bytes 6553600 | tf_op jit(solution)/shard_map/all_to_all | solution.py:657
  21.4 73.7 %all-to-all-done.tiles_ref = f32[32,200,128]{2,1,0:T(8,128)} async-done(((f32[32,200,128]{2,1,0:T(8,128)}), f32[32,200,128]{2,1,0:T(8,128)}, u32[]{:S(2)}, u32[]{:S(2)}) %all-to-all-start) | async-done | bytes 3276832 | tf_op jit(solution)/shard_map/all_to_all | solution.py:657
  95.1 14.3 %batch_tiles.1 = f32[32,192,128]{2,1,0:T(8,128)S(1)} custom-call(s32[8]{0:T(128)S(1)} %and_select_fusion.1.col_ref, f32[32,200,128]{2,1,0:T(8,128)} %all-to-all-done.tiles_ref, f32[512,1024]{1,0:T(8,128)S(1)} %bitcast.23, f32[1,1024]{1,0:T(1,128)S(1)} %copy-done.10, f32[1,1024]{1,0:T(1,128)S(1)} %copy-done.11, f32[3,1,1024]{2,1,0:T(1,128)S(1)} %copy-done.6), custom_call_target="tpu_custom_call" | custom-call | tf_op jit(solution)/shard_map/batch_tiles/pallas_call | solution.py:155
  111.0 2.9 all-to-all-start.1
  116.6 70.3 %all-to-all-done.1.tiles_ref = f32[32,192,128]{2,1,0:T(8,128)S(1)} async-done(((f32[32,192,128]{2,1,0:T(8,128)}), f32[32,192,128]{2,1,0:T(8,128)S(1)}, u32[]{:S(2)}, u32[]{:S(2)}) %all-to-all-start.1) | async-done | bytes 3145760 | tf_op jit(solution)/shard_map/all_to_all | solution.py:657
  203.0 14.2 %split_orbitals.1 = (bf16[128,128,512]{2,1,0:T(8,128)(2,1)}, f32[8,128]{1,0:T(8,128)}) custom-call(f32[8192,512]{1,0:T(8,128)} %all-gather.2.cloned.1.call-done.orb_ref), custom_call_target="tpu_custom_call" | custom-call | bytes 33554432 | tf_op jit(solution)/shard_map/split_orbitals/pallas_call | solution.py:221
  217.2 9.0 %collective-permute-done.1.refs_1_ = f32[1,32,32,128]{3,2,1,0:T(8,128)S(1)} collective-permute-done((f32[1,32,32,128]{3,2,1,0:T(8,128)}, f32[1,32,32,128]{3,2,1,0:T(8,128)S(1)}, u32[]{:S(2)}, u32[]{:S(2)}) %collective-permute-start.1) | collective-permute-done | bytes 524320 | tf_op jit(solution)/shard_map/ppermute | solution.py:690
  229.6 16.5 %add_rows.1 = (f32[32,64,512]{2,1,0:T(8,128)}, f32[32,64,512]{2,1,0:T(8,128)}, f32[32,64,512]{2,1,0:T(8,128)}) custom-call(s32[96]{0:T(128)} %reshape.65.refs_6_.row_id, s32[96]{0:T(128)} %reshape.66.refs_7_.col_id, s32[4]{0:T(128)} %pad_add_fusion.2.refs_8_.place_ref, f32[2,32,32,128]{3,2,1,0:T(8,128)} %get-tuple-element.72.refs_0_, ...), custom_call_target="tpu_custom_call" | custom-call | flops 9600000000 | bytes 8388608 | tf_op jit(solution)/shard_map/add_rows/pallas_call | solution.py:279
  246.1 6.0 %collective-permute-done.4.refs_0_ = f32[2,32,32,128]{3,2,1,0:T(8,128)S(1)} collective-permute-done((f32[2,32,32,128]{3,2,1,0:T(8,128)}, f32[2,32,32,128]{3,2,1,0:T(8,128)S(1)}, u32[]{:S(2)}, u32[]{:S(2)}) %collective-permute-start.4) | collective-permute-done | bytes 1048608 | tf_op jit(solution)/shard_map/ppermute | solution.py:690
  255.4 21.7 %collective-permute-done.6.refs_0_ = f32[2,32,32,128]{3,2,1,0:T(8,128)S(1)} collective-permute-done((f32[2,32,32,128]{3,2,1,0:T(8,128)}, f32[2,32,32,128]{3,2,1,0:T(8,128)S(1)}, u32[]{:S(2)}, u32[]{:S(2)}) %collective-permute-start.6) | collective-permute-done | bytes 1048608 | tf_op jit(solution)/shard_map/ppermute | solution.py:690
  282.6 3.3 collective-permute-done.8.refs_0_
  295.8 17.2 %response_piece.3 = (f32[16,64,512]{2,1,0:T(8,128)}, f32[32,64,512]{2,1,0:T(8,128)}) custom-call(s32[160]{0:T(256)} %reshape.62.refs_9_.row_id, s32[160]{0:T(256)} %reshape.63.refs_10_.col_id, s32[6]{0:T(128)} %pad_add_fusion.1.refs_11_.place_ref, f32[2,32,32,128]{3,2,1,0:T(8,128)} %get-tuple-element.84.refs_0_, ...), custom_call_target="tpu_custom_call" | custom-call | flops 20000000000 | bytes 8388608 | tf_op jit(solution)/shard_map/response_piece/pallas_call | solution.py:393
  313.0 2.9 collective-permute-start.17
  319.5 17.3 %response_piece.4 = (f32[16,64,512]{2,1,0:T(8,128)}, f32[32,64,512]{2,1,0:T(8,128)}) custom-call(s32[160]{0:T(256)} %reshape.62.refs_9_.row_id, s32[160]{0:T(256)} %reshape.63.refs_10_.col_id, s32[6]{0:T(128)} %pad_add_fusion.1.refs_11_.place_ref, f32[2,32,32,128]{3,2,1,0:T(8,128)} %get-tuple-element.84.refs_0_, ...), custom_call_target="tpu_custom_call" | custom-call | flops 20000000000 | bytes 8388608 | tf_op jit(solution)/shard_map/response_piece/pallas_call | solution.py:393
  342.5 2.6 collective-permute-done.21.refs_0_
  347.1 17.3 %response_piece.5 = (f32[16,64,512]{2,1,0:T(8,128)}, f32[32,64,512]{2,1,0:T(8,128)}) custom-call(s32[160]{0:T(256)} %reshape.62.refs_9_.row_id, s32[160]{0:T(256)} %reshape.63.refs_10_.col_id, s32[6]{0:T(128)} %pad_add_fusion.1.refs_11_.place_ref, f32[1,32,32,128]{3,2,1,0:T(8,128)} %get-tuple-element.122.refs_0_, ...), custom_call_target="tpu_custom_call" | custom-call | flops 20000000000 | bytes 8388608 | tf_op jit(solution)/shard_map/response_piece/pallas_call | solution.py:393
  364.4 5.7 %collective-permute-start.25 = (f32[16,64,512]{2,1,0:T(8,128)}, f32[16,64,512]{2,1,0:T(8,128)}, u32[]{:S(2)}, u32[]{:S(2)}) collective-permute-start(f32[16,64,512]{2,1,0:T(8,128)} %tie.18.refs_4_), channel_id=1, source_target_pairs={{0,16},{1,17},{10,26},{11,27},{20,4},{21,5},{30,14},{31,15}} | collective-permute-start | bytes 6291464 | tf_op jit(solution)/shard_map/ppermute | solution.py:586
  370.0 2.6 collective-permute-start.15
  373.2 15.3 %early_terms.1.refs_1_.refs_9_ = f32[3,1024,128]{2,1,0:T(8,128)} custom-call(s32[32]{0:T(128)} %get-tuple-element.68.row_id, s32[32]{0:T(128)} %get-tuple-element.69.col_id, s32[3]{0:T(128)} %pad_add_fusion.place_ref, f32[16,64,512]{2,1,0:T(8,128)} %get-tuple-element.112.refs_0_, f32[16,64,512]{2,1,0:T(8,128)} %collective-permute-done.16.refs_1_, ...), custom_call_target="tpu_custom_call" | custom-call | flops 100000000 | bytes 8388608 | tf_op jit(solution)/shard_map/early_terms/pallas_call | solution.py:279
  388.5 4.0 collective-permute-done.25.refs_0_
  392.7 22.4 %collective-permute-done.15.refs_0_ = f32[16,64,512]{2,1,0:T(8,128)} collective-permute-done((f32[16,64,512]{2,1,0:T(8,128)}, f32[16,64,512]{2,1,0:T(8,128)}, u32[]{:S(2)}, u32[]{:S(2)}) %collective-permute-start.15) | collective-permute-done | bytes 2097184 | tf_op jit(solution)/shard_map/ppermute | solution.py:586
  415.1 4.3 collective-permute-done.23.refs_3_
  421.0 9.9 %last_terms.1 = f32[3,32,4096]{2,1,0:T(8,128)} custom-call(s32[32]{0:T(128)S(1)} %copy-done.9, s32[32]{0:T(128)S(1)} %copy-done.8, s32[3]{0:T(128)S(1)} %copy-done.7, f32[16,64,512]{2,1,0:T(8,128)} %get-tuple-element.111.refs_0_, f32[16,64,512]{2,1,0:T(8,128)} %collective-permute-done.14.refs_1_, f32[16,64,512]{2,1,0:T(8,128)} %tie.17.refs_2_, ...), custom_call_target="tpu_custom_call" | custom-call | flops 3200000000 | bytes 8388608 | tf_op jit(solution)/shard_map/last_terms/pallas_call | solution.py:279
  (176 shorter events, 59.5 us)
Async XLA Ops:
  6.5 196.5 %all-gather.2.cloned.1.call-start = ((), (), s32[]{:S(2)}) async-start(), calls=%async_computation.2 | async-start | bytes 20971520 | tf_op jit(solution)/shard_map/all_gather | solution.py:653
  11.6 83.4 %all-to-all-start = ((f32[32,200,128]{2,1,0:T(8,128)}), f32[32,200,128]{2,1,0:T(8,128)}, u32[]{:S(2)}, u32[]{:S(2)}) async-start(f32[32,200,128]{2,1,0:T(8,128)} %pick_tiles.1), calls=%async_computation | async-start | bytes 6553600 | tf_op jit(solution)/shard_map/all_to_all | solution.py:657
  111.0 75.8 %all-to-all-start.1 = ((f32[32,192,128]{2,1,0:T(8,128)}), f32[32,192,128]{2,1,0:T(8,128)S(1)}, u32[]{:S(2)}, u32[]{:S(2)}) async-start(f32[32,192,128]{2,1,0:T(8,128)} %copy-done.1), calls=%async_computation.1 | async-start | bytes 6291456 | tf_op jit(solution)/shard_map/all_to_all | solution.py:657
  190.1 36.2 %collective-permute-start = (f32[2,32,32,128]{3,2,1,0:T(8,128)}, f32[2,32,32,128]{3,2,1,0:T(8,128)S(1)}, u32[]{:S(2)}, u32[]{:S(2)}) collective-permute-start(f32[2,32,32,128]{3,2,1,0:T(8,128)} %get-tuple-element.72.refs_0_), channel_id=1, source_target_pairs={{0,2},{2,4},{4,6},{6,7},{7,5},{5,3},{3,1},{1,0},{8,10},{10,12},{12... | collective-permute-start | bytes 3145736 | tf_op jit(solution)/shard_map/ppermute | solution.py:690
  190.1 36.2 %collective-permute-start.2 = (f32[2,32,32,128]{3,2,1,0:T(8,128)}, f32[2,32,32,128]{3,2,1,0:T(8,128)}, u32[]{:S(2)}, u32[]{:S(2)}) collective-permute-start(f32[2,32,32,128]{3,2,1,0:T(8,128)} %get-tuple-element.72.refs_0_), channel_id=1, source_target_pairs={{2,0},{4,2},{6,4},{7,6},{5,7},{3,5},{1,3},{0,1},{10,8},{12,10},{14... | collective-permute-start | bytes 3145736 | tf_op jit(solution)/shard_map/ppermute | solution.py:691
  193.4 32.8 %collective-permute-start.1 = (f32[1,32,32,128]{3,2,1,0:T(8,128)}, f32[1,32,32,128]{3,2,1,0:T(8,128)S(1)}, u32[]{:S(2)}, u32[]{:S(2)}) collective-permute-start(f32[1,32,32,128]{3,2,1,0:T(8,128)} %copy-done.5), channel_id=1, source_target_pairs={{0,2},{2,4},{4,6},{6,7},{7,5},{5,3},{3,1},{1,0},{8,10},{10,12},{12... | collective-permute-start | bytes 1572872 | tf_op jit(solution)/shard_map/ppermute | solution.py:690
  193.5 32.8 %collective-permute-start.3 = (f32[1,32,32,128]{3,2,1,0:T(8,128)}, f32[1,32,32,128]{3,2,1,0:T(8,128)S(1)}, u32[]{:S(2)}, u32[]{:S(2)}) collective-permute-start(f32[1,32,32,128]{3,2,1,0:T(8,128)} %copy-done.5), channel_id=1, source_target_pairs={{2,0},{4,2},{6,4},{7,6},{5,7},{3,5},{1,3},{0,1},{10,8},{12,10},{14... | collective-permute-start | bytes 1572872 | tf_op jit(solution)/shard_map/ppermute | solution.py:691
  227.6 24.5 %collective-permute-start.4 = (f32[2,32,32,128]{3,2,1,0:T(8,128)}, f32[2,32,32,128]{3,2,1,0:T(8,128)S(1)}, u32[]{:S(2)}, u32[]{:S(2)}) collective-permute-start(f32[2,32,32,128]{3,2,1,0:T(8,128)} %get-tuple-element.76.refs_2_), channel_id=1, source_target_pairs={{0,2},{2,4},{4,6},{6,7},{7,5},{5,3},{3,1},{1,0},{8,10},{10,12},{12... | collective-permute-start | bytes 3145736 | tf_op jit(solution)/shard_map/ppermute | solution.py:690
  228.0 24.2 %collective-permute-start.5 = (f32[2,32,32,128]{3,2,1,0:T(8,128)}, f32[2,32,32,128]{3,2,1,0:T(8,128)S(1)}, u32[]{:S(2)}, u32[]{:S(2)}) collective-permute-start(f32[2,32,32,128]{3,2,1,0:T(8,128)} %get-tuple-element.77.refs_4_), channel_id=1, source_target_pairs={{2,0},{4,2},{6,4},{7,6},{5,7},{3,5},{1,3},{0,1},{10,8},{12,10},{14... | collective-permute-start | bytes 3145736 | tf_op jit(solution)/shard_map/ppermute | solution.py:691
  253.4 23.8 %collective-permute-start.6 = (f32[2,32,32,128]{3,2,1,0:T(8,128)}, f32[2,32,32,128]{3,2,1,0:T(8,128)S(1)}, u32[]{:S(2)}, u32[]{:S(2)}) collective-permute-start(f32[2,32,32,128]{3,2,1,0:T(8,128)} %get-tuple-element.84.refs_0_), channel_id=1, source_target_pairs={{0,2},{2,4},{4,6},{6,7},{7,5},{5,3},{3,1},{1,0},{8,10},{10,12},{12... | collective-permute-start | bytes 3145736 | tf_op jit(solution)/shard_map/ppermute | solution.py:690
  254.6 22.7 %collective-permute-start.7 = (f32[2,32,32,128]{3,2,1,0:T(8,128)}, f32[2,32,32,128]{3,2,1,0:T(8,128)S(1)}, u32[]{:S(2)}, u32[]{:S(2)}) collective-permute-start(f32[2,32,32,128]{3,2,1,0:T(8,128)} %get-tuple-element.85.refs_1_), channel_id=1, source_target_pairs={{2,0},{4,2},{6,4},{7,6},{5,7},{3,5},{1,3},{0,1},{10,8},{12,10},{14... | collective-permute-start | bytes 3145736 | tf_op jit(solution)/shard_map/ppermute | solution.py:691
  290.0 25.8 %collective-permute-start.10 = (f32[1,16,32,128]{3,2,1,0:T(8,128)S(1)}, f32[1,16,32,128]{3,2,1,0:T(8,128)S(1)}, u32[]{:S(2)}, u32[]{:S(2)}) collective-permute-start(f32[1,16,32,128]{3,2,1,0:T(8,128)S(1)} %slice.32), channel_id=1, source_target_pairs={{0,2},{2,4},{4,6},{6,7},{7,5},{5,3},{3,1},{1,0},{8,10},{10,12},{12... | collective-permute-start | bytes 786440 | tf_op jit(solution)/shard_map/ppermute | solution.py:690
  293.5 22.4 %collective-permute-start.11 = (f32[1,16,32,128]{3,2,1,0:T(8,128)}, f32[1,16,32,128]{3,2,1,0:T(8,128)S(1)}, u32[]{:S(2)}, u32[]{:S(2)}) collective-permute-start(f32[1,16,32,128]{3,2,1,0:T(8,128)} %slice.33), channel_id=1, source_target_pairs={{2,0},{4,2},{6,4},{7,6},{5,7},{3,5},{1,3},{0,1},{10,8},{12,10},{14... | collective-permute-start | bytes 786440 | tf_op jit(solution)/shard_map/ppermute | solution.py:691
  293.8 22.1 %collective-permute-start.12 = (f32[1,32,32,128]{3,2,1,0:T(8,128)}, f32[1,32,32,128]{3,2,1,0:T(8,128)S(1)}, u32[]{:S(2)}, u32[]{:S(2)}) collective-permute-start(f32[1,32,32,128]{3,2,1,0:T(8,128)} %get-tuple-element.98), channel_id=1, source_target_pairs={{0,2},{2,4},{4,6},{6,7},{7,5},{5,3},{3,1},{1,0},{8,10},{10,12},{12... | collective-permute-start | bytes 1572872 | tf_op jit(solution)/shard_map/ppermute | solution.py:690
  295.6 20.4 %collective-permute-start.13 = (f32[1,32,32,128]{3,2,1,0:T(8,128)}, f32[1,32,32,128]{3,2,1,0:T(8,128)S(1)}, u32[]{:S(2)}, u32[]{:S(2)}) collective-permute-start(f32[1,32,32,128]{3,2,1,0:T(8,128)} %get-tuple-element.99), channel_id=1, source_target_pairs={{2,0},{4,2},{6,4},{7,6},{5,7},{3,5},{1,3},{0,1},{10,8},{12,10},{14... | collective-permute-start | bytes 1572872 | tf_op jit(solution)/shard_map/ppermute | solution.py:691
  313.0 29.0 %collective-permute-start.17 = (f32[16,64,512]{2,1,0:T(8,128)}, f32[16,64,512]{2,1,0:T(8,128)S(1)}, u32[]{:S(2)}, u32[]{:S(2)}) collective-permute-start(f32[16,64,512]{2,1,0:T(8,128)} %get-tuple-element.112.refs_0_), channel_id=1, source_target_pairs={{0,16},{1,17},{10,26},{11,27},{20,4},{21,5},{30,14},{31,15}} | collective-permute-start | bytes 6291464 | tf_op jit(solution)/shard_map/ppermute | solution.py:586
  317.4 19.3 %collective-permute-start.20 = (f32[1,32,32,128]{3,2,1,0:T(8,128)}, f32[1,32,32,128]{3,2,1,0:T(8,128)S(1)}, u32[]{:S(2)}, u32[]{:S(2)}) collective-permute-start(f32[1,32,32,128]{3,2,1,0:T(8,128)} %get-tuple-element.115.refs_3_), channel_id=1, source_target_pairs={{2,0},{4,2},{6,4},{7,6},{5,7},{3,5},{1,3},{0,1},{10,8},{12,10},{14... | collective-permute-start | bytes 1572872 | tf_op jit(solution)/shard_map/ppermute | solution.py:691
  342.0 30.7 %collective-permute-start.16 = (f32[16,64,512]{2,1,0:T(8,128)}, f32[16,64,512]{2,1,0:T(8,128)}, u32[]{:S(2)}, u32[]{:S(2)}) collective-permute-start(f32[16,64,512]{2,1,0:T(8,128)} %get-tuple-element.112.refs_0_), channel_id=1, source_target_pairs={{0,8},{8,0},{16,24},{24,16},{1,9},{9,1},{17,25},{25,17},{2,10},{10... | collective-permute-start | bytes 6291464 | tf_op jit(solution)/shard_map/ppermute | solution.py:586
  342.0 31.2 %collective-permute-start.18 = (f32[16,64,512]{2,1,0:T(8,128)S(1)}, f32[16,64,512]{2,1,0:T(8,128)}, u32[]{:S(2)}, u32[]{:S(2)}) collective-permute-start(f32[16,64,512]{2,1,0:T(8,128)S(1)} %collective-permute-done.17.refs_7_.refs_2_.refs_1_), channel_id=1, source_target_pairs={{0,8},{8,0},{16,24},{24,16},{1,9},{9,1},{17,25},{25,17},{2,10},{10... | collective-permute-start | bytes 6291464 | tf_op jit(solution)/shard_map/ppermute | solution.py:586
  364.4 28.2 %collective-permute-start.25 = (f32[16,64,512]{2,1,0:T(8,128)}, f32[16,64,512]{2,1,0:T(8,128)}, u32[]{:S(2)}, u32[]{:S(2)}) collective-permute-start(f32[16,64,512]{2,1,0:T(8,128)} %tie.18.refs_4_), channel_id=1, source_target_pairs={{0,16},{1,17},{10,26},{11,27},{20,4},{21,5},{30,14},{31,15}} | collective-permute-start | bytes 6291464 | tf_op jit(solution)/shard_map/ppermute | solution.py:586
  370.0 45.0 %collective-permute-start.15 = (f32[16,64,512]{2,1,0:T(8,128)}, f32[16,64,512]{2,1,0:T(8,128)}, u32[]{:S(2)}, u32[]{:S(2)}) collective-permute-start(f32[16,64,512]{2,1,0:T(8,128)} %get-tuple-element.111.refs_0_), channel_id=1, source_target_pairs={{0,16},{1,17},{10,26},{11,27},{20,4},{21,5},{30,14},{31,15}} | collective-permute-start | bytes 6291464 | tf_op jit(solution)/shard_map/ppermute | solution.py:586
  372.7 42.4 %collective-permute-start.14 = (f32[16,64,512]{2,1,0:T(8,128)}, f32[16,64,512]{2,1,0:T(8,128)}, u32[]{:S(2)}, u32[]{:S(2)}) collective-permute-start(f32[16,64,512]{2,1,0:T(8,128)} %get-tuple-element.111.refs_0_), channel_id=1, source_target_pairs={{0,8},{8,0},{16,24},{24,16},{1,9},{9,1},{17,25},{25,17},{2,10},{10... | collective-permute-start | bytes 6291464 | tf_op jit(solution)/shard_map/ppermute | solution.py:586
  372.7 42.4 %collective-permute-start.24 = (f32[16,64,512]{2,1,0:T(8,128)}, f32[16,64,512]{2,1,0:T(8,128)}, u32[]{:S(2)}, u32[]{:S(2)}) collective-permute-start(f32[16,64,512]{2,1,0:T(8,128)} %tie.18.refs_4_), channel_id=1, source_target_pairs={{0,8},{8,0},{16,24},{24,16},{1,9},{9,1},{17,25},{25,17},{2,10},{10... | collective-permute-start | bytes 6291464 | tf_op jit(solution)/shard_map/ppermute | solution.py:586
  392.6 22.5 %collective-permute-start.26 = (f32[16,64,512]{2,1,0:T(8,128)}, f32[16,64,512]{2,1,0:T(8,128)}, u32[]{:S(2)}, u32[]{:S(2)}) collective-permute-start(f32[16,64,512]{2,1,0:T(8,128)} %tie.19.refs_6_), channel_id=1, source_target_pairs={{0,8},{8,0},{16,24},{24,16},{1,9},{9,1},{17,25},{25,17},{2,10},{10... | collective-permute-start | bytes 6291464 | tf_op jit(solution)/shard_map/ppermute | solution.py:586
  (43 other events, 543.1 us)
Sparse Core Ops, SparseCore 0:
  8.9 169.4 all-gather.1
